TPU v7x, 256 devices: a whole 4x4x8 slice. The times are simulated.
256 devices in a mesh: samp: 64 (over y_lo, x, z), par: 4 (over y_hi, core).
Axes of the slice: x: 4, y: 4 (y_hi: 2, y_lo: 2; y = y_hi * 2 + y_lo), z: 8, core: 2. Of those that a mesh axis runs over, the one named last changes fastest.
Arguments:
- log_derivs: bfloat16 [8192, 8192], P('samp', 'par'), may hold values from -16 to 16
- sample_vector: float32 [8192], P('samp'), may hold values from -6 to 6
Outputs:
- gram: float32 [8192, 8192], P('samp', 'par')
- update: float32 [4, 2048], P('par', 'samp')
All inputs are finite; a program needn't handle non-finite values.
Results may differ from a plain program's by a relative error of at most 0.0003.
Values may be sent and summed in bfloat16 or wider, within the bound.
No kernel may reach another device: no remote copies, remote signals or barrier semaphores. Data moves between devices by JAX's collectives and lax.ppermute only.
A program may use at most 128 MiB of HBM per device.

v0:
```python
import math

import jax
import jax.numpy as jnp
from jax import lax
from jax.sharding import PartitionSpec as P


def body(log_derivs, sample_vector):
    rows = log_derivs.shape[0]
    panel = log_derivs.shape[1]
    cycle_size = lax.axis_size("samp")
    dims = (((1,), (1,)), ((), ()))
    tile = lax.dot_general(
        log_derivs,
        lax.all_gather(log_derivs, "samp", axis=0, tiled=True),
        dims,
        preferred_element_type=jnp.float32,
    )
    total_params = panel * lax.axis_size("par")
    gram = lax.psum_scatter(tile, "par", scatter_dimension=1, tiled=True) * (
        1.0 / math.sqrt(total_params)
    )
    term = jnp.dot(sample_vector, log_derivs.astype(jnp.float32), precision=lax.Precision.HIGHEST)
    summed = lax.psum_scatter(term[None, :], "samp", scatter_dimension=1, tiled=True)
    update = summed * (1.0 / math.sqrt(rows * cycle_size))
    return (gram, update)


def solution(mesh):
    return jax.shard_map(
        body,
        mesh=mesh,
        in_specs=(P("samp", "par"), P("samp")),
        out_specs=(P("samp", "par"), P("par", "samp")),
        check_vma=False,
    )
```

profile of v0, /device:TPU:16, one launch (start us, length us, event | category | flops | bytes accessed | tf_op | source)
XLA Modules:
  0.0 765.0 jit_solution(8450150786734430217)
XLA Ops:
  7.2 0.0 copy-start
  7.2 0.0 all-gather.2.cloned.1.call-start
  7.2 0.7 all-gather.2.cloned.1.call-update
  7.9 0.0 reduce-scatter.7.cloned.1.call-start
  8.0 0.0 copy-done
  8.0 2.7 convolution_bitcast_fusion
  10.7 0.0 reduce-scatter.7.cloned.1.call-update
  10.7 0.0 reduce-scatter.5.cloned.1.call-start
  10.7 380.1 %all-gather.2.cloned.1.call-done = bf16[8192,2048]{1,0:T(8,128)(2,1)} async-done(((bf16[128,2048]{1,0:T(8,128)(2,1)}), bf16[8192,2048]{1,0:T(8,128)(2,1)}) %all-gather.2.cloned.1.call-update) | async-done | bytes 33554448 | tf_op jit(solution)/shard_map/all_gather | solution.py:16
  390.9 17.8 %fusion.1 = f32[128,8192]{1,0:T(8,128)} fusion(bf16[128,2048]{1,0:T(8,128)(2,1)} %param.2, bf16[8192,2048]{1,0:T(8,128)(2,1)} %all-gather.2.cloned.1.call-done), kind=kOutput, calls=%fused_computation.4 | convolution fusion | flops 4294967296 | bytes 38273024 | tf_op jit(solution)/shard_map/dot_general | solution.py:14
  408.7 0.0 reduce-scatter.5.cloned.1.call-update
  408.7 296.6 %reduce-scatter.7.cloned.1.call-done = f32[32,1]{1,0:T(8,128)} async-done(((f32[2048,1]{1,0:T(8,128)}), f32[32,1]{1,0:T(8,128)}) %reduce-scatter.7.cloned.1.call-update) | async-done | bytes 144
  705.2 0.8 copy.5
  706.0 0.5 broadcast_multiply_fusion.1
  706.6 49.6 %reduce-scatter.5.cloned.1.call-done = f32[128,2048]{1,0:T(8,128)} async-done(((f32[128,8192]{1,0:T(8,128)}), f32[128,2048]{1,0:T(8,128)}) %reduce-scatter.5.cloned.1.call-update) | async-done | bytes 1048592 | tf_op jit(solution)/shard_map/reduce_scatter | solution.py:21
  756.1 2.3 broadcast_multiply_fusion
Async XLA Ops:
  7.2 0.8 copy-start
  7.2 383.7 %all-gather.2.cloned.1.call-start = ((), (), s32[]{:S(2)}) async-start(), calls=%async_computation.2 | async-start | bytes 34078720 | tf_op jit(solution)/shard_map/all_gather | solution.py:16
  7.9 697.3 %reduce-scatter.7.cloned.1.call-start = ((), (), s32[]{:S(2)}) async-start(), calls=%async_computation.4 | async-start | bytes 1064960
  10.7 745.5 %reduce-scatter.5.cloned.1.call-start = ((), (), s32[]{:S(2)}) async-start(), calls=%async_computation.3 | async-start | bytes 5242880 | tf_op jit(solution)/shard_map/reduce_scatter | solution.py:21
Sparse Core Ops, SparseCore 0:
  9.8 381.0 all-gather.1
  393.9 311.2 reduce-scatter.6
  708.3 47.8 reduce-scatter.4
where the time goes:
time: 769 us; the launch traced here: 765 us
  waiting for transfers between devices  727 us (95%)
  matrix products  20.5 us (3%)
  between operations  13.8 us (2%)
    all_gather x1, waiting for transfers between devices, body(): lax.all_gather(log_derivs, 'samp', axis=0, tiled=True)  380 us
    unnamed x4, waiting for transfers between devices  297 us
    reduce_scatter x1, waiting for transfers between devices, body(): lax.psum_scatter(tile, 'par', scatter_dimension=1, tiled=True)  49.6 us
    dot_general x1, matrix products, body(): lax.dot_general(log_derivs, lax.all_gather(log_derivs, 'samp', axis=0, ti...  17.8 us
  transfers between devices with their start and end apart: 3, of which 3 were waited for; matrix products, arithmetic and copies ran while one was open for 3% of the time, Pallas kernels for 0%

commit v1 on v0

v1 whole, which is shorter than its diff:
```python
import math

import jax
import jax.numpy as jnp
from jax import lax
from jax.experimental import pallas as pl
from jax.experimental.pallas import tpu as pltpu
from jax.sharding import Mesh, PartitionSpec as P

AXES = ("ylo", "x", "z", "yhi", "core")
SIZES = (2, 4, 8, 2, 2)
ROWS, PANEL = 128, 2048
NX, NZ = 4, 8
F32 = jnp.float32


def shift(value, axis, size, by):
    return lax.ppermute(value, axis, [(i, (i + by) % size) for i in range(size)])


def ring(own, axis, size):
    right, left = [own], [own]
    for _ in range(size // 2 - 1):
        right.append(shift(right[-1], axis, size, 1))
        left.append(shift(left[-1], axis, size, -1))
    half = own.shape[0] // 2
    first = shift(right[-1][:half], axis, size, 1)
    second = shift(left[-1][half:], axis, size, -1)
    return right, left, (first, second)


def slot_of(ylo_other, x_offset):
    x = lax.rem(lax.axis_index("x") + x_offset, NX)
    ylo = lax.rem(lax.axis_index("ylo") + ylo_other, 2)
    core = lax.rem(lax.div(x, 2) + lax.axis_index("core"), 2)
    yhi = lax.rem(ylo + lax.axis_index("yhi"), 2)
    return 2 * core + yhi, lax.rem(x, 2)


def products_kernel(scale, n_rows, n_cols, places, *refs):
    rows, cols = refs[:n_rows], refs[n_rows : n_rows + n_cols]
    keep, send, held, sems = refs[n_rows + n_cols :]
    copies = []
    for i, (ref, (ylo_other, x_offset, start)) in enumerate(zip(cols, places)):
        pair, odd = slot_of(ylo_other, x_offset)
        to = pl.multiple_of(odd * ROWS + start, 64)
        copy = pltpu.make_async_copy(ref, held.at[pair, pl.ds(to, ref.shape[0])], sems.at[i])
        copy.start()
        copies.append(copy)
    for copy in copies:
        copy.wait()
    block = jnp.concatenate([r[...] for r in rows], axis=0)
    for pair in range(4):
        out = keep if pair < 2 else send
        out[:, 256 * (pair % 2) : 256 * (pair % 2) + 256] = scale * lax.dot_general(
            block, held[pair], (((1,), (1,)), ((), ())), preferred_element_type=F32
        )


def products(scale, rows, cols, places):
    m = sum(r.shape[0] for r in rows)
    out = jax.ShapeDtypeStruct((m, 512), F32)
    vmem, anywhere = pl.BlockSpec(memory_space=pltpu.VMEM), pl.BlockSpec(memory_space=pl.ANY)

    def kernel(*refs):
        products_kernel(scale, len(rows), len(cols), places, *refs)

    return pl.pallas_call(
        kernel,
        out_shape=(out, out),
        in_specs=[vmem] * len(rows) + [anywhere] * len(cols),
        out_specs=(vmem, vmem),
        scratch_shapes=[
            pltpu.VMEM((4, 256, PANEL), jnp.bfloat16),
            pltpu.SemaphoreType.DMA((len(cols),)),
        ],
        compiler_params=pltpu.CompilerParams(vmem_limit_bytes=40 * 2**20),
        cost_estimate=pl.CostEstimate(
            flops=2 * m * 1024 * PANEL, bytes_accessed=2**22 + m * 8192, transcendentals=0
        ),
    )(*rows, *cols)


def term_kernel(places, vec, *refs):
    cols, out = refs[:-3], refs[-3]
    held, sems = refs[-2:]
    u = lax.axis_index("ylo") * NX + lax.axis_index("x")
    at = pl.multiple_of(u * 256, 256)
    copies = []
    for i, (ref, (ylo_other, x_offset, start)) in enumerate(zip(cols, places)):
        x = lax.rem(lax.axis_index("x") + x_offset, NX)
        ylo = lax.rem(lax.axis_index("ylo") + ylo_other, 2)
        to = pl.multiple_of((ylo * NX + x) * ROWS + start, 64)
        copy = pltpu.make_async_copy(
            ref.at[:, pl.ds(at, 256)], held.at[pl.ds(to, ref.shape[0])], sems.at[i]
        )
        copy.start()
        copies.append(copy)
    for copy in copies:
        copy.wait()
    v = vec[...]
    total = jnp.zeros((8, 256), F32)
    for _ in range(3):
        part = v.astype(jnp.bfloat16)
        v = v - part.astype(F32)
        total += jnp.dot(part, held[...], preferred_element_type=F32)
    out[...] = total


def term(vec, cols, places):
    vmem, anywhere = pl.BlockSpec(memory_space=pltpu.VMEM), pl.BlockSpec(memory_space=pl.ANY)

    def kernel(*refs):
        term_kernel(places, *refs)

    return pl.pallas_call(
        kernel,
        out_shape=jax.ShapeDtypeStruct((8, 256), F32),
        in_specs=[vmem] + [anywhere] * len(cols),
        out_specs=vmem,
        scratch_shapes=[
            pltpu.VMEM((1024, 256), jnp.bfloat16),
            pltpu.SemaphoreType.DMA((len(cols),)),
        ],
        cost_estimate=pl.CostEstimate(flops=2**23, bytes_accessed=2**19, transcendentals=0),
    )(vec, *cols)


def place_kernel(offsets, *refs):
    blocks, out = refs[:-1], refs[-1]
    for block, offset in zip(blocks, offsets):
        z = lax.rem(lax.axis_index("z") + offset, NZ)
        at = pl.multiple_of(z * ROWS, ROWS)
        out[:, pl.ds(at, ROWS)] = block[:, :ROWS]
        out[:, pl.ds(at + NZ * ROWS, ROWS)] = block[:, ROWS:]


def place(blocks, offsets):
    vmem = pl.BlockSpec(memory_space=pltpu.VMEM)

    def kernel(*refs):
        place_kernel(offsets, *refs)

    return pl.pallas_call(
        kernel,
        out_shape=jax.ShapeDtypeStruct((ROWS, PANEL), F32),
        in_specs=[vmem] * len(blocks),
        out_specs=vmem,
        cost_estimate=pl.CostEstimate(flops=0, bytes_accessed=2**21, transcendentals=0),
    )(*blocks)


def body(log_derivs, sample_vector):
    scale_gram = 1.0 / math.sqrt(PANEL * 4)
    scale_update = 1.0 / math.sqrt(ROWS * 64)

    vec = lax.all_gather(sample_vector, ("ylo", "x"), axis=0, tiled=True)

    z_right, z_left, z_far = ring(log_derivs, "z", NZ)
    partner = shift(log_derivs, "ylo", 2, 1)
    cols, places = [], []
    for ylo_other, own in ((0, log_derivs), (1, partner)):
        right, left, far = ring(own, "x", NX)
        cols += [own, right[1], left[1], *far]
        places += [(ylo_other, 0, 0), (ylo_other, 3, 0), (ylo_other, 1, 0), (ylo_other, 2, 0), (ylo_other, 2, 64)]

    mine = jnp.sum(term(jnp.broadcast_to(vec[None], (8, 1024)), cols, places)[:1], axis=0)
    shared = lax.all_gather(mine[None], "z", axis=0, tiled=True)
    owned = lax.dynamic_slice_in_dim(jnp.sum(shared, axis=0), lax.axis_index("z") * 32, 32)
    update = (owned * scale_update)[None]

    groups = [
        ([0, 1, -1], [log_derivs, z_right[1], z_left[1]]),
        ([2, -2], [z_right[2], z_left[2]]),
        ([3, -3, 4], [z_right[3], z_left[3], *z_far]),
    ]
    blocks, offsets = [], []
    for backs, rows in groups:
        keep, send = products(scale_gram, rows, cols, places)
        both = keep + shift(send, "core", 2, 1)
        full = both[:, :256] + shift(both[:, 256:], "yhi", 2, 1)
        for i, back in enumerate(backs):
            block = full[ROWS * i : ROWS * (i + 1)]
            blocks.append(block if back == 0 else shift(block, "z", NZ, -back))
            offsets.append(back % NZ)
    return place(blocks, offsets), update


def solution(mesh):
    fine = Mesh(mesh.devices.reshape(SIZES), AXES)
    samp, par = AXES[:3], AXES[3:]
    return jax.shard_map(
        body,
        mesh=fine,
        in_specs=(P(samp, par), P(samp)),
        out_specs=(P(samp, par), P(par, samp)),
        check_vma=False,
    )
```

time: 769 us -> 142 us (0.18)
  waiting for transfers between devices: 727 us -> 36 us
  starting transfers between devices: 0.12 us -> 45.8 us
  blocking collectives: 0 us -> 36.6 us
  matrix products: 20.5 us -> 0 us
  Pallas kernels: 0 us -> 13.3 us
  between operations: 13.8 us -> 1.07 us
    all_gather x1 -> x0, waiting for transfers between devices: 380 us -> none  [body(): lax.all_gather(log_derivs, 'samp', axis=0, tiled=True)]
    unnamed x4 -> x0, waiting for transfers between devices: 297 us -> none
    reduce_scatter x1 -> x0, waiting for transfers between devices: 49.6 us -> none  [body(): lax.psum_scatter(tile, 'par', scatter_dimension=1, tiled=True)]
    ppermute x0 -> x30, starting transfers between devices: none -> 45.8 us  [shift(): lax.ppermute(value, axis, [(i, (i + by) % size) for i in range(size)])]
    all_gather x0 -> x2, blocking collectives: none -> 36.6 us  [the longest x1 18.4 us: body(): shared = lax.all_gather(mine[None], 'z', axis=0, tiled=True)]
    ppermute x0 -> x30, waiting for transfers between devices: none -> 36 us  [shift(): lax.ppermute(value, axis, [(i, (i + by) % size) for i in range(size)])]
    dot_general x1 -> x0, matrix products: 17.8 us -> none  [body(): lax.dot_general(log_derivs, lax.all_gather(log_derivs, 'samp', axis=0, ti...]
    pallas_call x0 -> x5, Pallas kernels: none -> 13.3 us  [the longest x3 8.09 us: products(): pl.pallas_call(kernel, out_shape=(out, out), in_specs=[vmem] * len(rows)...]
  transfers between devices with their start and end apart: 3 -> 30, of which waited for: 3 -> 10; matrix products, arithmetic and copies ran while one was open for 3% -> 3% of each run, Pallas kernels for 0% -> 8%
where the time goes in v1:
time: 142 us; the launch traced here: 140 us
  starting transfers between devices  45.8 us (32%)
  blocking collectives  36.6 us (26%)
  waiting for transfers between devices  36 us (25%)
  Pallas kernels  13.3 us (9%)
  local copies, waits for them, and re-layouts  4.38 us (3%)
  other arithmetic  2.28 us (2%)
    ppermute x30, starting transfers between devices, shift(): lax.ppermute(value, axis, [(i, (i + by) % size) for i in range(size)])  45.8 us
    ppermute x30, waiting for transfers between devices, shift(): lax.ppermute(value, axis, [(i, (i + by) % size) for i in range(size)])  36 us
    all_gather x1, blocking collectives, body(): shared = lax.all_gather(mine[None], 'z', axis=0, tiled=True)  18.4 us
    all_gather x1, blocking collectives, body(): vec = lax.all_gather(sample_vector, ('ylo', 'x'), axis=0, tiled=True)  18.2 us
    pallas_call x3, Pallas kernels, products(): pl.pallas_call(kernel, out_shape=(out, out), in_specs=[vmem] * len(rows)...  8.09 us
    pallas_call x1, Pallas kernels, term(): pl.pallas_call(kernel, out_shape=jax.ShapeDtypeStruct((8, 256), F32), in_...  2.86 us
    unnamed x45, local copies, waits for them, and re-layouts  2.86 us
  transfers between devices with their start and end apart: 30, of which 10 were waited for; matrix products, arithmetic and copies ran while one was open for 3% of the time, Pallas kernels for 8%

profile of v1, /device:TPU:16, one launch (start us, length us, event | category | flops | bytes accessed | tf_op | source)
XLA Modules:
  0.0 139.5 jit_solution(10999308756845976434)
XLA Ops:
  2.0 1.9 %collective-permute-start = (bf16[128,2048]{1,0:T(8,128)(2,1)}, bf16[128,2048]{1,0:T(8,128)(2,1)S(1)}, u32[]{:S(2)}, u32[]{:S(2)}) collective-permute-start(bf16[128,2048]{1,0:T(8,128)(2,1)} %refs_1_.1), channel_id=1, source_target_pairs={{0,4},{4,8},{8,12},{12,16},{16,20},{20,24},{24,28},{28,0},{1,5},{5... | collective-permute-start | bytes 1572872 | tf_op jit(solution)/shard_map/ppermute | solution.py:18
  3.9 3.9 %collective-permute-start.1 = (bf16[128,2048]{1,0:T(8,128)(2,1)}, bf16[128,2048]{1,0:T(8,128)(2,1)S(1)}, u32[]{:S(2)}, u32[]{:S(2)}) collective-permute-start(bf16[128,2048]{1,0:T(8,128)(2,1)} %refs_1_.1), channel_id=1, source_target_pairs={{0,28},{4,0},{8,4},{12,8},{16,12},{20,16},{24,20},{28,24},{1,29},{... | collective-permute-start | bytes 1572872 | tf_op jit(solution)/shard_map/ppermute | solution.py:18
  11.1 3.5 %collective-permute-done.6.refs_8_.refs_7_.refs_9_.refs_6_ = bf16[128,2048]{1,0:T(8,128)(2,1)S(1)} collective-permute-done((bf16[128,2048]{1,0:T(8,128)(2,1)}, bf16[128,2048]{1,0:T(8,128)(2,1)S(1)}, u32[]{:S(2)}, u32[]{:S(2)}) %collective-permute-start.6) | collective-permute-done | bytes 524320 | tf_op jit(solution)/shard_map/ppermute | solution.py:18
  16.1 3.7 %collective-permute-done.refs_1_ = bf16[128,2048]{1,0:T(8,128)(2,1)S(1)} collective-permute-done((bf16[128,2048]{1,0:T(8,128)(2,1)}, bf16[128,2048]{1,0:T(8,128)(2,1)S(1)}, u32[]{:S(2)}, u32[]{:S(2)}) %collective-permute-start) | collective-permute-done | bytes 524320 | tf_op jit(solution)/shard_map/ppermute | solution.py:18
  19.7 2.8 %collective-permute-start.8 = (bf16[128,2048]{1,0:T(8,128)(2,1)S(1)}, bf16[128,2048]{1,0:T(8,128)(2,1)S(1)}, u32[]{:S(2)}, u32[]{:S(2)}) collective-permute-start(bf16[128,2048]{1,0:T(8,128)(2,1)S(1)} %collective-permute-done.6.refs_8_.refs_7_.refs_9_.refs_6_), channel_id=1, source_target_pairs={{0,96},{32,0},{64,32},{96,64},{1,97},{33,1},{65,33},{97,65},{2,98}... | collective-permute-start | bytes 1572872 | tf_op jit(solution)/shard_map/ppermute | solution.py:18
  25.9 9.5 %collective-permute-done.7.refs_9_.refs_8_.refs_10_.refs_7_ = bf16[128,2048]{1,0:T(8,128)(2,1)S(1)} collective-permute-done((bf16[128,2048]{1,0:T(8,128)(2,1)S(1)}, bf16[128,2048]{1,0:T(8,128)(2,1)S(1)}, u32[]{:S(2)}, u32[]{:S(2)}) %collective-permute-start.7) | collective-permute-done | bytes 524320 | tf_op jit(solution)/shard_map/ppermute | solution.py:18
  37.5 3.4 %collective-permute-done.4.refs_6_.refs_5_.refs_7_.refs_4_ = bf16[64,2048]{1,0:T(8,128)(2,1)S(1)} collective-permute-done((bf16[64,2048]{1,0:T(8,128)(2,1)S(1)}, bf16[64,2048]{1,0:T(8,128)(2,1)S(1)}, u32[]{:S(2)}, u32[]{:S(2)}) %collective-permute-start.4) | collective-permute-done | bytes 262176 | tf_op jit(solution)/shard_map/ppermute | solution.py:18
  42.6 3.2 %collective-permute-start.22 = (bf16[128,2048]{1,0:T(8,128)(2,1)S(1)}, bf16[128,2048]{1,0:T(8,128)(2,1)S(1)}, u32[]{:S(2)}, u32[]{:S(2)}) collective-permute-start(bf16[128,2048]{1,0:T(8,128)(2,1)S(1)} %collective-permute-done.16.refs_1_), channel_id=1, source_target_pairs={{0,28},{4,0},{8,4},{12,8},{16,12},{20,16},{24,20},{28,24},{1,29},{... | collective-permute-start | bytes 1572872 | tf_op jit(solution)/shard_map/ppermute | solution.py:18
  47.4 3.1 %shard_map.41 = (f32[384,512]{1,0:T(8,128)S(1)}, f32[384,512]{1,0:T(8,128)}) custom-call(bf16[128,2048]{1,0:T(8,128)(2,1)S(1)} %copy-done.4, bf16[128,2048]{1,0:T(8,128)(2,1)S(1)} %collective-permute-done.refs_1_, bf16[128,2048]{1,0:T(8,128)(2,1)S(1)} %collective-permute-done.1.refs_2_, bf16[128,2048]{1,0:T(8,128)(2,1)S(1)} %copy-done.4, ...), custom_call_target="tpu_custom_call" | custom-call | flops 1610612736 | bytes 7340032 | tf_op jit(solution)/shard_map/pallas_call | solution.py:68
  50.6 1.8 %shard_map.42 = (f32[256,512]{1,0:T(8,128)S(1)}, f32[256,512]{1,0:T(8,128)S(1)}) custom-call(bf16[128,2048]{1,0:T(8,128)(2,1)S(1)} %collective-permute-done.15.refs_0_, bf16[128,2048]{1,0:T(8,128)(2,1)S(1)} %collective-permute-done.16.refs_1_, bf16[128,2048]{1,0:T(8,128)(2,1)S(1)} %copy-done.4, ...), custom_call_target="tpu_custom_call" | custom-call | flops 1073741824 | bytes 6291456 | tf_op jit(solution)/shard_map/pallas_call | solution.py:68
  54.0 3.3 %collective-permute-start.24 = (bf16[64,2048]{1,0:T(8,128)(2,1)S(1)}, bf16[64,2048]{1,0:T(8,128)(2,1)S(1)}, u32[]{:S(2)}, u32[]{:S(2)}) collective-permute-start(bf16[64,2048]{1,0:T(8,128)(2,1)S(1)} %slice.98), channel_id=1, source_target_pairs={{0,28},{4,0},{8,4},{12,8},{16,12},{20,16},{24,20},{28,24},{1,29},{... | collective-permute-start | bytes 786440 | tf_op jit(solution)/shard_map/ppermute | solution.py:18
  57.3 5.2 %collective-permute-done.23.refs_2_ = bf16[64,2048]{1,0:T(8,128)(2,1)S(1)} collective-permute-done((bf16[64,2048]{1,0:T(8,128)(2,1)S(1)}, bf16[64,2048]{1,0:T(8,128)(2,1)S(1)}, u32[]{:S(2)}, u32[]{:S(2)}) %collective-permute-start.23) | collective-permute-done | bytes 262176 | tf_op jit(solution)/shard_map/ppermute | solution.py:18
  62.6 3.2 %shard_map.43 = (f32[384,512]{1,0:T(8,128)S(1)}, f32[384,512]{1,0:T(8,128)}) custom-call(bf16[128,2048]{1,0:T(8,128)(2,1)S(1)} %collective-permute-done.21.refs_0_, bf16[128,2048]{1,0:T(8,128)(2,1)S(1)} %collective-permute-done.22.refs_1_, bf16[64,2048]{1,0:T(8,128)(2,1)S(1)} %collective-permute-done.23.refs_2_, ...), custom_call_target="tpu_custom_call" | custom-call | flops 1610612736 | bytes 7340032 | tf_op jit(solution)/shard_map/pallas_call | solution.py:68
  68.1 18.2 %all-gather = f32[8,1,128]{2,1,0:T(1,128)S(1)} all-gather(f32[1,1,128]{2,1,0:T(1,128)S(1)} %bitcast.7), channel_id=1, replica_groups=mesh['ylo'=2,'x'=4,'z'=8,'yhi'=2,'core'=2] {'ylo','x'}, dimensions={0}, use_global_device_ids=true | all-gather | bytes 4608 | tf_op jit(solution)/shard_map/all_gather | solution.py:157
  86.9 2.9 %shard_map.45 = f32[8,256]{1,0:T(8,128)} custom-call(f32[8,1024]{1,0:T(8,128)} %broadcast_in_dim.4.refs_0_, bf16[128,2048]{1,0:T(8,128)(2,1)} %refs_1_.1, bf16[128,2048]{1,0:T(8,128)(2,1)} %copy-done, bf16[128,2048]{1,0:T(8,128)(2,1)} %copy-done.1, bf16[64,2048]{1,0:T(8,128)(2,1)} %copy-done.6, bf16[64,2048]{1,0:T(8,128)(2,1)} %copy-done.7, ...), custom_call_target="tpu_custom_call" | custom-call | flops 8388608 | bytes 524288 | tf_op jit(solution)/shard_map/pallas_call | solution.py:116
  91.1 2.1 %collective-permute-start.12 = (f32[384,256]{1,0:T(8,128)S(1)}, f32[384,256]{1,0:T(8,128)S(1)}, u32[]{:S(2)}, u32[]{:S(2)}) collective-permute-start(f32[384,256]{1,0:T(8,128)S(1)} %slice.89), channel_id=1, source_target_pairs={{0,2},{2,0},{1,3},{3,1},{4,6},{6,4},{5,7},{7,5},{8,10},{10,8},{9,1... | collective-permute-start | bytes 1179656 | tf_op jit(solution)/shard_map/ppermute | solution.py:18
  93.3 1.8 %collective-permute-start.19 = (f32[128,256]{1,0:T(8,128)S(1)}, f32[128,256]{1,0:T(8,128)S(1)}, u32[]{:S(2)}, u32[]{:S(2)}) collective-permute-start(f32[128,256]{1,0:T(8,128)S(1)} %get-tuple-element.21), channel_id=1, source_target_pairs={{0,24},{4,28},{8,0},{12,4},{16,8},{20,12},{24,16},{28,20},{1,25},{... | collective-permute-start | bytes 393224 | tf_op jit(solution)/shard_map/ppermute | solution.py:18
  96.5 1.8 %collective-permute-start.26 = (f32[384,256]{1,0:T(8,128)S(1)}, f32[384,256]{1,0:T(8,128)S(1)}, u32[]{:S(2)}, u32[]{:S(2)}) collective-permute-start(f32[384,256]{1,0:T(8,128)S(1)} %slice.100), channel_id=1, source_target_pairs={{0,2},{2,0},{1,3},{3,1},{4,6},{6,4},{5,7},{7,5},{8,10},{10,8},{9,1... | collective-permute-start | bytes 1179656 | tf_op jit(solution)/shard_map/ppermute | solution.py:18
  98.3 5.9 %collective-permute-done.12 = f32[384,256]{1,0:T(8,128)S(1)} collective-permute-done((f32[384,256]{1,0:T(8,128)S(1)}, f32[384,256]{1,0:T(8,128)S(1)}, u32[]{:S(2)}, u32[]{:S(2)}) %collective-permute-start.12) | collective-permute-done | bytes 393248 | tf_op jit(solution)/shard_map/ppermute | solution.py:18
  105.0 2.8 %collective-permute-start.13 = (f32[128,256]{1,0:T(8,128)S(1)}, f32[128,256]{1,0:T(8,128)S(1)}, u32[]{:S(2)}, u32[]{:S(2)}) collective-permute-start(f32[128,256]{1,0:T(8,128)S(1)} %get-tuple-element.18), channel_id=1, source_target_pairs={{0,28},{4,0},{8,4},{12,8},{16,12},{20,16},{24,20},{28,24},{1,29},{... | collective-permute-start | bytes 393224 | tf_op jit(solution)/shard_map/ppermute | solution.py:18
  108.6 3.0 %collective-permute-start.27 = (f32[128,256]{1,0:T(8,128)S(1)}, f32[128,256]{1,0:T(8,128)S(1)}, u32[]{:S(2)}, u32[]{:S(2)}) collective-permute-start(f32[128,256]{1,0:T(8,128)S(1)} %get-tuple-element.16), channel_id=1, source_target_pairs={{0,20},{4,24},{8,28},{12,0},{16,4},{20,8},{24,12},{28,16},{1,21},{... | collective-permute-start | bytes 393224 | tf_op jit(solution)/shard_map/ppermute | solution.py:18
  113.3 3.2 %collective-permute-start.29 = (f32[128,256]{1,0:T(8,128)S(1)}, f32[128,256]{1,0:T(8,128)S(1)}, u32[]{:S(2)}, u32[]{:S(2)}) collective-permute-start(f32[128,256]{1,0:T(8,128)S(1)} %get-tuple-element.14), channel_id=1, source_target_pairs={{0,16},{4,20},{8,24},{12,28},{16,0},{20,4},{24,8},{28,12},{1,17},{... | collective-permute-start | bytes 393224 | tf_op jit(solution)/shard_map/ppermute | solution.py:18
  117.2 18.4 %all-gather.1 = f32[8,1,256]{2,1,0:T(1,128)S(1)} all-gather(f32[1,1,256]{2,1,0:T(1,128)S(1)} %slice_bitcast_fusion), channel_id=1, replica_groups=mesh['ylo'=2,'x'=4,'z'=8,'yhi'=2,'core'=2] {'z'}, dimensions={0}, use_global_device_ids=true | all-gather | bytes 9216 | tf_op jit(solution)/shard_map/all_gather | solution.py:168
  137.2 2.4 %shard_map.44 = f32[128,2048]{1,0:T(8,128)} custom-call(f32[128,256]{1,0:T(8,128)} %get-tuple-element.19.refs_0_, f32[128,256]{1,0:T(8,128)} %copy-done.16, f32[128,256]{1,0:T(8,128)} %copy-done.17, f32[128,256]{1,0:T(8,128)} %copy-done.14, f32[128,256]{1,0:T(8,128)} %copy-done.15, f32[128,256]{1,0:T(8,128)} %copy-done.18, f32[128,256]{1,0:T(8,128)} %copy-done.19, ...), custom_call_target="tpu_custom_call" | custom-call | bytes 2097152 | tf_op jit(solution)/shard_map/pallas_call | solution.py:144
  (109 shorter events, 27.4 us)
Async XLA Ops:
  0.6 14.0 %collective-permute-start.6 = (bf16[128,2048]{1,0:T(8,128)(2,1)}, bf16[128,2048]{1,0:T(8,128)(2,1)S(1)}, u32[]{:S(2)}, u32[]{:S(2)}) collective-permute-start(bf16[128,2048]{1,0:T(8,128)(2,1)} %refs_1_.1), channel_id=1, source_target_pairs={{0,128},{128,0},{1,129},{129,1},{2,130},{130,2},{3,131},{131,3},{4... | collective-permute-start | bytes 1572872 | tf_op jit(solution)/shard_map/ppermute | solution.py:18
  2.0 17.7 %collective-permute-start = (bf16[128,2048]{1,0:T(8,128)(2,1)}, bf16[128,2048]{1,0:T(8,128)(2,1)S(1)}, u32[]{:S(2)}, u32[]{:S(2)}) collective-permute-start(bf16[128,2048]{1,0:T(8,128)(2,1)} %refs_1_.1), channel_id=1, source_target_pairs={{0,4},{4,8},{8,12},{12,16},{16,20},{20,24},{24,28},{28,0},{1,5},{5... | collective-permute-start | bytes 1572872 | tf_op jit(solution)/shard_map/ppermute | solution.py:18
  3.9 18.6 %collective-permute-start.1 = (bf16[128,2048]{1,0:T(8,128)(2,1)}, bf16[128,2048]{1,0:T(8,128)(2,1)S(1)}, u32[]{:S(2)}, u32[]{:S(2)}) collective-permute-start(bf16[128,2048]{1,0:T(8,128)(2,1)} %refs_1_.1), channel_id=1, source_target_pairs={{0,28},{4,0},{8,4},{12,8},{16,12},{20,16},{24,20},{28,24},{1,29},{... | collective-permute-start | bytes 1572872 | tf_op jit(solution)/shard_map/ppermute | solution.py:18
  7.9 16.3 %collective-permute-start.2 = (bf16[128,2048]{1,0:T(8,128)(2,1)}, bf16[128,2048]{1,0:T(8,128)(2,1)S(1)}, u32[]{:S(2)}, u32[]{:S(2)}) collective-permute-start(bf16[128,2048]{1,0:T(8,128)(2,1)} %refs_1_.1), channel_id=1, source_target_pairs={{0,32},{32,64},{64,96},{96,0},{1,33},{33,65},{65,97},{97,1},{2,34}... | collective-permute-start | bytes 1572872 | tf_op jit(solution)/shard_map/ppermute | solution.py:18
  9.3 16.4 %collective-permute-start.3 = (bf16[128,2048]{1,0:T(8,128)(2,1)}, bf16[128,2048]{1,0:T(8,128)(2,1)S(1)}, u32[]{:S(2)}, u32[]{:S(2)}) collective-permute-start(bf16[128,2048]{1,0:T(8,128)(2,1)} %refs_1_.1), channel_id=1, source_target_pairs={{0,96},{32,0},{64,32},{96,64},{1,97},{33,1},{65,33},{97,65},{2,98}... | collective-permute-start | bytes 1572872 | tf_op jit(solution)/shard_map/ppermute | solution.py:18
  14.6 20.8 %collective-permute-start.7 = (bf16[128,2048]{1,0:T(8,128)(2,1)S(1)}, bf16[128,2048]{1,0:T(8,128)(2,1)S(1)}, u32[]{:S(2)}, u32[]{:S(2)}) collective-permute-start(bf16[128,2048]{1,0:T(8,128)(2,1)S(1)} %collective-permute-done.6.refs_8_.refs_7_.refs_9_.refs_6_), channel_id=1, source_target_pairs={{0,32},{32,64},{64,96},{96,0},{1,33},{33,65},{65,97},{97,1},{2,34}... | collective-permute-start | bytes 1572872 | tf_op jit(solution)/shard_map/ppermute | solution.py:18
  19.7 17.2 %collective-permute-start.8 = (bf16[128,2048]{1,0:T(8,128)(2,1)S(1)}, bf16[128,2048]{1,0:T(8,128)(2,1)S(1)}, u32[]{:S(2)}, u32[]{:S(2)}) collective-permute-start(bf16[128,2048]{1,0:T(8,128)(2,1)S(1)} %collective-permute-done.6.refs_8_.refs_7_.refs_9_.refs_6_), channel_id=1, source_target_pairs={{0,96},{32,0},{64,32},{96,64},{1,97},{33,1},{65,33},{97,65},{2,98}... | collective-permute-start | bytes 1572872 | tf_op jit(solution)/shard_map/ppermute | solution.py:18
  22.5 20.1 %collective-permute-start.15 = (bf16[128,2048]{1,0:T(8,128)(2,1)S(1)}, bf16[128,2048]{1,0:T(8,128)(2,1)S(1)}, u32[]{:S(2)}, u32[]{:S(2)}) collective-permute-start(bf16[128,2048]{1,0:T(8,128)(2,1)S(1)} %collective-permute-done.refs_1_), channel_id=1, source_target_pairs={{0,4},{4,8},{8,12},{12,16},{16,20},{20,24},{24,28},{28,0},{1,5},{5... | collective-permute-start | bytes 1572872 | tf_op jit(solution)/shard_map/ppermute | solution.py:18
  24.1 18.4 %collective-permute-start.16 = (bf16[128,2048]{1,0:T(8,128)(2,1)S(1)}, bf16[128,2048]{1,0:T(8,128)(2,1)S(1)}, u32[]{:S(2)}, u32[]{:S(2)}) collective-permute-start(bf16[128,2048]{1,0:T(8,128)(2,1)S(1)} %collective-permute-done.1.refs_2_), channel_id=1, source_target_pairs={{0,28},{4,0},{8,4},{12,8},{16,12},{20,16},{24,20},{28,24},{1,29},{... | collective-permute-start | bytes 1572872 | tf_op jit(solution)/shard_map/ppermute | solution.py:18
  25.8 15.2 %collective-permute-start.4 = (bf16[64,2048]{1,0:T(8,128)(2,1)S(1)}, bf16[64,2048]{1,0:T(8,128)(2,1)S(1)}, u32[]{:S(2)}, u32[]{:S(2)}) collective-permute-start(bf16[64,2048]{1,0:T(8,128)(2,1)S(1)} %slice.84), channel_id=1, source_target_pairs={{0,32},{32,64},{64,96},{96,0},{1,33},{33,65},{65,97},{97,1},{2,34}... | collective-permute-start | bytes 786440 | tf_op jit(solution)/shard_map/ppermute | solution.py:18
  42.6 11.5 %collective-permute-start.22 = (bf16[128,2048]{1,0:T(8,128)(2,1)S(1)}, bf16[128,2048]{1,0:T(8,128)(2,1)S(1)}, u32[]{:S(2)}, u32[]{:S(2)}) collective-permute-start(bf16[128,2048]{1,0:T(8,128)(2,1)S(1)} %collective-permute-done.16.refs_1_), channel_id=1, source_target_pairs={{0,28},{4,0},{8,4},{12,8},{16,12},{20,16},{24,20},{28,24},{1,29},{... | collective-permute-start | bytes 1572872 | tf_op jit(solution)/shard_map/ppermute | solution.py:18
  50.5 39.2 %collective-permute-start.11 = (f32[384,512]{1,0:T(8,128)}, f32[384,512]{1,0:T(8,128)}, u32[]{:S(2)}, u32[]{:S(2)}) collective-permute-start(f32[384,512]{1,0:T(8,128)} %get-tuple-element.9), channel_id=1, source_target_pairs={{0,1},{1,0},{2,3},{3,2},{4,5},{5,4},{6,7},{7,6},{8,9},{9,8},{10,11... | collective-permute-start | bytes 2359304 | tf_op jit(solution)/shard_map/ppermute | solution.py:18
  52.4 13.5 %collective-permute-start.17 = (f32[256,512]{1,0:T(8,128)S(1)}, f32[256,512]{1,0:T(8,128)S(1)}, u32[]{:S(2)}, u32[]{:S(2)}) collective-permute-start(f32[256,512]{1,0:T(8,128)S(1)} %get-tuple-element.11), channel_id=1, source_target_pairs={{0,1},{1,0},{2,3},{3,2},{4,5},{5,4},{6,7},{7,6},{8,9},{9,8},{10,11... | collective-permute-start | bytes 1572872 | tf_op jit(solution)/shard_map/ppermute | solution.py:18
  65.8 30.5 %collective-permute-start.25 = (f32[384,512]{1,0:T(8,128)}, f32[384,512]{1,0:T(8,128)S(1)}, u32[]{:S(2)}, u32[]{:S(2)}) collective-permute-start(f32[384,512]{1,0:T(8,128)} %get-tuple-element.13), channel_id=1, source_target_pairs={{0,1},{1,0},{2,3},{3,2},{4,5},{5,4},{6,7},{7,6},{8,9},{9,8},{10,11... | collective-permute-start | bytes 2359304 | tf_op jit(solution)/shard_map/ppermute | solution.py:18
  66.7 26.5 %collective-permute-start.18 = (f32[256,256]{1,0:T(8,128)S(1)}, f32[256,256]{1,0:T(8,128)S(1)}, u32[]{:S(2)}, u32[]{:S(2)}) collective-permute-start(f32[256,256]{1,0:T(8,128)S(1)} %slice.94), channel_id=1, source_target_pairs={{0,2},{2,0},{1,3},{3,1},{4,6},{6,4},{5,7},{7,5},{8,10},{10,8},{9,1... | collective-permute-start | bytes 786440 | tf_op jit(solution)/shard_map/ppermute | solution.py:18
  91.1 13.1 %collective-permute-start.12 = (f32[384,256]{1,0:T(8,128)S(1)}, f32[384,256]{1,0:T(8,128)S(1)}, u32[]{:S(2)}, u32[]{:S(2)}) collective-permute-start(f32[384,256]{1,0:T(8,128)S(1)} %slice.89), channel_id=1, source_target_pairs={{0,2},{2,0},{1,3},{3,1},{4,6},{6,4},{5,7},{7,5},{8,10},{10,8},{9,1... | collective-permute-start | bytes 1179656 | tf_op jit(solution)/shard_map/ppermute | solution.py:18
  93.3 18.3 %collective-permute-start.19 = (f32[128,256]{1,0:T(8,128)S(1)}, f32[128,256]{1,0:T(8,128)S(1)}, u32[]{:S(2)}, u32[]{:S(2)}) collective-permute-start(f32[128,256]{1,0:T(8,128)S(1)} %get-tuple-element.21), channel_id=1, source_target_pairs={{0,24},{4,28},{8,0},{12,4},{16,8},{20,12},{24,16},{28,20},{1,25},{... | collective-permute-start | bytes 393224 | tf_op jit(solution)/shard_map/ppermute | solution.py:18
  95.1 18.3 %collective-permute-start.20 = (f32[128,256]{1,0:T(8,128)S(1)}, f32[128,256]{1,0:T(8,128)S(1)}, u32[]{:S(2)}, u32[]{:S(2)}) collective-permute-start(f32[128,256]{1,0:T(8,128)S(1)} %get-tuple-element.20), channel_id=1, source_target_pairs={{0,8},{4,12},{8,16},{12,20},{16,24},{20,28},{24,0},{28,4},{1,9},{5... | collective-permute-start | bytes 393224 | tf_op jit(solution)/shard_map/ppermute | solution.py:18
  96.5 12.0 %collective-permute-start.26 = (f32[384,256]{1,0:T(8,128)S(1)}, f32[384,256]{1,0:T(8,128)S(1)}, u32[]{:S(2)}, u32[]{:S(2)}) collective-permute-start(f32[384,256]{1,0:T(8,128)S(1)} %slice.100), channel_id=1, source_target_pairs={{0,2},{2,0},{1,3},{3,1},{4,6},{6,4},{5,7},{7,5},{8,10},{10,8},{9,1... | collective-permute-start | bytes 1179656 | tf_op jit(solution)/shard_map/ppermute | solution.py:18
  105.0 31.3 %collective-permute-start.13 = (f32[128,256]{1,0:T(8,128)S(1)}, f32[128,256]{1,0:T(8,128)S(1)}, u32[]{:S(2)}, u32[]{:S(2)}) collective-permute-start(f32[128,256]{1,0:T(8,128)S(1)} %get-tuple-element.18), channel_id=1, source_target_pairs={{0,28},{4,0},{8,4},{12,8},{16,12},{20,16},{24,20},{28,24},{1,29},{... | collective-permute-start | bytes 393224 | tf_op jit(solution)/shard_map/ppermute | solution.py:18
  107.8 28.5 %collective-permute-start.14 = (f32[128,256]{1,0:T(8,128)S(1)}, f32[128,256]{1,0:T(8,128)S(1)}, u32[]{:S(2)}, u32[]{:S(2)}) collective-permute-start(f32[128,256]{1,0:T(8,128)S(1)} %get-tuple-element.17), channel_id=1, source_target_pairs={{0,4},{4,8},{8,12},{12,16},{16,20},{20,24},{24,28},{28,0},{1,5},{5... | collective-permute-start | bytes 393224 | tf_op jit(solution)/shard_map/ppermute | solution.py:18
  108.6 27.7 %collective-permute-start.27 = (f32[128,256]{1,0:T(8,128)S(1)}, f32[128,256]{1,0:T(8,128)S(1)}, u32[]{:S(2)}, u32[]{:S(2)}) collective-permute-start(f32[128,256]{1,0:T(8,128)S(1)} %get-tuple-element.16), channel_id=1, source_target_pairs={{0,20},{4,24},{8,28},{12,0},{16,4},{20,8},{24,12},{28,16},{1,21},{... | collective-permute-start | bytes 393224 | tf_op jit(solution)/shard_map/ppermute | solution.py:18
  111.6 24.7 %collective-permute-start.28 = (f32[128,256]{1,0:T(8,128)S(1)}, f32[128,256]{1,0:T(8,128)S(1)}, u32[]{:S(2)}, u32[]{:S(2)}) collective-permute-start(f32[128,256]{1,0:T(8,128)S(1)} %get-tuple-element.15), channel_id=1, source_target_pairs={{0,12},{4,16},{8,20},{12,24},{16,28},{20,0},{24,4},{28,8},{1,13},{... | collective-permute-start | bytes 393224 | tf_op jit(solution)/shard_map/ppermute | solution.py:18
  113.3 23.0 %collective-permute-start.29 = (f32[128,256]{1,0:T(8,128)S(1)}, f32[128,256]{1,0:T(8,128)S(1)}, u32[]{:S(2)}, u32[]{:S(2)}) collective-permute-start(f32[128,256]{1,0:T(8,128)S(1)} %get-tuple-element.14), channel_id=1, source_target_pairs={{0,16},{4,20},{8,24},{12,28},{16,0},{20,4},{24,8},{28,12},{1,17},{... | collective-permute-start | bytes 393224 | tf_op jit(solution)/shard_map/ppermute | solution.py:18
  (28 other events, 384.8 us)

commit v2 on v0

v2 whole, which is shorter than its diff:
```python
import math

import jax
import jax.numpy as jnp
from jax import lax
from jax.experimental import pallas as pl
from jax.experimental.pallas import tpu as pltpu
from jax.sharding import Mesh, PartitionSpec as P

AXES = ("ylo", "x", "z", "yhi", "core")
SIZES = (2, 4, 8, 2, 2)
ROWS, PANEL = 128, 2048
NX, NZ = 4, 8
F32 = jnp.float32
GROUPS = ((0, 1, -1), (2, -2, 3, -3, 4))
VMEM = pl.BlockSpec(memory_space=pltpu.VMEM)
ANYWHERE = pl.BlockSpec(memory_space=pl.ANY)
SMALL = pltpu.CompilerParams(vmem_limit_bytes=16 * 2**20)


def shift(value, axis, by):
    size = SIZES[AXES.index(axis)]
    pairs = [(2 * i + c, 2 * ((i + (by, -by)[c]) % size) + c) for i in range(size) for c in range(2)]
    return lax.ppermute(value, (axis, "core"), pairs)


def swap(value, axis):
    return lax.ppermute(value, axis, [(0, 1), (1, 0)])


def turn(by):
    return by * (1 - 2 * lax.axis_index("core"))


def after(value, *others):
    return lax.optimization_barrier((value, *others))[0]


def gather(log_derivs, packed):
    rows = {0: log_derivs}
    rows[1], rows[-1] = shift(log_derivs, "z", 1), shift(log_derivs, "z", -1)
    partner = swap(packed, "ylo")
    columns = {(0, 0): packed, (1, 0): partner}
    for by in (1, -1):
        columns[0, by] = shift(packed, "x", by)
    rows[2], rows[-2] = shift(rows[1], "z", 1), shift(rows[-1], "z", -1)
    for by in (1, -1):
        columns[1, by] = shift(partner, "x", by)
    rows[3], rows[-3] = shift(rows[2], "z", 1), shift(rows[-2], "z", -1)
    columns[0, 2] = shift(columns[0, 1], "x", 1)
    columns[1, 2] = shift(columns[1, 1], "x", 1)
    rows[4] = shift(rows[3], "z", 1)
    return rows, columns


def pack(log_derivs, sample_vector):
    def kernel(entries, vec, out):
        out[:, :PANEL] = entries[...]
        left = jnp.transpose(jnp.broadcast_to(vec[...], (ROWS, ROWS)))
        lane = lax.broadcasted_iota(jnp.int32, (ROWS, ROWS), 1)
        parts = jnp.zeros((ROWS, ROWS), F32)
        for i in range(3):
            part = left.astype(jnp.bfloat16).astype(F32)
            left = left - part
            parts = jnp.where(lane == i, part, parts)
        out[:, PANEL:] = parts.astype(jnp.bfloat16)

    return pl.pallas_call(
        kernel,
        out_shape=jax.ShapeDtypeStruct((ROWS, PANEL + ROWS), jnp.bfloat16),
        in_specs=[VMEM] * 2,
        out_specs=VMEM,
        compiler_params=SMALL,
        cost_estimate=pl.CostEstimate(flops=0, bytes_accessed=2**20, transcendentals=0),
    )(log_derivs, sample_vector[None])


def products(scale, rows, columns):
    m, n = ROWS * len(rows), len(rows)

    def kernel(*refs):
        cols = refs[n : n + len(columns)]
        keep, send, held, sems = refs[n + len(columns) :]
        copies = []
        for i, (ref, (ylo, back)) in enumerate(zip(cols, columns)):
            x = lax.rem(lax.axis_index("x") + NX - turn(back), NX)
            core = lax.rem(lax.div(x, 2) + lax.axis_index("core"), 2)
            yhi = lax.rem(lax.axis_index("ylo") + ylo + lax.axis_index("yhi"), 2)
            to = pl.multiple_of(lax.rem(x, 2) * ROWS, ROWS)
            copy = pltpu.make_async_copy(
                ref.at[:, pl.ds(0, PANEL)], held.at[2 * core + yhi, pl.ds(to, ROWS)], sems.at[i]
            )
            copy.start()
            copies.append(copy)
        for copy in copies:
            copy.wait()
        block = jnp.concatenate([r[...] for r in refs[:n]], axis=0)
        for pair in range(4):
            out = keep if pair < 2 else send
            out[:, 256 * (pair % 2) : 256 * (pair % 2) + 256] = scale * lax.dot_general(
                block, held[pair], (((1,), (1,)), ((), ())), preferred_element_type=F32
            )

    out = jax.ShapeDtypeStruct((m, 512), F32)
    return pl.pallas_call(
        kernel,
        out_shape=(out, out),
        in_specs=[VMEM] * n + [ANYWHERE] * len(columns),
        out_specs=(VMEM, VMEM),
        scratch_shapes=[
            pltpu.VMEM((4, 256, PANEL), jnp.bfloat16),
            pltpu.SemaphoreType.DMA((len(columns),)),
        ],
        compiler_params=pltpu.CompilerParams(vmem_limit_bytes=24 * 2**20),
        cost_estimate=pl.CostEstimate(
            flops=2 * m * 1024 * PANEL, bytes_accessed=2**22 + m * 8192, transcendentals=0
        ),
    )(*rows, *columns.values())


def term(scale, columns):
    def kernel(*refs):
        cols = refs[: len(columns)]
        out, held, vecs, sems = refs[len(columns) :]
        u = lax.axis_index("ylo") * NX + lax.axis_index("x")
        mine = pl.multiple_of(u * 256, 256)
        copies = []
        for i, ref in enumerate(cols):
            for j, (part, target) in enumerate(((pl.ds(mine, 256), held), (pl.ds(PANEL, ROWS), vecs))):
                copy = pltpu.make_async_copy(
                    ref.at[:, part], target.at[pl.ds(ROWS * i, ROWS)], sems.at[2 * i + j]
                )
                copy.start()
                copies.append(copy)
        for copy in copies:
            copy.wait()
        parts = lax.dot_general(
            vecs[...], held[...], (((0,), (0,)), ((), ())), preferred_element_type=F32
        )
        out[...] = jnp.broadcast_to(scale * jnp.sum(parts, axis=0, keepdims=True), (8, 256))

    return pl.pallas_call(
        kernel,
        out_shape=jax.ShapeDtypeStruct((8, 256), F32),
        in_specs=[ANYWHERE] * len(columns),
        out_specs=VMEM,
        scratch_shapes=[
            pltpu.VMEM((8 * ROWS, 256), jnp.bfloat16),
            pltpu.VMEM((8 * ROWS, ROWS), jnp.bfloat16),
            pltpu.SemaphoreType.DMA((2 * len(columns),)),
        ],
        compiler_params=SMALL,
        cost_estimate=pl.CostEstimate(flops=2**26, bytes_accessed=2**20, transcendentals=0),
    )(*columns.values())


def peak(value):
    top = jnp.maximum(jnp.max(jnp.abs(value)), 1e-30)
    return jnp.broadcast_to(top, (16, 256)).astype(jnp.bfloat16)


def encode(value, top):
    power = value * (2.0**15 / top.astype(F32)[:1])
    for _ in range(3):
        power = power * power
    return jnp.where(value < 0, -power, power).astype(jnp.bfloat16)


def decode(code, top):
    code = code.astype(F32)
    root = jnp.abs(code)
    for _ in range(3):
        root = jnp.sqrt(root)
    return jnp.where(code < 0, -root, root) * (top.astype(F32)[:1] * 2.0**-15)


def split_yhi(keep, received, backs):
    m = keep.shape[0]
    order = [backs.index(-back if -back in backs else back) for back in backs]

    def kernel(a, b, own, code):
        b = jnp.concatenate([b[ROWS * i : ROWS * (i + 1)] for i in order], axis=0)
        own[...] = a[:, :256] + b[:, :256]
        other = a[:, 256:] + b[:, 256:]
        top = peak(other)
        code[:m] = encode(other, top)
        code[m:] = top

    return pl.pallas_call(
        kernel,
        out_shape=(
            jax.ShapeDtypeStruct((m, 256), F32),
            jax.ShapeDtypeStruct((m + 16, 256), jnp.bfloat16),
        ),
        in_specs=[VMEM] * 2,
        out_specs=(VMEM, VMEM),
        compiler_params=SMALL,
        cost_estimate=pl.CostEstimate(flops=0, bytes_accessed=m * 6000, transcendentals=0),
    )(keep, received)


def split_z(own, received, last_rows, backs):
    m = own.shape[0]

    def kernel(own, code, rows, *outs):
        full = own[...] + decode(code[:m], code[m:])
        left, parts = rows[:1], []
        for _ in range(3):
            parts.append(left.astype(jnp.bfloat16).astype(F32))
            left = left - parts[-1]
        row = lax.broadcasted_iota(jnp.int32, (16, 256), 0)
        for i, (back, out) in enumerate(zip(backs, outs)):
            block = full[ROWS * i : ROWS * (i + 1)]
            if back == 0:
                out[...] = block
                continue
            top = peak(block)
            out[:ROWS] = encode(block, top)
            tail = jnp.where(row == 0, top.astype(F32), 0.0)
            for j in range(3):
                tail = jnp.where(row == j + 1, parts[j], tail)
            out[ROWS:] = tail.astype(jnp.bfloat16)

    whole = jax.ShapeDtypeStruct((ROWS, 256), F32)
    coded = jax.ShapeDtypeStruct((ROWS + 16, 256), jnp.bfloat16)
    return pl.pallas_call(
        kernel,
        out_shape=tuple(coded if back else whole for back in backs),
        in_specs=[VMEM] * 3,
        out_specs=tuple(VMEM for _ in backs),
        compiler_params=SMALL,
        cost_estimate=pl.CostEstimate(flops=0, bytes_accessed=m * 2000, transcendentals=0),
    )(own, received, last_rows)


def place(blocks, backs, last_rows):
    def kernel(*refs):
        rows, out, update = refs[len(blocks) :]
        total = rows[:1]
        for block, back in zip(refs, backs):
            z = lax.rem(lax.axis_index("z") + NZ + turn(back), NZ)
            at = pl.multiple_of(z * ROWS, ROWS)
            if back:
                tail = block[ROWS:]
                value = decode(block[:ROWS], tail)
                total = total + jnp.sum(tail[1:4].astype(F32), axis=0, keepdims=True)
            else:
                value = block[...]
            out[:, pl.ds(at, ROWS)] = value[:, :ROWS]
            out[:, pl.ds(at + NZ * ROWS, ROWS)] = value[:, ROWS:]
        owned = jnp.zeros((1, 32), F32)
        for z in range(NZ):
            owned = jnp.where(lax.axis_index("z") == z, total[:, 32 * z : 32 * z + 32], owned)
        update[...] = owned

    return pl.pallas_call(
        kernel,
        out_shape=(
            jax.ShapeDtypeStruct((ROWS, PANEL), F32),
            jax.ShapeDtypeStruct((1, 32), F32),
        ),
        in_specs=[VMEM] * (len(blocks) + 1),
        out_specs=(VMEM, VMEM),
        compiler_params=SMALL,
        cost_estimate=pl.CostEstimate(flops=0, bytes_accessed=2**21, transcendentals=0),
    )(*blocks, last_rows)


def body(log_derivs, sample_vector):
    scale_gram = 1.0 / math.sqrt(PANEL * 4)
    scale_update = 1.0 / math.sqrt(ROWS * 64)

    rows, columns = gather(log_derivs, pack(log_derivs, sample_vector))
    last_rows = term(scale_update, columns)

    blocks = {}
    for backs in GROUPS:
        keep, send = products(scale_gram, [rows[back] for back in backs], columns)
        own, code = split_yhi(keep, swap(send, "core"), backs)
        for back, block in zip(backs, split_z(own, swap(code, "yhi"), last_rows, backs)):
            blocks[back] = shift(block, "z", -back) if back else block
    return place(blocks.values(), list(blocks), last_rows)


def solution(mesh):
    fine = Mesh(mesh.devices.reshape(SIZES), AXES)
    samp, par = AXES[:3], AXES[3:]
    return jax.shard_map(
        body,
        mesh=fine,
        in_specs=(P(samp, par), P(samp)),
        out_specs=(P(samp, par), P(par, samp)),
        check_vma=False,
    )
```

time: 769 us -> 108 us (0.14)
  waiting for transfers between devices: 727 us -> 44.5 us
  starting transfers between devices: 0.12 us -> 48.8 us
  matrix products: 20.5 us -> 0 us
  between operations: 13.8 us -> 0.74 us
  Pallas kernels: 0 us -> 10.7 us
    all_gather x1 -> x0, waiting for transfers between devices: 380 us -> none  [body(): lax.all_gather(log_derivs, 'samp', axis=0, tiled=True)]
    unnamed x4 -> x0, waiting for transfers between devices: 297 us -> none
    reduce_scatter x1 -> x0, waiting for transfers between devices: 49.6 us -> none  [body(): lax.psum_scatter(tile, 'par', scatter_dimension=1, tiled=True)]
    ppermute x0 -> x25, starting transfers between devices: none -> 48.8 us  [the longest x20 44.2 us: shift(): return lax.ppermute(value, (axis, 'core'), pairs)]
    ppermute x0 -> x25, waiting for transfers between devices: none -> 44.5 us  [the longest x20 32 us: shift(): return lax.ppermute(value, (axis, 'core'), pairs)]
    dot_general x1 -> x0, matrix products: 17.8 us -> none  [body(): lax.dot_general(log_derivs, lax.all_gather(log_derivs, 'samp', axis=0, ti...]
    pallas_call x0 -> x9, Pallas kernels: none -> 10.7 us  [the longest x2 5.58 us: products(): pl.pallas_call(kernel, out_shape=(out, out), in_specs=[VMEM] * n + [ANYWH...]
  transfers between devices with their start and end apart: 3 -> 25, of which waited for: 3 -> 12; matrix products, arithmetic and copies ran while one was open for 3% -> 0% of each run, Pallas kernels for 0% -> 5%
where the time goes in v2:
time: 108 us; the launch traced here: 107 us
  starting transfers between devices  48.8 us (45%)
  waiting for transfers between devices  44.5 us (41%)
  Pallas kernels  10.7 us (10%)
  local copies, waits for them, and re-layouts  1.74 us (2%)
    ppermute x20, starting transfers between devices, shift(): return lax.ppermute(value, (axis, 'core'), pairs)  44.2 us
    ppermute x20, waiting for transfers between devices, shift(): return lax.ppermute(value, (axis, 'core'), pairs)  32 us
    ppermute x5, waiting for transfers between devices, swap(): return lax.ppermute(value, axis, [(0, 1), (1, 0)])  12.5 us
    pallas_call x2, Pallas kernels, products(): pl.pallas_call(kernel, out_shape=(out, out), in_specs=[VMEM] * n + [ANYWH...  5.58 us
    ppermute x5, starting transfers between devices, swap(): return lax.ppermute(value, axis, [(0, 1), (1, 0)])  4.68 us
  transfers between devices with their start and end apart: 25, of which 12 were waited for; matrix products, arithmetic and copies ran while one was open for 0% of the time, Pallas kernels for 5%

profile of v2, /device:TPU:16, one launch (start us, length us, event | category | flops | bytes accessed | tf_op | source)
XLA Modules:
  0.0 106.6 jit_solution(2229748664711261676)
XLA Ops:
  0.6 2.0 %collective-permute-start = (bf16[128,2048]{1,0:T(8,128)(2,1)}, bf16[128,2048]{1,0:T(8,128)(2,1)S(1)}, u32[]{:S(2)}, u32[]{:S(2)}) collective-permute-start(bf16[128,2048]{1,0:T(8,128)(2,1)} %refs_0_.1), channel_id=1, source_target_pairs={{0,4},{1,29},{4,8},{5,1},{8,12},{9,5},{12,16},{13,9},{16,20},{17,1... | collective-permute-start | bytes 1572872 | tf_op jit(solution)/shard_map/ppermute | solution.py:24
  5.8 3.9 %collective-permute-start.1 = (bf16[128,2048]{1,0:T(8,128)(2,1)S(1)}, bf16[128,2048]{1,0:T(8,128)(2,1)S(1)}, u32[]{:S(2)}, u32[]{:S(2)}) collective-permute-start(bf16[128,2048]{1,0:T(8,128)(2,1)S(1)} %copy-done), channel_id=1, source_target_pairs={{0,28},{1,5},{4,0},{5,9},{8,4},{9,13},{12,8},{13,17},{16,12},{17,2... | collective-permute-start | bytes 1572872 | tf_op jit(solution)/shard_map/ppermute | solution.py:24
  9.8 5.1 %collective-permute-done.refs_1_ = bf16[128,2048]{1,0:T(8,128)(2,1)S(1)} collective-permute-done((bf16[128,2048]{1,0:T(8,128)(2,1)}, bf16[128,2048]{1,0:T(8,128)(2,1)S(1)}, u32[]{:S(2)}, u32[]{:S(2)}) %collective-permute-start) | collective-permute-done | bytes 524320 | tf_op jit(solution)/shard_map/ppermute | solution.py:24
  15.5 1.5 %collective-permute-start.3 = (bf16[128,2176]{1,0:T(8,128)(2,1)S(1)}, bf16[128,2176]{1,0:T(8,128)(2,1)S(1)}, u32[]{:S(2)}, u32[]{:S(2)}) collective-permute-start(bf16[128,2176]{1,0:T(8,128)(2,1)S(1)} %shard_map.41.refs_3_.refs_0_.refs_5_), channel_id=1, source_target_pairs={{0,32},{1,97},{32,64},{33,1},{64,96},{65,33},{96,0},{97,65},{2,34}... | collective-permute-start | bytes 1671176 | tf_op jit(solution)/shard_map/ppermute | solution.py:24
  17.0 1.7 %collective-permute-start.4 = (bf16[128,2176]{1,0:T(8,128)(2,1)S(1)}, bf16[128,2176]{1,0:T(8,128)(2,1)S(1)}, u32[]{:S(2)}, u32[]{:S(2)}) collective-permute-start(bf16[128,2176]{1,0:T(8,128)(2,1)S(1)} %shard_map.41.refs_3_.refs_0_.refs_5_), channel_id=1, source_target_pairs={{0,96},{1,33},{32,0},{33,65},{64,32},{65,97},{96,64},{97,1},{2,98}... | collective-permute-start | bytes 1671176 | tf_op jit(solution)/shard_map/ppermute | solution.py:24
  19.0 6.1 %collective-permute-start.14 = (bf16[128,2048]{1,0:T(8,128)(2,1)S(1)}, bf16[128,2048]{1,0:T(8,128)(2,1)S(1)}, u32[]{:S(2)}, u32[]{:S(2)}) collective-permute-start(bf16[128,2048]{1,0:T(8,128)(2,1)S(1)} %collective-permute-done.1.refs_2_), channel_id=1, source_target_pairs={{0,28},{1,5},{4,0},{5,9},{8,4},{9,13},{12,8},{13,17},{16,12},{17,2... | collective-permute-start | bytes 1572872 | tf_op jit(solution)/shard_map/ppermute | solution.py:24
  26.3 1.5 %collective-permute-start.15 = (bf16[128,2048]{1,0:T(8,128)(2,1)S(1)}, bf16[128,2048]{1,0:T(8,128)(2,1)S(1)}, u32[]{:S(2)}, u32[]{:S(2)}) collective-permute-start(bf16[128,2048]{1,0:T(8,128)(2,1)S(1)} %collective-permute-done.13.refs_0_), channel_id=1, source_target_pairs={{0,4},{1,29},{4,8},{5,1},{8,12},{9,5},{12,16},{13,9},{16,20},{17,1... | collective-permute-start | bytes 1572872 | tf_op jit(solution)/shard_map/ppermute | solution.py:24
  28.9 3.5 %collective-permute-start.6 = (bf16[128,2176]{1,0:T(8,128)(2,1)S(1)}, bf16[128,2176]{1,0:T(8,128)(2,1)S(1)}, u32[]{:S(2)}, u32[]{:S(2)}) collective-permute-start(bf16[128,2176]{1,0:T(8,128)(2,1)S(1)} %collective-permute-done.2.refs_4_.refs_1_.refs_6_), channel_id=1, source_target_pairs={{0,96},{1,33},{32,0},{33,65},{64,32},{65,97},{96,64},{97,1},{2,98}... | collective-permute-start | bytes 1671176 | tf_op jit(solution)/shard_map/ppermute | solution.py:24
  32.4 1.5 %collective-permute-start.7 = (bf16[128,2176]{1,0:T(8,128)(2,1)S(1)}, bf16[128,2176]{1,0:T(8,128)(2,1)S(1)}, u32[]{:S(2)}, u32[]{:S(2)}) collective-permute-start(bf16[128,2176]{1,0:T(8,128)(2,1)S(1)} %collective-permute-done.3.refs_5_.refs_2_.refs_7_), channel_id=1, source_target_pairs={{0,32},{1,97},{32,64},{33,1},{64,96},{65,33},{96,0},{97,65},{2,34}... | collective-permute-start | bytes 1671176 | tf_op jit(solution)/shard_map/ppermute | solution.py:24
  33.9 5.9 %collective-permute-done.5.refs_7_.refs_4_.refs_9_ = bf16[128,2176]{1,0:T(8,128)(2,1)S(1)} collective-permute-done((bf16[128,2176]{1,0:T(8,128)(2,1)S(1)}, bf16[128,2176]{1,0:T(8,128)(2,1)S(1)}, u32[]{:S(2)}, u32[]{:S(2)}) %collective-permute-start.5) | collective-permute-done | bytes 557088 | tf_op jit(solution)/shard_map/ppermute | solution.py:24
  39.9 1.7 %collective-permute-start.8 = (bf16[128,2176]{1,0:T(8,128)(2,1)S(1)}, bf16[128,2176]{1,0:T(8,128)(2,1)S(1)}, u32[]{:S(2)}, u32[]{:S(2)}) collective-permute-start(bf16[128,2176]{1,0:T(8,128)(2,1)S(1)} %collective-permute-done.5.refs_7_.refs_4_.refs_9_), channel_id=1, source_target_pairs={{0,32},{1,97},{32,64},{33,1},{64,96},{65,33},{96,0},{97,65},{2,34}... | collective-permute-start | bytes 1671176 | tf_op jit(solution)/shard_map/ppermute | solution.py:24
  41.5 6.2 %collective-permute-start.16 = (bf16[128,2048]{1,0:T(8,128)(2,1)S(1)}, bf16[128,2048]{1,0:T(8,128)(2,1)S(1)}, u32[]{:S(2)}, u32[]{:S(2)}) collective-permute-start(bf16[128,2048]{1,0:T(8,128)(2,1)S(1)} %collective-permute-done.14.refs_1_), channel_id=1, source_target_pairs={{0,28},{1,5},{4,0},{5,9},{8,4},{9,13},{12,8},{13,17},{16,12},{17,2... | collective-permute-start | bytes 1572872 | tf_op jit(solution)/shard_map/ppermute | solution.py:24
  47.7 2.4 %collective-permute-done.7.refs_9_.refs_6_.refs_11_ = bf16[128,2176]{1,0:T(8,128)(2,1)S(1)} collective-permute-done((bf16[128,2176]{1,0:T(8,128)(2,1)S(1)}, bf16[128,2176]{1,0:T(8,128)(2,1)S(1)}, u32[]{:S(2)}, u32[]{:S(2)}) %collective-permute-start.7) | collective-permute-done | bytes 557088 | tf_op jit(solution)/shard_map/ppermute | solution.py:24
  50.1 9.6 %collective-permute-done.16.refs_3_ = bf16[128,2048]{1,0:T(8,128)(2,1)S(1)} collective-permute-done((bf16[128,2048]{1,0:T(8,128)(2,1)S(1)}, bf16[128,2048]{1,0:T(8,128)(2,1)S(1)}, u32[]{:S(2)}, u32[]{:S(2)}) %collective-permute-start.16) | collective-permute-done | bytes 524320 | tf_op jit(solution)/shard_map/ppermute | solution.py:24
  60.5 3.3 %shard_map.46 = (f32[640,512]{1,0:T(8,128)S(1)}, f32[640,512]{1,0:T(8,128)S(1)}) custom-call(bf16[128,2048]{1,0:T(8,128)(2,1)S(1)} %collective-permute-done.13.refs_0_, bf16[128,2048]{1,0:T(8,128)(2,1)S(1)} %collective-permute-done.14.refs_1_, bf16[128,2048]{1,0:T(8,128)(2,1)S(1)} %collective-permute-done.15.refs_2_, ...), custom_call_target="tpu_custom_call" | custom-call | flops 2684354560 | bytes 9437184 | tf_op jit(solution)/shard_map/pallas_call | solution.py:105
  63.9 2.3 %shard_map.42 = (f32[384,512]{1,0:T(8,128)S(1)}, f32[384,512]{1,0:T(8,128)S(1)}) custom-call(bf16[128,2048]{1,0:T(8,128)(2,1)S(1)} %copy-done.1, bf16[128,2048]{1,0:T(8,128)(2,1)S(1)} %collective-permute-done.refs_1_, bf16[128,2048]{1,0:T(8,128)(2,1)S(1)} %collective-permute-done.1.refs_2_, bf16[128,2176]{1,0:T(8,128)(2,1)S(1)} %shard_map.41.refs_3_.refs_0_.refs_5_, ...), custom_call_target="tpu_custom_call" | custom-call | flops 1610612736 | bytes 7340032 | tf_op jit(solution)/shard_map/pallas_call | solution.py:105
  69.0 2.5 %collective-permute-start.10 = (bf16[400,256]{1,0:T(8,128)(2,1)S(1)}, bf16[400,256]{1,0:T(8,128)(2,1)S(1)}, u32[]{:S(2)}, u32[]{:S(2)}) collective-permute-start(bf16[400,256]{1,0:T(8,128)(2,1)S(1)} %get-tuple-element.21), channel_id=1, source_target_pairs={{0,2},{2,0},{1,3},{3,1},{4,6},{6,4},{5,7},{7,5},{8,10},{10,8},{9,1... | collective-permute-start | bytes 614408 | tf_op jit(solution)/shard_map/ppermute | solution.py:28
  72.1 11.3 %collective-permute-done.10.code = bf16[400,256]{1,0:T(8,128)(2,1)S(1)} collective-permute-done((bf16[400,256]{1,0:T(8,128)(2,1)S(1)}, bf16[400,256]{1,0:T(8,128)(2,1)S(1)}, u32[]{:S(2)}, u32[]{:S(2)}) %collective-permute-start.10) | collective-permute-done | bytes 204832 | tf_op jit(solution)/shard_map/ppermute | solution.py:28
  84.0 3.0 %collective-permute-start.11 = (bf16[144,256]{1,0:T(8,128)(2,1)S(1)}, bf16[144,256]{1,0:T(8,128)(2,1)S(1)}, u32[]{:S(2)}, u32[]{:S(2)}) collective-permute-start(bf16[144,256]{1,0:T(8,128)(2,1)S(1)} %get-tuple-element.23), channel_id=1, source_target_pairs={{0,28},{1,5},{4,0},{5,9},{8,4},{9,13},{12,8},{13,17},{16,12},{17,2... | collective-permute-start | bytes 221192 | tf_op jit(solution)/shard_map/ppermute | solution.py:24
  87.9 1.6 %collective-permute-start.20 = (bf16[144,256]{1,0:T(8,128)(2,1)S(1)}, bf16[144,256]{1,0:T(8,128)(2,1)S(1)}, u32[]{:S(2)}, u32[]{:S(2)}) collective-permute-start(bf16[144,256]{1,0:T(8,128)(2,1)S(1)} %get-tuple-element.29), channel_id=1, source_target_pairs={{0,24},{1,9},{4,28},{5,13},{8,0},{9,17},{12,4},{13,21},{16,8},{17,... | collective-permute-start | bytes 221192 | tf_op jit(solution)/shard_map/ppermute | solution.py:24
  90.9 2.8 %collective-permute-start.22 = (bf16[144,256]{1,0:T(8,128)(2,1)S(1)}, bf16[144,256]{1,0:T(8,128)(2,1)S(1)}, u32[]{:S(2)}, u32[]{:S(2)}) collective-permute-start(bf16[144,256]{1,0:T(8,128)(2,1)S(1)} %get-tuple-element.31), channel_id=1, source_target_pairs={{0,20},{1,13},{4,24},{5,17},{8,28},{9,21},{12,0},{13,25},{16,4},{1... | collective-permute-start | bytes 221192 | tf_op jit(solution)/shard_map/ppermute | solution.py:24
  94.8 3.9 %collective-permute-start.24 = (bf16[144,256]{1,0:T(8,128)(2,1)S(1)}, bf16[144,256]{1,0:T(8,128)(2,1)S(1)}, u32[]{:S(2)}, u32[]{:S(2)}) collective-permute-start(bf16[144,256]{1,0:T(8,128)(2,1)S(1)} %get-tuple-element.33), channel_id=1, source_target_pairs={{0,16},{1,17},{4,20},{5,21},{8,24},{9,25},{12,28},{13,29},{16,0},{... | collective-permute-start | bytes 221192 | tf_op jit(solution)/shard_map/ppermute | solution.py:24
  98.7 5.8 %collective-permute-done.23.refs_6_ = bf16[144,256]{1,0:T(8,128)(2,1)S(1)} collective-permute-done((bf16[144,256]{1,0:T(8,128)(2,1)S(1)}, bf16[144,256]{1,0:T(8,128)(2,1)S(1)}, u32[]{:S(2)}, u32[]{:S(2)}) %collective-permute-start.23) | collective-permute-done | bytes 73760 | tf_op jit(solution)/shard_map/ppermute | solution.py:24
  104.5 2.1 %shard_map.49 = (f32[128,2048]{1,0:T(8,128)}, f32[1,32]{1,0:T(1,128)}) custom-call(f32[128,256]{1,0:T(8,128)S(1)} %get-tuple-element.22.refs_0_, bf16[144,256]{1,0:T(8,128)(2,1)S(1)} %collective-permute-done.11.refs_1_, bf16[144,256]{1,0:T(8,128)(2,1)S(1)} %collective-permute-done.12.refs_2_, bf16[144,256]{1,0:T(8,128)(2,1)S(1)} %collective-permute-done.20.refs_3_, ...), custom_call_target="tpu_custom_call" | custom-call | bytes 2097152 | tf_op jit(solution)/shard_map/pallas_call | solution.py:256
  (41 shorter events, 14.5 us)
Async XLA Ops:
  0.6 14.3 %collective-permute-start = (bf16[128,2048]{1,0:T(8,128)(2,1)}, bf16[128,2048]{1,0:T(8,128)(2,1)S(1)}, u32[]{:S(2)}, u32[]{:S(2)}) collective-permute-start(bf16[128,2048]{1,0:T(8,128)(2,1)} %refs_0_.1), channel_id=1, source_target_pairs={{0,4},{1,29},{4,8},{5,1},{8,12},{9,5},{12,16},{13,9},{16,20},{17,1... | collective-permute-start | bytes 1572872 | tf_op jit(solution)/shard_map/ppermute | solution.py:24
  4.5 14.3 %collective-permute-start.2 = (bf16[128,2176]{1,0:T(8,128)(2,1)S(1)}, bf16[128,2176]{1,0:T(8,128)(2,1)S(1)}, u32[]{:S(2)}, u32[]{:S(2)}) collective-permute-start(bf16[128,2176]{1,0:T(8,128)(2,1)S(1)} %shard_map.41.refs_3_.refs_0_.refs_5_), channel_id=1, source_target_pairs={{0,128},{128,0},{1,129},{129,1},{2,130},{130,2},{3,131},{131,3},{4... | collective-permute-start | bytes 1671176 | tf_op jit(solution)/shard_map/ppermute | solution.py:28
  5.8 13.2 %collective-permute-start.1 = (bf16[128,2048]{1,0:T(8,128)(2,1)S(1)}, bf16[128,2048]{1,0:T(8,128)(2,1)S(1)}, u32[]{:S(2)}, u32[]{:S(2)}) collective-permute-start(bf16[128,2048]{1,0:T(8,128)(2,1)S(1)} %copy-done), channel_id=1, source_target_pairs={{0,28},{1,5},{4,0},{5,9},{8,4},{9,13},{12,8},{13,17},{16,12},{17,2... | collective-permute-start | bytes 1572872 | tf_op jit(solution)/shard_map/ppermute | solution.py:24
  14.9 11.4 %collective-permute-start.13 = (bf16[128,2048]{1,0:T(8,128)(2,1)S(1)}, bf16[128,2048]{1,0:T(8,128)(2,1)S(1)}, u32[]{:S(2)}, u32[]{:S(2)}) collective-permute-start(bf16[128,2048]{1,0:T(8,128)(2,1)S(1)} %collective-permute-done.refs_1_), channel_id=1, source_target_pairs={{0,4},{1,29},{4,8},{5,1},{8,12},{9,5},{12,16},{13,9},{16,20},{17,1... | collective-permute-start | bytes 1572872 | tf_op jit(solution)/shard_map/ppermute | solution.py:24
  15.5 13.4 %collective-permute-start.3 = (bf16[128,2176]{1,0:T(8,128)(2,1)S(1)}, bf16[128,2176]{1,0:T(8,128)(2,1)S(1)}, u32[]{:S(2)}, u32[]{:S(2)}) collective-permute-start(bf16[128,2176]{1,0:T(8,128)(2,1)S(1)} %shard_map.41.refs_3_.refs_0_.refs_5_), channel_id=1, source_target_pairs={{0,32},{1,97},{32,64},{33,1},{64,96},{65,33},{96,0},{97,65},{2,34}... | collective-permute-start | bytes 1671176 | tf_op jit(solution)/shard_map/ppermute | solution.py:24
  17.0 15.5 %collective-permute-start.4 = (bf16[128,2176]{1,0:T(8,128)(2,1)S(1)}, bf16[128,2176]{1,0:T(8,128)(2,1)S(1)}, u32[]{:S(2)}, u32[]{:S(2)}) collective-permute-start(bf16[128,2176]{1,0:T(8,128)(2,1)S(1)} %shard_map.41.refs_3_.refs_0_.refs_5_), channel_id=1, source_target_pairs={{0,96},{1,33},{32,0},{33,65},{64,32},{65,97},{96,64},{97,1},{2,98}... | collective-permute-start | bytes 1671176 | tf_op jit(solution)/shard_map/ppermute | solution.py:24
  18.7 21.1 %collective-permute-start.5 = (bf16[128,2176]{1,0:T(8,128)(2,1)S(1)}, bf16[128,2176]{1,0:T(8,128)(2,1)S(1)}, u32[]{:S(2)}, u32[]{:S(2)}) collective-permute-start(bf16[128,2176]{1,0:T(8,128)(2,1)S(1)} %collective-permute-done.2.refs_4_.refs_1_.refs_6_), channel_id=1, source_target_pairs={{0,32},{1,97},{32,64},{33,1},{64,96},{65,33},{96,0},{97,65},{2,34}... | collective-permute-start | bytes 1671176 | tf_op jit(solution)/shard_map/ppermute | solution.py:24
  19.0 22.5 %collective-permute-start.14 = (bf16[128,2048]{1,0:T(8,128)(2,1)S(1)}, bf16[128,2048]{1,0:T(8,128)(2,1)S(1)}, u32[]{:S(2)}, u32[]{:S(2)}) collective-permute-start(bf16[128,2048]{1,0:T(8,128)(2,1)S(1)} %collective-permute-done.1.refs_2_), channel_id=1, source_target_pairs={{0,28},{1,5},{4,0},{5,9},{8,4},{9,13},{12,8},{13,17},{16,12},{17,2... | collective-permute-start | bytes 1572872 | tf_op jit(solution)/shard_map/ppermute | solution.py:24
  26.3 21.4 %collective-permute-start.15 = (bf16[128,2048]{1,0:T(8,128)(2,1)S(1)}, bf16[128,2048]{1,0:T(8,128)(2,1)S(1)}, u32[]{:S(2)}, u32[]{:S(2)}) collective-permute-start(bf16[128,2048]{1,0:T(8,128)(2,1)S(1)} %collective-permute-done.13.refs_0_), channel_id=1, source_target_pairs={{0,4},{1,29},{4,8},{5,1},{8,12},{9,5},{12,16},{13,9},{16,20},{17,1... | collective-permute-start | bytes 1572872 | tf_op jit(solution)/shard_map/ppermute | solution.py:24
  28.9 18.8 %collective-permute-start.6 = (bf16[128,2176]{1,0:T(8,128)(2,1)S(1)}, bf16[128,2176]{1,0:T(8,128)(2,1)S(1)}, u32[]{:S(2)}, u32[]{:S(2)}) collective-permute-start(bf16[128,2176]{1,0:T(8,128)(2,1)S(1)} %collective-permute-done.2.refs_4_.refs_1_.refs_6_), channel_id=1, source_target_pairs={{0,96},{1,33},{32,0},{33,65},{64,32},{65,97},{96,64},{97,1},{2,98}... | collective-permute-start | bytes 1671176 | tf_op jit(solution)/shard_map/ppermute | solution.py:24
  32.4 17.7 %collective-permute-start.7 = (bf16[128,2176]{1,0:T(8,128)(2,1)S(1)}, bf16[128,2176]{1,0:T(8,128)(2,1)S(1)}, u32[]{:S(2)}, u32[]{:S(2)}) collective-permute-start(bf16[128,2176]{1,0:T(8,128)(2,1)S(1)} %collective-permute-done.3.refs_5_.refs_2_.refs_7_), channel_id=1, source_target_pairs={{0,32},{1,97},{32,64},{33,1},{64,96},{65,33},{96,0},{97,65},{2,34}... | collective-permute-start | bytes 1671176 | tf_op jit(solution)/shard_map/ppermute | solution.py:24
  39.9 19.9 %collective-permute-start.8 = (bf16[128,2176]{1,0:T(8,128)(2,1)S(1)}, bf16[128,2176]{1,0:T(8,128)(2,1)S(1)}, u32[]{:S(2)}, u32[]{:S(2)}) collective-permute-start(bf16[128,2176]{1,0:T(8,128)(2,1)S(1)} %collective-permute-done.5.refs_7_.refs_4_.refs_9_), channel_id=1, source_target_pairs={{0,32},{1,97},{32,64},{33,1},{64,96},{65,33},{96,0},{97,65},{2,34}... | collective-permute-start | bytes 1671176 | tf_op jit(solution)/shard_map/ppermute | solution.py:24
  41.5 18.2 %collective-permute-start.16 = (bf16[128,2048]{1,0:T(8,128)(2,1)S(1)}, bf16[128,2048]{1,0:T(8,128)(2,1)S(1)}, u32[]{:S(2)}, u32[]{:S(2)}) collective-permute-start(bf16[128,2048]{1,0:T(8,128)(2,1)S(1)} %collective-permute-done.14.refs_1_), channel_id=1, source_target_pairs={{0,28},{1,5},{4,0},{5,9},{8,4},{9,13},{12,8},{13,17},{16,12},{17,2... | collective-permute-start | bytes 1572872 | tf_op jit(solution)/shard_map/ppermute | solution.py:24
  47.7 12.8 %collective-permute-start.17 = (bf16[128,2048]{1,0:T(8,128)(2,1)S(1)}, bf16[128,2048]{1,0:T(8,128)(2,1)S(1)}, u32[]{:S(2)}, u32[]{:S(2)}) collective-permute-start(bf16[128,2048]{1,0:T(8,128)(2,1)S(1)} %collective-permute-done.15.refs_2_), channel_id=1, source_target_pairs={{0,4},{1,29},{4,8},{5,1},{8,12},{9,5},{12,16},{13,9},{16,20},{17,1... | collective-permute-start | bytes 1572872 | tf_op jit(solution)/shard_map/ppermute | solution.py:24
  63.8 3.1 %collective-permute-start.18 = (f32[640,512]{1,0:T(8,128)S(1)}, f32[640,512]{1,0:T(8,128)S(1)}, u32[]{:S(2)}, u32[]{:S(2)}) collective-permute-start(f32[640,512]{1,0:T(8,128)S(1)} %get-tuple-element.26), channel_id=1, source_target_pairs={{0,1},{1,0},{2,3},{3,2},{4,5},{5,4},{6,7},{7,6},{8,9},{9,8},{10,11... | collective-permute-start | bytes 3932168 | tf_op jit(solution)/shard_map/ppermute | solution.py:28
  67.5 19.6 %collective-permute-start.19 = (bf16[656,256]{1,0:T(8,128)(2,1)S(1)}, bf16[656,256]{1,0:T(8,128)(2,1)S(1)}, u32[]{:S(2)}, u32[]{:S(2)}) collective-permute-start(bf16[656,256]{1,0:T(8,128)(2,1)S(1)} %get-tuple-element.28), channel_id=1, source_target_pairs={{0,2},{2,0},{1,3},{3,1},{4,6},{6,4},{5,7},{7,5},{8,10},{10,8},{9,1... | collective-permute-start | bytes 1007624 | tf_op jit(solution)/shard_map/ppermute | solution.py:28
  69.0 14.4 %collective-permute-start.10 = (bf16[400,256]{1,0:T(8,128)(2,1)S(1)}, bf16[400,256]{1,0:T(8,128)(2,1)S(1)}, u32[]{:S(2)}, u32[]{:S(2)}) collective-permute-start(bf16[400,256]{1,0:T(8,128)(2,1)S(1)} %get-tuple-element.21), channel_id=1, source_target_pairs={{0,2},{2,0},{1,3},{3,1},{4,6},{6,4},{5,7},{7,5},{8,10},{10,8},{9,1... | collective-permute-start | bytes 614408 | tf_op jit(solution)/shard_map/ppermute | solution.py:28
  84.0 9.7 %collective-permute-start.11 = (bf16[144,256]{1,0:T(8,128)(2,1)S(1)}, bf16[144,256]{1,0:T(8,128)(2,1)S(1)}, u32[]{:S(2)}, u32[]{:S(2)}) collective-permute-start(bf16[144,256]{1,0:T(8,128)(2,1)S(1)} %get-tuple-element.23), channel_id=1, source_target_pairs={{0,28},{1,5},{4,0},{5,9},{8,4},{9,13},{12,8},{13,17},{16,12},{17,2... | collective-permute-start | bytes 221192 | tf_op jit(solution)/shard_map/ppermute | solution.py:24
  87.1 7.7 %collective-permute-start.12 = (bf16[144,256]{1,0:T(8,128)(2,1)S(1)}, bf16[144,256]{1,0:T(8,128)(2,1)S(1)}, u32[]{:S(2)}, u32[]{:S(2)}) collective-permute-start(bf16[144,256]{1,0:T(8,128)(2,1)S(1)} %get-tuple-element.24), channel_id=1, source_target_pairs={{0,4},{1,29},{4,8},{5,1},{8,12},{9,5},{12,16},{13,9},{16,20},{17,1... | collective-permute-start | bytes 221192 | tf_op jit(solution)/shard_map/ppermute | solution.py:24
  87.9 10.7 %collective-permute-start.20 = (bf16[144,256]{1,0:T(8,128)(2,1)S(1)}, bf16[144,256]{1,0:T(8,128)(2,1)S(1)}, u32[]{:S(2)}, u32[]{:S(2)}) collective-permute-start(bf16[144,256]{1,0:T(8,128)(2,1)S(1)} %get-tuple-element.29), channel_id=1, source_target_pairs={{0,24},{1,9},{4,28},{5,13},{8,0},{9,17},{12,4},{13,21},{16,8},{17,... | collective-permute-start | bytes 221192 | tf_op jit(solution)/shard_map/ppermute | solution.py:24
  89.6 9.1 %collective-permute-start.21 = (bf16[144,256]{1,0:T(8,128)(2,1)S(1)}, bf16[144,256]{1,0:T(8,128)(2,1)S(1)}, u32[]{:S(2)}, u32[]{:S(2)}) collective-permute-start(bf16[144,256]{1,0:T(8,128)(2,1)S(1)} %get-tuple-element.30), channel_id=1, source_target_pairs={{0,8},{1,25},{4,12},{5,29},{8,16},{9,1},{12,20},{13,5},{16,24},{17... | collective-permute-start | bytes 221192 | tf_op jit(solution)/shard_map/ppermute | solution.py:24
  90.9 7.7 %collective-permute-start.22 = (bf16[144,256]{1,0:T(8,128)(2,1)S(1)}, bf16[144,256]{1,0:T(8,128)(2,1)S(1)}, u32[]{:S(2)}, u32[]{:S(2)}) collective-permute-start(bf16[144,256]{1,0:T(8,128)(2,1)S(1)} %get-tuple-element.31), channel_id=1, source_target_pairs={{0,20},{1,13},{4,24},{5,17},{8,28},{9,21},{12,0},{13,25},{16,4},{1... | collective-permute-start | bytes 221192 | tf_op jit(solution)/shard_map/ppermute | solution.py:24
  93.7 10.8 %collective-permute-start.23 = (bf16[144,256]{1,0:T(8,128)(2,1)S(1)}, bf16[144,256]{1,0:T(8,128)(2,1)S(1)}, u32[]{:S(2)}, u32[]{:S(2)}) collective-permute-start(bf16[144,256]{1,0:T(8,128)(2,1)S(1)} %get-tuple-element.32), channel_id=1, source_target_pairs={{0,12},{1,21},{4,16},{5,25},{8,20},{9,29},{12,24},{13,1},{16,28},{... | collective-permute-start | bytes 221192 | tf_op jit(solution)/shard_map/ppermute | solution.py:24
  94.8 9.7 %collective-permute-start.24 = (bf16[144,256]{1,0:T(8,128)(2,1)S(1)}, bf16[144,256]{1,0:T(8,128)(2,1)S(1)}, u32[]{:S(2)}, u32[]{:S(2)}) collective-permute-start(bf16[144,256]{1,0:T(8,128)(2,1)S(1)} %get-tuple-element.33), channel_id=1, source_target_pairs={{0,16},{1,17},{4,20},{5,21},{8,24},{9,25},{12,28},{13,29},{16,0},{... | collective-permute-start | bytes 221192 | tf_op jit(solution)/shard_map/ppermute | solution.py:24
  (4 other events, 63.6 us)

commit v3 on v2

--- a/solution.py
+++ b/solution.py
@@ -12,7 +12,7 @@
 ROWS, PANEL = 128, 2048
 NX, NZ = 4, 8
 F32 = jnp.float32
-GROUPS = ((0, 1, -1), (2, -2, 3, -3, 4))
+GROUPS = ((0, 1, -1, 2, -2), (3, -3, 4))
 VMEM = pl.BlockSpec(memory_space=pltpu.VMEM)
 ANYWHERE = pl.BlockSpec(memory_space=pl.ANY)
 SMALL = pltpu.CompilerParams(vmem_limit_bytes=16 * 2**20)
@@ -37,19 +37,21 @@
 
 
 def gather(log_derivs, packed):
-    rows = {0: log_derivs}
-    rows[1], rows[-1] = shift(log_derivs, "z", 1), shift(log_derivs, "z", -1)
+    z_a1, z_b1 = shift(log_derivs, "z", 1), shift(log_derivs, "z", -1)
+    x_a0, x_b0 = shift(packed, "x", 1), shift(packed, "x", -1)
     partner = swap(packed, "ylo")
-    columns = {(0, 0): packed, (1, 0): partner}
-    for by in (1, -1):
-        columns[0, by] = shift(packed, "x", by)
-    rows[2], rows[-2] = shift(rows[1], "z", 1), shift(rows[-1], "z", -1)
-    for by in (1, -1):
-        columns[1, by] = shift(partner, "x", by)
-    rows[3], rows[-3] = shift(rows[2], "z", 1), shift(rows[-2], "z", -1)
-    columns[0, 2] = shift(columns[0, 1], "x", 1)
-    columns[1, 2] = shift(columns[1, 1], "x", 1)
-    rows[4] = shift(rows[3], "z", 1)
+
+    z_a2, z_b2 = shift(z_a1, "z", 1), shift(z_b1, "z", -1)
+    x_a1, x_far0 = shift(partner, "x", 1), shift(x_a0, "x", 1)
+    x_b1 = swap(x_b0, "ylo")
+
+    z_a3, z_b3 = shift(z_a2, "z", 1), shift(z_b2, "z", -1)
+    x_far1 = shift(after(x_a1, x_far0, x_b1), "x", 1)
+
+    z_a4 = shift(after(z_a3, z_b3), "z", 1)
+    rows = {0: log_derivs, 1: z_a1, -1: z_b1, 2: z_a2, -2: z_b2, 3: z_a3, -3: z_b3, 4: z_a4}
+    columns = {(0, 0): packed, (0, 1): x_a0, (0, -1): x_b0, (0, 2): x_far0}
+    columns |= {(1, 0): partner, (1, 1): x_a1, (1, -1): x_b1, (1, 2): x_far1}
     return rows, columns
 
 
@@ -80,7 +82,8 @@
 
     def kernel(*refs):
         cols = refs[n : n + len(columns)]
-        keep, send, held, sems = refs[n + len(columns) :]
+        keep, *sends = refs[n + len(columns) : 2 * n + len(columns) + 1]
+        held, sems = refs[2 * n + len(columns) + 1 :]
         copies = []
         for i, (ref, (ylo, back)) in enumerate(zip(cols, columns)):
             x = lax.rem(lax.axis_index("x") + NX - turn(back), NX)
@@ -95,18 +98,23 @@
         for copy in copies:
             copy.wait()
         block = jnp.concatenate([r[...] for r in refs[:n]], axis=0)
-        for pair in range(4):
-            out = keep if pair < 2 else send
-            out[:, 256 * (pair % 2) : 256 * (pair % 2) + 256] = scale * lax.dot_general(
+        for pair in (2, 3, 0, 1):
+            at = slice(256 * (pair % 2), 256 * (pair % 2) + 256)
+            value = scale * lax.dot_general(
                 block, held[pair], (((1,), (1,)), ((), ())), preferred_element_type=F32
             )
-
-    out = jax.ShapeDtypeStruct((m, 512), F32)
-    return pl.pallas_call(
-        kernel,
-        out_shape=(out, out),
+            if pair < 2:
+                keep[:, at] = value
+            else:
+                for i, send in enumerate(sends):
+                    send[:, at] = value[ROWS * i : ROWS * (i + 1)]
+
+    out = [jax.ShapeDtypeStruct((rows, 512), F32) for rows in [m] + [ROWS] * n]
+    return pl.pallas_call(
+        kernel,
+        out_shape=out,
         in_specs=[VMEM] * n + [ANYWHERE] * len(columns),
-        out_specs=(VMEM, VMEM),
+        out_specs=[VMEM] * (n + 1),
         scratch_shapes=[
             pltpu.VMEM((4, 256, PANEL), jnp.bfloat16),
             pltpu.SemaphoreType.DMA((len(columns),)),
@@ -160,26 +168,25 @@
 
 
 def encode(value, top):
-    power = value * (2.0**15 / top.astype(F32)[:1])
-    for _ in range(3):
-        power = power * power
+    size = jnp.log2(jnp.maximum(jnp.abs(value) * (1.0 / top.astype(F32)[:1]), 2.0**-26))
+    power = jnp.exp2(jnp.maximum(126.0 + 22.0 * size, 5.0 * size - 10.0))
     return jnp.where(value < 0, -power, power).astype(jnp.bfloat16)
 
 
 def decode(code, top):
     code = code.astype(F32)
-    root = jnp.abs(code)
-    for _ in range(3):
-        root = jnp.sqrt(root)
-    return jnp.where(code < 0, -root, root) * (top.astype(F32)[:1] * 2.0**-15)
+    size = jnp.log2(jnp.maximum(jnp.abs(code), 2.0**-126))
+    value = jnp.exp2(jnp.minimum((size - 126.0) * (1.0 / 22.0), (size + 10.0) * 0.2)) * top.astype(F32)[:1]
+    return jnp.where(code < 0, -value, jnp.where(code > 0, value, 0.0))
 
 
 def split_yhi(keep, received, backs):
     m = keep.shape[0]
     order = [backs.index(-back if -back in backs else back) for back in backs]
 
-    def kernel(a, b, own, code):
-        b = jnp.concatenate([b[ROWS * i : ROWS * (i + 1)] for i in order], axis=0)
+    def kernel(a, *refs):
+        own, code = refs[len(backs) :]
+        b = jnp.concatenate([refs[i][...] for i in order], axis=0)
         own[...] = a[:, :256] + b[:, :256]
         other = a[:, 256:] + b[:, 256:]
         top = peak(other)
@@ -192,11 +199,11 @@
             jax.ShapeDtypeStruct((m, 256), F32),
             jax.ShapeDtypeStruct((m + 16, 256), jnp.bfloat16),
         ),
-        in_specs=[VMEM] * 2,
+        in_specs=[VMEM] * (1 + len(backs)),
         out_specs=(VMEM, VMEM),
         compiler_params=SMALL,
         cost_estimate=pl.CostEstimate(flops=0, bytes_accessed=m * 6000, transcendentals=0),
-    )(keep, received)
+    )(keep, *received)
 
 
 def split_z(own, received, last_rows, backs):
@@ -273,12 +280,18 @@
     rows, columns = gather(log_derivs, pack(log_derivs, sample_vector))
     last_rows = term(scale_update, columns)
 
-    blocks = {}
+    blocks, sent, received = {}, [], []
     for backs in GROUPS:
-        keep, send = products(scale_gram, [rows[back] for back in backs], columns)
-        own, code = split_yhi(keep, swap(send, "core"), backs)
-        for back, block in zip(backs, split_z(own, swap(code, "yhi"), last_rows, backs)):
-            blocks[back] = shift(block, "z", -back) if back else block
+        keep, *sends = products(scale_gram, [rows[back] for back in backs], columns)
+        sends = [swap(send, "core") for send in sends]
+        own, code = split_yhi(keep, sends, backs)
+        code = swap(after(code, *received), "yhi")
+        received.append(code)
+        waited, sent = sent, []
+        for back, block in zip(backs, split_z(own, code, last_rows, backs)):
+            blocks[back] = shift(after(block, *waited), "z", -back) if back else block
+            if back and len(sent) < 1:
+                sent.append(blocks[back])
     return place(blocks.values(), list(blocks), last_rows)
 
 

time: 108 us -> 99.8 us (0.924)
  the two profiles are of different devices: /device:TPU:16 before, /device:TPU:1 now
where the time goes in v3:
time: 99.8 us; the launch traced here: 99.6 us
  starting transfers between devices  49 us (49%)
  waiting for transfers between devices  36.6 us (37%)
  Pallas kernels  10.5 us (11%)
  local copies, waits for them, and re-layouts  2.73 us (3%)
    ppermute x19, starting transfers between devices, shift(): return lax.ppermute(value, (axis, 'core'), pairs)  32.1 us
    ppermute x19, waiting for transfers between devices, shift(): return lax.ppermute(value, (axis, 'core'), pairs)  26.2 us
    ppermute x12, starting transfers between devices, swap(): return lax.ppermute(value, axis, [(0, 1), (1, 0)])  16.9 us
    ppermute x12, waiting for transfers between devices, swap(): return lax.ppermute(value, axis, [(0, 1), (1, 0)])  10.4 us
    pallas_call x2, Pallas kernels, products(): pl.pallas_call(kernel, out_shape=out, in_specs=[VMEM] * n + [ANYWHERE] *...  5.56 us
    unnamed x6, local copies, waits for them, and re-layouts  2.73 us
  transfers between devices with their start and end apart: 31, of which 20 were waited for; matrix products, arithmetic and copies ran while one was open for 0% of the time, Pallas kernels for 9%

profile of v3, /device:TPU:1, one launch (start us, length us, event | category | flops | bytes accessed | tf_op | source)
XLA Modules:
  0.0 99.6 jit_solution(11363722635922416272)
XLA Ops:
  2.4 3.4 %collective-permute-start.4 = (bf16[128,2176]{1,0:T(8,128)(2,1)S(1)}, bf16[128,2176]{1,0:T(8,128)(2,1)S(1)}, u32[]{:S(2)}, u32[]{:S(2)}) collective-permute-start(bf16[128,2176]{1,0:T(8,128)(2,1)S(1)} %shard_map.41.refs_5_.refs_0_.refs_3_), channel_id=1, source_target_pairs={{0,32},{1,97},{32,64},{33,1},{64,96},{65,33},{96,0},{97,65},{2,34}... | collective-permute-start | bytes 1671176 | tf_op jit(solution)/shard_map/ppermute | solution.py:24
  7.1 5.6 %collective-permute-start = (bf16[128,2048]{1,0:T(8,128)(2,1)S(1)}, bf16[128,2048]{1,0:T(8,128)(2,1)S(1)}, u32[]{:S(2)}, u32[]{:S(2)}) collective-permute-start(bf16[128,2048]{1,0:T(8,128)(2,1)S(1)} %copy-done), channel_id=1, source_target_pairs={{0,4},{1,29},{4,8},{5,1},{8,12},{9,5},{12,16},{13,9},{16,20},{17,1... | collective-permute-start | bytes 1572872 | tf_op jit(solution)/shard_map/ppermute | solution.py:24
  12.7 2.1 %collective-permute-done.4.refs_6_.refs_1_.refs_4_ = bf16[128,2176]{1,0:T(8,128)(2,1)S(1)} collective-permute-done((bf16[128,2176]{1,0:T(8,128)(2,1)S(1)}, bf16[128,2176]{1,0:T(8,128)(2,1)S(1)}, u32[]{:S(2)}, u32[]{:S(2)}) %collective-permute-start.4) | collective-permute-done | bytes 557088 | tf_op jit(solution)/shard_map/ppermute | solution.py:24
  14.8 3.4 %collective-permute-start.6 = (bf16[128,2176]{1,0:T(8,128)(2,1)S(1)}, bf16[128,2176]{1,0:T(8,128)(2,1)S(1)}, u32[]{:S(2)}, u32[]{:S(2)}) collective-permute-start(bf16[128,2176]{1,0:T(8,128)(2,1)S(1)} %collective-permute-done.4.refs_6_.refs_1_.refs_4_), channel_id=1, source_target_pairs={{0,32},{1,97},{32,64},{33,1},{64,96},{65,33},{96,0},{97,65},{2,34}... | collective-permute-start | bytes 1671176 | tf_op jit(solution)/shard_map/ppermute | solution.py:24
  20.1 2.0 %collective-permute-done.5.refs_7_.refs_2_.refs_5_ = bf16[128,2176]{1,0:T(8,128)(2,1)S(1)} collective-permute-done((bf16[128,2176]{1,0:T(8,128)(2,1)S(1)}, bf16[128,2176]{1,0:T(8,128)(2,1)S(1)}, u32[]{:S(2)}, u32[]{:S(2)}) %collective-permute-start.5) | collective-permute-done | bytes 557088 | tf_op jit(solution)/shard_map/ppermute | solution.py:24
  22.2 5.0 %collective-permute-start.2 = (bf16[128,2048]{1,0:T(8,128)(2,1)S(1)}, bf16[128,2048]{1,0:T(8,128)(2,1)S(1)}, u32[]{:S(2)}, u32[]{:S(2)}) collective-permute-start(bf16[128,2048]{1,0:T(8,128)(2,1)S(1)} %collective-permute-done.refs_1_), channel_id=1, source_target_pairs={{0,4},{1,29},{4,8},{5,1},{8,12},{9,5},{12,16},{13,9},{16,20},{17,1... | collective-permute-start | bytes 1572872 | tf_op jit(solution)/shard_map/ppermute | solution.py:24
  27.2 3.5 %collective-permute-done.8.refs_10_.refs_5_.refs_8_ = bf16[128,2176]{1,0:T(8,128)(2,1)S(1)} collective-permute-done((bf16[128,2176]{1,0:T(8,128)(2,1)S(1)}, bf16[128,2176]{1,0:T(8,128)(2,1)S(1)}, u32[]{:S(2)}, u32[]{:S(2)}) %collective-permute-start.8) | collective-permute-done | bytes 557088 | tf_op jit(solution)/shard_map/ppermute | solution.py:24
  30.7 5.6 %collective-permute-done.9.refs_11_.refs_6_.refs_9_ = bf16[128,2176]{1,0:T(8,128)(2,1)S(1)} collective-permute-done((bf16[128,2176]{1,0:T(8,128)(2,1)S(1)}, bf16[128,2176]{1,0:T(8,128)(2,1)S(1)}, u32[]{:S(2)}, u32[]{:S(2)}) %collective-permute-start.9) | collective-permute-done | bytes 557088 | tf_op jit(solution)/shard_map/ppermute | solution.py:28
  36.3 3.6 %collective-permute-start.21 = (bf16[128,2048]{1,0:T(8,128)(2,1)S(1)}, bf16[128,2048]{1,0:T(8,128)(2,1)S(1)}, u32[]{:S(2)}, u32[]{:S(2)}) collective-permute-start(bf16[128,2048]{1,0:T(8,128)(2,1)S(1)} %collective-permute-done.2.refs_3_), channel_id=1, source_target_pairs={{0,4},{1,29},{4,8},{5,1},{8,12},{9,5},{12,16},{13,9},{16,20},{17,1... | collective-permute-start | bytes 1572872 | tf_op jit(solution)/shard_map/ppermute | solution.py:24
  39.9 2.4 %collective-permute-done.3.refs_4_ = bf16[128,2048]{1,0:T(8,128)(2,1)S(1)} collective-permute-done((bf16[128,2048]{1,0:T(8,128)(2,1)S(1)}, bf16[128,2048]{1,0:T(8,128)(2,1)S(1)}, u32[]{:S(2)}, u32[]{:S(2)}) %collective-permute-start.3) | collective-permute-done | bytes 524320 | tf_op jit(solution)/shard_map/ppermute | solution.py:24
  42.3 2.7 %collective-permute-done.10.refs_12_.refs_7_.refs_10_ = bf16[128,2176]{1,0:T(8,128)(2,1)S(1)} collective-permute-done((bf16[128,2176]{1,0:T(8,128)(2,1)S(1)}, bf16[128,2176]{1,0:T(8,128)(2,1)S(1)}, u32[]{:S(2)}, u32[]{:S(2)}) %collective-permute-start.10) | collective-permute-done | bytes 557088 | tf_op jit(solution)/shard_map/ppermute | solution.py:24
  46.0 3.3 %shard_map.42 = (f32[640,512]{1,0:T(8,128)S(1)}, f32[128,512]{1,0:T(8,128)S(1)}, f32[128,512]{1,0:T(8,128)S(1)}, f32[128,512]{1,0:T(8,128)S(1)}, f32[128,512]{1,0:T(8,128)S(1)}, /*index=5*/f32[128,512]{1,0:T(8,128)S(1)}) custom-call(bf16[128,2048]{1,0:T(8,128)(2,1)S(1)} %copy-done.1, bf16[128,2048]{1,0:T(8,128)(2,1)S(1)} %collective-permute-done.refs_1_, ...), custom_call_target="tpu_custom_call" | custom-call | flops 2684354560 | bytes 9437184 | tf_op jit(solution)/shard_map/pallas_call | solution.py:113
  49.3 4.4 %collective-permute-start.11 = (f32[128,512]{1,0:T(8,128)S(1)}, f32[128,512]{1,0:T(8,128)S(1)}, u32[]{:S(2)}, u32[]{:S(2)}) collective-permute-start(f32[128,512]{1,0:T(8,128)S(1)} %get-tuple-element.32), channel_id=1, source_target_pairs={{0,1},{1,0},{2,3},{3,2},{4,5},{5,4},{6,7},{7,6},{8,9},{9,8},{10,11... | collective-permute-start | bytes 786440 | tf_op jit(solution)/shard_map/ppermute | solution.py:28
  53.7 2.9 %collective-permute-done.22.refs_1_ = bf16[128,2048]{1,0:T(8,128)(2,1)S(1)} collective-permute-done((bf16[128,2048]{1,0:T(8,128)(2,1)S(1)}, bf16[128,2048]{1,0:T(8,128)(2,1)S(1)}, u32[]{:S(2)}, u32[]{:S(2)}) %collective-permute-start.22) | collective-permute-done | bytes 524320 | tf_op jit(solution)/shard_map/ppermute | solution.py:24
  60.9 2.8 %collective-permute-start.16 = (bf16[656,256]{1,0:T(8,128)(2,1)S(1)}, bf16[656,256]{1,0:T(8,128)(2,1)S(1)}, u32[]{:S(2)}, u32[]{:S(2)}) collective-permute-start(bf16[656,256]{1,0:T(8,128)(2,1)S(1)} %get-tuple-element.38), channel_id=1, source_target_pairs={{0,2},{2,0},{1,3},{3,1},{4,6},{6,4},{5,7},{7,5},{8,10},{10,8},{9,1... | collective-permute-start | bytes 1007624 | tf_op jit(solution)/shard_map/ppermute | solution.py:28
  64.9 2.2 %shard_map.46 = (f32[384,512]{1,0:T(8,128)S(1)}, f32[128,512]{1,0:T(8,128)S(1)}, f32[128,512]{1,0:T(8,128)S(1)}, f32[128,512]{1,0:T(8,128)S(1)}) custom-call(bf16[128,2048]{1,0:T(8,128)(2,1)S(1)} %collective-permute-done.21.refs_0_, bf16[128,2048]{1,0:T(8,128)(2,1)S(1)} %collective-permute-done.22.refs_1_, ...), custom_call_target="tpu_custom_call" | custom-call | flops 1610612736 | bytes 7340032 | tf_op jit(solution)/shard_map/pallas_call | solution.py:113
  67.2 3.4 %collective-permute-start.24 = (f32[128,512]{1,0:T(8,128)S(1)}, f32[128,512]{1,0:T(8,128)S(1)}, u32[]{:S(2)}, u32[]{:S(2)}) collective-permute-start(f32[128,512]{1,0:T(8,128)S(1)} %get-tuple-element.46), channel_id=1, source_target_pairs={{0,1},{1,0},{2,3},{3,2},{4,5},{5,4},{6,7},{7,6},{8,9},{9,8},{10,11... | collective-permute-start | bytes 786440 | tf_op jit(solution)/shard_map/ppermute | solution.py:28
  73.0 2.8 %collective-permute-start.27 = (bf16[400,256]{1,0:T(8,128)(2,1)S(1)}, bf16[400,256]{1,0:T(8,128)(2,1)S(1)}, u32[]{:S(2)}, u32[]{:S(2)}) collective-permute-start(bf16[400,256]{1,0:T(8,128)(2,1)S(1)} %get-tuple-element.51), channel_id=1, source_target_pairs={{0,2},{2,0},{1,3},{3,1},{4,6},{6,4},{5,7},{7,5},{8,10},{10,8},{9,1... | collective-permute-start | bytes 614408 | tf_op jit(solution)/shard_map/ppermute | solution.py:28
  77.1 2.7 %collective-permute-start.18 = (bf16[144,256]{1,0:T(8,128)(2,1)S(1)}, bf16[144,256]{1,0:T(8,128)(2,1)S(1)}, u32[]{:S(2)}, u32[]{:S(2)}) collective-permute-start(bf16[144,256]{1,0:T(8,128)(2,1)S(1)} %get-tuple-element.41), channel_id=1, source_target_pairs={{0,4},{1,29},{4,8},{5,1},{8,12},{9,5},{12,16},{13,9},{16,20},{17,1... | collective-permute-start | bytes 221192 | tf_op jit(solution)/shard_map/ppermute | solution.py:24
  79.8 3.6 %collective-permute-start.20 = (bf16[144,256]{1,0:T(8,128)(2,1)S(1)}, bf16[144,256]{1,0:T(8,128)(2,1)S(1)}, u32[]{:S(2)}, u32[]{:S(2)}) collective-permute-start(bf16[144,256]{1,0:T(8,128)(2,1)S(1)} %get-tuple-element.43), channel_id=1, source_target_pairs={{0,8},{1,25},{4,12},{5,29},{8,16},{9,1},{12,20},{13,5},{16,24},{17... | collective-permute-start | bytes 221192 | tf_op jit(solution)/shard_map/ppermute | solution.py:24
  84.0 4.5 %collective-permute-start.29 = (bf16[144,256]{1,0:T(8,128)(2,1)S(1)}, bf16[144,256]{1,0:T(8,128)(2,1)S(1)}, u32[]{:S(2)}, u32[]{:S(2)}) collective-permute-start(bf16[144,256]{1,0:T(8,128)(2,1)S(1)} %get-tuple-element.55), channel_id=1, source_target_pairs={{0,12},{1,21},{4,16},{5,25},{8,20},{9,29},{12,24},{13,1},{16,28},{... | collective-permute-start | bytes 221192 | tf_op jit(solution)/shard_map/ppermute | solution.py:24
  88.7 2.1 %collective-permute-done.28.refs_5_ = bf16[144,256]{1,0:T(8,128)(2,1)S(1)} collective-permute-done((bf16[144,256]{1,0:T(8,128)(2,1)S(1)}, bf16[144,256]{1,0:T(8,128)(2,1)S(1)}, u32[]{:S(2)}, u32[]{:S(2)}) %collective-permute-start.28) | collective-permute-done | bytes 73760 | tf_op jit(solution)/shard_map/ppermute | solution.py:24
  90.8 4.2 %collective-permute-done.29.refs_6_ = bf16[144,256]{1,0:T(8,128)(2,1)S(1)} collective-permute-done((bf16[144,256]{1,0:T(8,128)(2,1)S(1)}, bf16[144,256]{1,0:T(8,128)(2,1)S(1)}, u32[]{:S(2)}, u32[]{:S(2)}) %collective-permute-start.29) | collective-permute-done | bytes 73760 | tf_op jit(solution)/shard_map/ppermute | solution.py:24
  95.0 2.9 %collective-permute-done.30.refs_7_ = bf16[144,256]{1,0:T(8,128)(2,1)S(1)} collective-permute-done((bf16[144,256]{1,0:T(8,128)(2,1)S(1)}, bf16[144,256]{1,0:T(8,128)(2,1)S(1)}, u32[]{:S(2)}, u32[]{:S(2)}) %collective-permute-start.30) | collective-permute-done | bytes 73760 | tf_op jit(solution)/shard_map/ppermute | solution.py:24
  (53 shorter events, 18.0 us)
Async XLA Ops:
  2.4 12.4 %collective-permute-start.4 = (bf16[128,2176]{1,0:T(8,128)(2,1)S(1)}, bf16[128,2176]{1,0:T(8,128)(2,1)S(1)}, u32[]{:S(2)}, u32[]{:S(2)}) collective-permute-start(bf16[128,2176]{1,0:T(8,128)(2,1)S(1)} %shard_map.41.refs_5_.refs_0_.refs_3_), channel_id=1, source_target_pairs={{0,32},{1,97},{32,64},{33,1},{64,96},{65,33},{96,0},{97,65},{2,34}... | collective-permute-start | bytes 1671176 | tf_op jit(solution)/shard_map/ppermute | solution.py:24
  5.8 14.2 %collective-permute-start.7 = (bf16[128,2176]{1,0:T(8,128)(2,1)S(1)}, bf16[128,2176]{1,0:T(8,128)(2,1)S(1)}, u32[]{:S(2)}, u32[]{:S(2)}) collective-permute-start(bf16[128,2176]{1,0:T(8,128)(2,1)S(1)} %shard_map.41.refs_5_.refs_0_.refs_3_), channel_id=1, source_target_pairs={{0,128},{128,0},{1,129},{129,1},{2,130},{130,2},{3,131},{131,3},{4... | collective-permute-start | bytes 1671176 | tf_op jit(solution)/shard_map/ppermute | solution.py:28
  7.1 15.0 %collective-permute-start.5 = (bf16[128,2176]{1,0:T(8,128)(2,1)S(1)}, bf16[128,2176]{1,0:T(8,128)(2,1)S(1)}, u32[]{:S(2)}, u32[]{:S(2)}) collective-permute-start(bf16[128,2176]{1,0:T(8,128)(2,1)S(1)} %shard_map.41.refs_5_.refs_0_.refs_3_), channel_id=1, source_target_pairs={{0,96},{1,33},{32,0},{33,65},{64,32},{65,97},{96,64},{97,1},{2,98}... | collective-permute-start | bytes 1671176 | tf_op jit(solution)/shard_map/ppermute | solution.py:24
  7.1 15.1 %collective-permute-start = (bf16[128,2048]{1,0:T(8,128)(2,1)S(1)}, bf16[128,2048]{1,0:T(8,128)(2,1)S(1)}, u32[]{:S(2)}, u32[]{:S(2)}) collective-permute-start(bf16[128,2048]{1,0:T(8,128)(2,1)S(1)} %copy-done), channel_id=1, source_target_pairs={{0,4},{1,29},{4,8},{5,1},{8,12},{9,5},{12,16},{13,9},{16,20},{17,1... | collective-permute-start | bytes 1572872 | tf_op jit(solution)/shard_map/ppermute | solution.py:24
  12.7 14.5 %collective-permute-start.1 = (bf16[128,2048]{1,0:T(8,128)(2,1)S(1)}, bf16[128,2048]{1,0:T(8,128)(2,1)S(1)}, u32[]{:S(2)}, u32[]{:S(2)}) collective-permute-start(bf16[128,2048]{1,0:T(8,128)(2,1)S(1)} %copy-done), channel_id=1, source_target_pairs={{0,28},{1,5},{4,0},{5,9},{8,4},{9,13},{12,8},{13,17},{16,12},{17,2... | collective-permute-start | bytes 1572872 | tf_op jit(solution)/shard_map/ppermute | solution.py:24
  14.8 12.4 %collective-permute-start.6 = (bf16[128,2176]{1,0:T(8,128)(2,1)S(1)}, bf16[128,2176]{1,0:T(8,128)(2,1)S(1)}, u32[]{:S(2)}, u32[]{:S(2)}) collective-permute-start(bf16[128,2176]{1,0:T(8,128)(2,1)S(1)} %collective-permute-done.4.refs_6_.refs_1_.refs_4_), channel_id=1, source_target_pairs={{0,32},{1,97},{32,64},{33,1},{64,96},{65,33},{96,0},{97,65},{2,34}... | collective-permute-start | bytes 1671176 | tf_op jit(solution)/shard_map/ppermute | solution.py:24
  20.0 10.7 %collective-permute-start.8 = (bf16[128,2176]{1,0:T(8,128)(2,1)S(1)}, bf16[128,2176]{1,0:T(8,128)(2,1)S(1)}, u32[]{:S(2)}, u32[]{:S(2)}) collective-permute-start(bf16[128,2176]{1,0:T(8,128)(2,1)S(1)} %collective-permute-done.7.refs_9_.refs_4_.refs_7_), channel_id=1, source_target_pairs={{0,32},{1,97},{32,64},{33,1},{64,96},{65,33},{96,0},{97,65},{2,34}... | collective-permute-start | bytes 1671176 | tf_op jit(solution)/shard_map/ppermute | solution.py:24
  22.1 14.2 %collective-permute-start.9 = (bf16[128,2176]{1,0:T(8,128)(2,1)S(1)}, bf16[128,2176]{1,0:T(8,128)(2,1)S(1)}, u32[]{:S(2)}, u32[]{:S(2)}) collective-permute-start(bf16[128,2176]{1,0:T(8,128)(2,1)S(1)} %collective-permute-done.5.refs_7_.refs_2_.refs_5_), channel_id=1, source_target_pairs={{0,128},{128,0},{1,129},{129,1},{2,130},{130,2},{3,131},{131,3},{4... | collective-permute-start | bytes 1671176 | tf_op jit(solution)/shard_map/ppermute | solution.py:28
  22.2 14.1 %collective-permute-start.2 = (bf16[128,2048]{1,0:T(8,128)(2,1)S(1)}, bf16[128,2048]{1,0:T(8,128)(2,1)S(1)}, u32[]{:S(2)}, u32[]{:S(2)}) collective-permute-start(bf16[128,2048]{1,0:T(8,128)(2,1)S(1)} %collective-permute-done.refs_1_), channel_id=1, source_target_pairs={{0,4},{1,29},{4,8},{5,1},{8,12},{9,5},{12,16},{13,9},{16,20},{17,1... | collective-permute-start | bytes 1572872 | tf_op jit(solution)/shard_map/ppermute | solution.py:24
  27.2 15.1 %collective-permute-start.3 = (bf16[128,2048]{1,0:T(8,128)(2,1)S(1)}, bf16[128,2048]{1,0:T(8,128)(2,1)S(1)}, u32[]{:S(2)}, u32[]{:S(2)}) collective-permute-start(bf16[128,2048]{1,0:T(8,128)(2,1)S(1)} %collective-permute-done.1.refs_2_), channel_id=1, source_target_pairs={{0,28},{1,5},{4,0},{5,9},{8,4},{9,13},{12,8},{13,17},{16,12},{17,2... | collective-permute-start | bytes 1572872 | tf_op jit(solution)/shard_map/ppermute | solution.py:24
  36.3 8.7 %collective-permute-start.10 = (bf16[128,2176]{1,0:T(8,128)(2,1)S(1)}, bf16[128,2176]{1,0:T(8,128)(2,1)S(1)}, u32[]{:S(2)}, u32[]{:S(2)}) collective-permute-start(bf16[128,2176]{1,0:T(8,128)(2,1)S(1)} %collective-permute-done.8.refs_10_.refs_5_.refs_8_), channel_id=1, source_target_pairs={{0,32},{1,97},{32,64},{33,1},{64,96},{65,33},{96,0},{97,65},{2,34}... | collective-permute-start | bytes 1671176 | tf_op jit(solution)/shard_map/ppermute | solution.py:24
  36.3 17.4 %collective-permute-start.21 = (bf16[128,2048]{1,0:T(8,128)(2,1)S(1)}, bf16[128,2048]{1,0:T(8,128)(2,1)S(1)}, u32[]{:S(2)}, u32[]{:S(2)}) collective-permute-start(bf16[128,2048]{1,0:T(8,128)(2,1)S(1)} %collective-permute-done.2.refs_3_), channel_id=1, source_target_pairs={{0,4},{1,29},{4,8},{5,1},{8,12},{9,5},{12,16},{13,9},{16,20},{17,1... | collective-permute-start | bytes 1572872 | tf_op jit(solution)/shard_map/ppermute | solution.py:24
  42.3 14.3 %collective-permute-start.22 = (bf16[128,2048]{1,0:T(8,128)(2,1)S(1)}, bf16[128,2048]{1,0:T(8,128)(2,1)S(1)}, u32[]{:S(2)}, u32[]{:S(2)}) collective-permute-start(bf16[128,2048]{1,0:T(8,128)(2,1)S(1)} %collective-permute-done.3.refs_4_), channel_id=1, source_target_pairs={{0,28},{1,5},{4,0},{5,9},{8,4},{9,13},{12,8},{13,17},{16,12},{17,2... | collective-permute-start | bytes 1572872 | tf_op jit(solution)/shard_map/ppermute | solution.py:24
  49.3 9.0 %collective-permute-start.11 = (f32[128,512]{1,0:T(8,128)S(1)}, f32[128,512]{1,0:T(8,128)S(1)}, u32[]{:S(2)}, u32[]{:S(2)}) collective-permute-start(f32[128,512]{1,0:T(8,128)S(1)} %get-tuple-element.32), channel_id=1, source_target_pairs={{0,1},{1,0},{2,3},{3,2},{4,5},{5,4},{6,7},{7,6},{8,9},{9,8},{10,11... | collective-permute-start | bytes 786440 | tf_op jit(solution)/shard_map/ppermute | solution.py:28
  56.6 8.3 %collective-permute-start.23 = (bf16[128,2048]{1,0:T(8,128)(2,1)S(1)}, bf16[128,2048]{1,0:T(8,128)(2,1)S(1)}, u32[]{:S(2)}, u32[]{:S(2)}) collective-permute-start(bf16[128,2048]{1,0:T(8,128)(2,1)S(1)} %collective-permute-done.21.refs_0_), channel_id=1, source_target_pairs={{0,4},{1,29},{4,8},{5,1},{8,12},{9,5},{12,16},{13,9},{16,20},{17,1... | collective-permute-start | bytes 1572872 | tf_op jit(solution)/shard_map/ppermute | solution.py:24
  60.9 12.1 %collective-permute-start.16 = (bf16[656,256]{1,0:T(8,128)(2,1)S(1)}, bf16[656,256]{1,0:T(8,128)(2,1)S(1)}, u32[]{:S(2)}, u32[]{:S(2)}) collective-permute-start(bf16[656,256]{1,0:T(8,128)(2,1)S(1)} %get-tuple-element.38), channel_id=1, source_target_pairs={{0,2},{2,0},{1,3},{3,1},{4,6},{6,4},{5,7},{7,5},{8,10},{10,8},{9,1... | collective-permute-start | bytes 1007624 | tf_op jit(solution)/shard_map/ppermute | solution.py:28
  73.0 10.3 %collective-permute-start.27 = (bf16[400,256]{1,0:T(8,128)(2,1)S(1)}, bf16[400,256]{1,0:T(8,128)(2,1)S(1)}, u32[]{:S(2)}, u32[]{:S(2)}) collective-permute-start(bf16[400,256]{1,0:T(8,128)(2,1)S(1)} %get-tuple-element.51), channel_id=1, source_target_pairs={{0,2},{2,0},{1,3},{3,1},{4,6},{6,4},{5,7},{7,5},{8,10},{10,8},{9,1... | collective-permute-start | bytes 614408 | tf_op jit(solution)/shard_map/ppermute | solution.py:28
  77.0 6.9 %collective-permute-start.17 = (bf16[144,256]{1,0:T(8,128)(2,1)S(1)}, bf16[144,256]{1,0:T(8,128)(2,1)S(1)}, u32[]{:S(2)}, u32[]{:S(2)}) collective-permute-start(bf16[144,256]{1,0:T(8,128)(2,1)S(1)} %get-tuple-element.40), channel_id=1, source_target_pairs={{0,28},{1,5},{4,0},{5,9},{8,4},{9,13},{12,8},{13,17},{16,12},{17,2... | collective-permute-start | bytes 221192 | tf_op jit(solution)/shard_map/ppermute | solution.py:24
  77.1 11.3 %collective-permute-start.18 = (bf16[144,256]{1,0:T(8,128)(2,1)S(1)}, bf16[144,256]{1,0:T(8,128)(2,1)S(1)}, u32[]{:S(2)}, u32[]{:S(2)}) collective-permute-start(bf16[144,256]{1,0:T(8,128)(2,1)S(1)} %get-tuple-element.41), channel_id=1, source_target_pairs={{0,4},{1,29},{4,8},{5,1},{8,12},{9,5},{12,16},{13,9},{16,20},{17,1... | collective-permute-start | bytes 221192 | tf_op jit(solution)/shard_map/ppermute | solution.py:24
  79.8 8.9 %collective-permute-start.19 = (bf16[144,256]{1,0:T(8,128)(2,1)S(1)}, bf16[144,256]{1,0:T(8,128)(2,1)S(1)}, u32[]{:S(2)}, u32[]{:S(2)}) collective-permute-start(bf16[144,256]{1,0:T(8,128)(2,1)S(1)} %get-tuple-element.42), channel_id=1, source_target_pairs={{0,24},{1,9},{4,28},{5,13},{8,0},{9,17},{12,4},{13,21},{16,8},{17,... | collective-permute-start | bytes 221192 | tf_op jit(solution)/shard_map/ppermute | solution.py:24
  79.8 8.9 %collective-permute-start.20 = (bf16[144,256]{1,0:T(8,128)(2,1)S(1)}, bf16[144,256]{1,0:T(8,128)(2,1)S(1)}, u32[]{:S(2)}, u32[]{:S(2)}) collective-permute-start(bf16[144,256]{1,0:T(8,128)(2,1)S(1)} %get-tuple-element.43), channel_id=1, source_target_pairs={{0,8},{1,25},{4,12},{5,29},{8,16},{9,1},{12,20},{13,5},{16,24},{17... | collective-permute-start | bytes 221192 | tf_op jit(solution)/shard_map/ppermute | solution.py:24
  83.9 6.9 %collective-permute-start.28 = (bf16[144,256]{1,0:T(8,128)(2,1)S(1)}, bf16[144,256]{1,0:T(8,128)(2,1)S(1)}, u32[]{:S(2)}, u32[]{:S(2)}) collective-permute-start(bf16[144,256]{1,0:T(8,128)(2,1)S(1)} %get-tuple-element.53), channel_id=1, source_target_pairs={{0,20},{1,13},{4,24},{5,17},{8,28},{9,21},{12,0},{13,25},{16,4},{1... | collective-permute-start | bytes 221192 | tf_op jit(solution)/shard_map/ppermute | solution.py:24
  84.0 11.0 %collective-permute-start.29 = (bf16[144,256]{1,0:T(8,128)(2,1)S(1)}, bf16[144,256]{1,0:T(8,128)(2,1)S(1)}, u32[]{:S(2)}, u32[]{:S(2)}) collective-permute-start(bf16[144,256]{1,0:T(8,128)(2,1)S(1)} %get-tuple-element.55), channel_id=1, source_target_pairs={{0,12},{1,21},{4,16},{5,25},{8,20},{9,29},{12,24},{13,1},{16,28},{... | collective-permute-start | bytes 221192 | tf_op jit(solution)/shard_map/ppermute | solution.py:24
  88.4 9.4 %collective-permute-start.30 = (bf16[144,256]{1,0:T(8,128)(2,1)S(1)}, bf16[144,256]{1,0:T(8,128)(2,1)S(1)}, u32[]{:S(2)}, u32[]{:S(2)}) collective-permute-start(bf16[144,256]{1,0:T(8,128)(2,1)S(1)} %get-tuple-element.57), channel_id=1, source_target_pairs={{0,16},{1,17},{4,20},{5,21},{8,24},{9,25},{12,28},{13,29},{16,0},{... | collective-permute-start | bytes 221192 | tf_op jit(solution)/shard_map/ppermute | solution.py:24
  (10 other events, 18.2 us)

commit v4 on v3

--- a/solution.py
+++ b/solution.py
@@ -13,9 +13,15 @@
 NX, NZ = 4, 8
 F32 = jnp.float32
 GROUPS = ((0, 1, -1, 2, -2), (3, -3, 4))
+PARTS = ((160,) * 4, (128,) * 3)
+COSTS = ((0, 0, 10), (2.2, 0.5, 0.5))
 VMEM = pl.BlockSpec(memory_space=pltpu.VMEM)
 ANYWHERE = pl.BlockSpec(memory_space=pl.ANY)
 SMALL = pltpu.CompilerParams(vmem_limit_bytes=16 * 2**20)
+
+
+def takes(work):
+    return pl.CostEstimate(flops=int(1e9 * work), bytes_accessed=0, transcendentals=0)
 
 
 def shift(value, axis, by):
@@ -73,17 +79,17 @@
         in_specs=[VMEM] * 2,
         out_specs=VMEM,
         compiler_params=SMALL,
-        cost_estimate=pl.CostEstimate(flops=0, bytes_accessed=2**20, transcendentals=0),
+        cost_estimate=takes(0),
     )(log_derivs, sample_vector[None])
 
 
-def products(scale, rows, columns):
+def products(scale, rows, columns, parts, cost):
     m, n = ROWS * len(rows), len(rows)
 
     def kernel(*refs):
         cols = refs[n : n + len(columns)]
-        keep, *sends = refs[n + len(columns) : 2 * n + len(columns) + 1]
-        held, sems = refs[2 * n + len(columns) + 1 :]
+        keep, *sends = refs[n + len(columns) : -2]
+        held, sems = refs[-2:]
         copies = []
         for i, (ref, (ylo, back)) in enumerate(zip(cols, columns)):
             x = lax.rem(lax.axis_index("x") + NX - turn(back), NX)
@@ -106,23 +112,23 @@
             if pair < 2:
                 keep[:, at] = value
             else:
-                for i, send in enumerate(sends):
-                    send[:, at] = value[ROWS * i : ROWS * (i + 1)]
-
-    out = [jax.ShapeDtypeStruct((rows, 512), F32) for rows in [m] + [ROWS] * n]
+                first = 0
+                for send in sends:
+                    send[:, at] = value[first : first + send.shape[0]]
+                    first += send.shape[0]
+
+    out = [jax.ShapeDtypeStruct((count, 512), F32) for count in (m, *parts)]
     return pl.pallas_call(
         kernel,
         out_shape=out,
         in_specs=[VMEM] * n + [ANYWHERE] * len(columns),
-        out_specs=[VMEM] * (n + 1),
+        out_specs=[VMEM] * len(out),
         scratch_shapes=[
             pltpu.VMEM((4, 256, PANEL), jnp.bfloat16),
             pltpu.SemaphoreType.DMA((len(columns),)),
         ],
         compiler_params=pltpu.CompilerParams(vmem_limit_bytes=24 * 2**20),
-        cost_estimate=pl.CostEstimate(
-            flops=2 * m * 1024 * PANEL, bytes_accessed=2**22 + m * 8192, transcendentals=0
-        ),
+        cost_estimate=takes(cost),
     )(*rows, *columns.values())
 
 
@@ -180,13 +186,14 @@
     return jnp.where(code < 0, -value, jnp.where(code > 0, value, 0.0))
 
 
-def split_yhi(keep, received, backs):
+def split_yhi(keep, received, backs, cost):
     m = keep.shape[0]
     order = [backs.index(-back if -back in backs else back) for back in backs]
 
     def kernel(a, *refs):
-        own, code = refs[len(backs) :]
-        b = jnp.concatenate([refs[i][...] for i in order], axis=0)
+        own, code = refs[len(received) :]
+        b = jnp.concatenate([ref[...] for ref in refs[: len(received)]], axis=0)
+        b = jnp.concatenate([b[ROWS * i : ROWS * (i + 1)] for i in order], axis=0)
         own[...] = a[:, :256] + b[:, :256]
         other = a[:, 256:] + b[:, 256:]
         top = peak(other)
@@ -199,14 +206,14 @@
             jax.ShapeDtypeStruct((m, 256), F32),
             jax.ShapeDtypeStruct((m + 16, 256), jnp.bfloat16),
         ),
-        in_specs=[VMEM] * (1 + len(backs)),
+        in_specs=[VMEM] * (1 + len(received)),
         out_specs=(VMEM, VMEM),
         compiler_params=SMALL,
-        cost_estimate=pl.CostEstimate(flops=0, bytes_accessed=m * 6000, transcendentals=0),
+        cost_estimate=takes(cost),
     )(keep, *received)
 
 
-def split_z(own, received, last_rows, backs):
+def split_z(own, received, last_rows, backs, cost):
     m = own.shape[0]
 
     def kernel(own, code, rows, *outs):
@@ -236,7 +243,7 @@
         in_specs=[VMEM] * 3,
         out_specs=tuple(VMEM for _ in backs),
         compiler_params=SMALL,
-        cost_estimate=pl.CostEstimate(flops=0, bytes_accessed=m * 2000, transcendentals=0),
+        cost_estimate=takes(cost),
     )(own, received, last_rows)
 
 
@@ -280,18 +287,13 @@
     rows, columns = gather(log_derivs, pack(log_derivs, sample_vector))
     last_rows = term(scale_update, columns)
 
-    blocks, sent, received = {}, [], []
-    for backs in GROUPS:
-        keep, *sends = products(scale_gram, [rows[back] for back in backs], columns)
-        sends = [swap(send, "core") for send in sends]
-        own, code = split_yhi(keep, sends, backs)
-        code = swap(after(code, *received), "yhi")
-        received.append(code)
-        waited, sent = sent, []
-        for back, block in zip(backs, split_z(own, code, last_rows, backs)):
-            blocks[back] = shift(after(block, *waited), "z", -back) if back else block
-            if back and len(sent) < 1:
-                sent.append(blocks[back])
+    blocks = {}
+    for backs, parts, costs in zip(GROUPS, PARTS, COSTS):
+        keep, *sends = products(scale_gram, [rows[back] for back in backs], columns, parts, costs[0])
+        own, code = split_yhi(keep, [swap(send, "core") for send in sends], backs, costs[1])
+        done = split_z(own, swap(code, "yhi"), last_rows, backs, costs[2])
+        for back, block in zip(backs, done):
+            blocks[back] = shift(block, "z", -back) if back else block
     return place(blocks.values(), list(blocks), last_rows)
 
 

time: 99.8 us -> 94.7 us (0.949)
  the two profiles are of different devices: /device:TPU:1 before, /device:TPU:16 now
where the time goes in v4:
time: 94.7 us; the launch traced here: 92.9 us
  starting transfers between devices  42.5 us (45%)
  waiting for transfers between devices  37.6 us (40%)
  Pallas kernels  10.5 us (11%)
  local copies, waits for them, and re-layouts  1.73 us (2%)
    ppermute x19, starting transfers between devices, shift(): return lax.ppermute(value, (axis, 'core'), pairs)  35 us
    ppermute x19, waiting for transfers between devices, shift(): return lax.ppermute(value, (axis, 'core'), pairs)  30.7 us
    ppermute x11, starting transfers between devices, swap(): return lax.ppermute(value, axis, [(0, 1), (1, 0)])  7.43 us
    ppermute x11, waiting for transfers between devices, swap(): return lax.ppermute(value, axis, [(0, 1), (1, 0)])  6.9 us
    pallas_call x2, Pallas kernels, products(): pl.pallas_call(kernel, out_shape=out, in_specs=[VMEM] * n + [ANYWHERE] *...  5.56 us
  transfers between devices with their start and end apart: 30, of which 18 were waited for; matrix products, arithmetic and copies ran while one was open for 0% of the time, Pallas kernels for 9%

profile of v4, /device:TPU:16, one launch (start us, length us, event | category | flops | bytes accessed | tf_op | source)
XLA Modules:
  0.0 92.9 jit_solution(14456505694086938335)
XLA Ops:
  0.6 2.0 %collective-permute-start = (bf16[128,2048]{1,0:T(8,128)(2,1)}, bf16[128,2048]{1,0:T(8,128)(2,1)S(1)}, u32[]{:S(2)}, u32[]{:S(2)}) collective-permute-start(bf16[128,2048]{1,0:T(8,128)(2,1)} %refs_0_.1), channel_id=1, source_target_pairs={{0,4},{1,29},{4,8},{5,1},{8,12},{9,5},{12,16},{13,9},{16,20},{17,1... | collective-permute-start | bytes 1572872 | tf_op jit(solution)/shard_map/ppermute | solution.py:30
  2.6 4.0 %collective-permute-start.1 = (bf16[128,2048]{1,0:T(8,128)(2,1)}, bf16[128,2048]{1,0:T(8,128)(2,1)S(1)}, u32[]{:S(2)}, u32[]{:S(2)}) collective-permute-start(bf16[128,2048]{1,0:T(8,128)(2,1)} %refs_0_.1), channel_id=1, source_target_pairs={{0,28},{1,5},{4,0},{5,9},{8,4},{9,13},{12,8},{13,17},{16,12},{17,2... | collective-permute-start | bytes 1572872 | tf_op jit(solution)/shard_map/ppermute | solution.py:30
  8.5 1.6 %collective-permute-start.4 = (bf16[128,2176]{1,0:T(8,128)(2,1)S(1)}, bf16[128,2176]{1,0:T(8,128)(2,1)S(1)}, u32[]{:S(2)}, u32[]{:S(2)}) collective-permute-start(bf16[128,2176]{1,0:T(8,128)(2,1)S(1)} %shard_map.41.refs_5_.refs_0_.refs_3_), channel_id=1, source_target_pairs={{0,32},{1,97},{32,64},{33,1},{64,96},{65,33},{96,0},{97,65},{2,34}... | collective-permute-start | bytes 1671176 | tf_op jit(solution)/shard_map/ppermute | solution.py:30
  11.3 1.7 %collective-permute-start.5 = (bf16[128,2176]{1,0:T(8,128)(2,1)S(1)}, bf16[128,2176]{1,0:T(8,128)(2,1)S(1)}, u32[]{:S(2)}, u32[]{:S(2)}) collective-permute-start(bf16[128,2176]{1,0:T(8,128)(2,1)S(1)} %shard_map.41.refs_5_.refs_0_.refs_3_), channel_id=1, source_target_pairs={{0,96},{1,33},{32,0},{33,65},{64,32},{65,97},{96,64},{97,1},{2,98}... | collective-permute-start | bytes 1671176 | tf_op jit(solution)/shard_map/ppermute | solution.py:30
  13.1 4.6 %collective-permute-done.refs_1_ = bf16[128,2048]{1,0:T(8,128)(2,1)S(1)} collective-permute-done((bf16[128,2048]{1,0:T(8,128)(2,1)}, bf16[128,2048]{1,0:T(8,128)(2,1)S(1)}, u32[]{:S(2)}, u32[]{:S(2)}) %collective-permute-start) | collective-permute-done | bytes 524320 | tf_op jit(solution)/shard_map/ppermute | solution.py:30
  18.1 3.6 %collective-permute-start.3 = (bf16[128,2048]{1,0:T(8,128)(2,1)S(1)}, bf16[128,2048]{1,0:T(8,128)(2,1)S(1)}, u32[]{:S(2)}, u32[]{:S(2)}) collective-permute-start(bf16[128,2048]{1,0:T(8,128)(2,1)S(1)} %collective-permute-done.1.refs_2_), channel_id=1, source_target_pairs={{0,28},{1,5},{4,0},{5,9},{8,4},{9,13},{12,8},{13,17},{16,12},{17,2... | collective-permute-start | bytes 1572872 | tf_op jit(solution)/shard_map/ppermute | solution.py:30
  21.6 1.6 %collective-permute-done.4.refs_6_.refs_1_.refs_4_ = bf16[128,2176]{1,0:T(8,128)(2,1)S(1)} collective-permute-done((bf16[128,2176]{1,0:T(8,128)(2,1)S(1)}, bf16[128,2176]{1,0:T(8,128)(2,1)S(1)}, u32[]{:S(2)}, u32[]{:S(2)}) %collective-permute-start.4) | collective-permute-done | bytes 557088 | tf_op jit(solution)/shard_map/ppermute | solution.py:30
  23.2 1.6 %collective-permute-start.6 = (bf16[128,2176]{1,0:T(8,128)(2,1)S(1)}, bf16[128,2176]{1,0:T(8,128)(2,1)S(1)}, u32[]{:S(2)}, u32[]{:S(2)}) collective-permute-start(bf16[128,2176]{1,0:T(8,128)(2,1)S(1)} %collective-permute-done.4.refs_6_.refs_1_.refs_4_), channel_id=1, source_target_pairs={{0,32},{1,97},{32,64},{33,1},{64,96},{65,33},{96,0},{97,65},{2,34}... | collective-permute-start | bytes 1671176 | tf_op jit(solution)/shard_map/ppermute | solution.py:30
  25.1 1.8 %collective-permute-start.8 = (bf16[128,2176]{1,0:T(8,128)(2,1)S(1)}, bf16[128,2176]{1,0:T(8,128)(2,1)S(1)}, u32[]{:S(2)}, u32[]{:S(2)}) collective-permute-start(bf16[128,2176]{1,0:T(8,128)(2,1)S(1)} %collective-permute-done.7.refs_9_.refs_4_.refs_7_), channel_id=1, source_target_pairs={{0,32},{1,97},{32,64},{33,1},{64,96},{65,33},{96,0},{97,65},{2,34}... | collective-permute-start | bytes 1671176 | tf_op jit(solution)/shard_map/ppermute | solution.py:30
  27.6 5.0 %collective-permute-done.2.refs_3_ = bf16[128,2048]{1,0:T(8,128)(2,1)S(1)} collective-permute-done((bf16[128,2048]{1,0:T(8,128)(2,1)S(1)}, bf16[128,2048]{1,0:T(8,128)(2,1)S(1)}, u32[]{:S(2)}, u32[]{:S(2)}) %collective-permute-start.2) | collective-permute-done | bytes 524320 | tf_op jit(solution)/shard_map/ppermute | solution.py:30
  32.6 3.2 %collective-permute-start.21 = (bf16[128,2048]{1,0:T(8,128)(2,1)S(1)}, bf16[128,2048]{1,0:T(8,128)(2,1)S(1)}, u32[]{:S(2)}, u32[]{:S(2)}) collective-permute-start(bf16[128,2048]{1,0:T(8,128)(2,1)S(1)} %collective-permute-done.3.refs_4_), channel_id=1, source_target_pairs={{0,28},{1,5},{4,0},{5,9},{8,4},{9,13},{12,8},{13,17},{16,12},{17,2... | collective-permute-start | bytes 1572872 | tf_op jit(solution)/shard_map/ppermute | solution.py:30
  35.8 4.4 %collective-permute-done.8.refs_10_.refs_5_.refs_8_ = bf16[128,2176]{1,0:T(8,128)(2,1)S(1)} collective-permute-done((bf16[128,2176]{1,0:T(8,128)(2,1)S(1)}, bf16[128,2176]{1,0:T(8,128)(2,1)S(1)}, u32[]{:S(2)}, u32[]{:S(2)}) %collective-permute-start.8) | collective-permute-done | bytes 557088 | tf_op jit(solution)/shard_map/ppermute | solution.py:30
  41.1 7.0 %collective-permute-done.20.refs_0_ = bf16[128,2048]{1,0:T(8,128)(2,1)S(1)} collective-permute-done((bf16[128,2048]{1,0:T(8,128)(2,1)S(1)}, bf16[128,2048]{1,0:T(8,128)(2,1)S(1)}, u32[]{:S(2)}, u32[]{:S(2)}) %collective-permute-start.20) | collective-permute-done | bytes 524320 | tf_op jit(solution)/shard_map/ppermute | solution.py:30
  48.1 2.8 %collective-permute-done.10.refs_12_.refs_7_.refs_10_ = bf16[128,2176]{1,0:T(8,128)(2,1)S(1)} collective-permute-done((bf16[128,2176]{1,0:T(8,128)(2,1)S(1)}, bf16[128,2176]{1,0:T(8,128)(2,1)S(1)}, u32[]{:S(2)}, u32[]{:S(2)}) %collective-permute-start.10) | collective-permute-done | bytes 557088 | tf_op jit(solution)/shard_map/ppermute | solution.py:30
  51.0 3.3 %shard_map.42 = (f32[640,512]{1,0:T(8,128)S(1)}, f32[160,512]{1,0:T(8,128)S(1)}, f32[160,512]{1,0:T(8,128)S(1)}, f32[160,512]{1,0:T(8,128)S(1)}, f32[160,512]{1,0:T(8,128)S(1)}) custom-call(bf16[128,2048]{1,0:T(8,128)(2,1)S(1)} %copy-done.1, bf16[128,2048]{1,0:T(8,128)(2,1)S(1)} %collective-permute-done.refs_1_, ...), custom_call_target="tpu_custom_call" | custom-call | tf_op jit(solution)/shard_map/pallas_call | solution.py:121
  58.5 2.2 %shard_map.46 = (f32[384,512]{1,0:T(8,128)S(1)}, f32[128,512]{1,0:T(8,128)S(1)}, f32[128,512]{1,0:T(8,128)S(1)}, f32[128,512]{1,0:T(8,128)S(1)}) custom-call(bf16[128,2048]{1,0:T(8,128)(2,1)S(1)} %collective-permute-done.20.refs_0_, bf16[128,2048]{1,0:T(8,128)(2,1)S(1)} %collective-permute-done.21.refs_1_, ...), custom_call_target="tpu_custom_call" | custom-call | flops 2200000000 | tf_op jit(solution)/shard_map/pallas_call | solution.py:121
  63.7 3.4 %collective-permute-start.26 = (bf16[400,256]{1,0:T(8,128)(2,1)S(1)}, bf16[400,256]{1,0:T(8,128)(2,1)S(1)}, u32[]{:S(2)}, u32[]{:S(2)}) collective-permute-start(bf16[400,256]{1,0:T(8,128)(2,1)S(1)} %get-tuple-element.44), channel_id=1, source_target_pairs={{0,2},{2,0},{1,3},{3,1},{4,6},{6,4},{5,7},{7,5},{8,10},{10,8},{9,1... | collective-permute-start | bytes 614408 | tf_op jit(solution)/shard_map/ppermute | solution.py:34
  67.0 3.5 %collective-permute-done.15.code = bf16[656,256]{1,0:T(8,128)(2,1)S(1)} collective-permute-done((bf16[656,256]{1,0:T(8,128)(2,1)S(1)}, bf16[656,256]{1,0:T(8,128)(2,1)S(1)}, u32[]{:S(2)}, u32[]{:S(2)}) %collective-permute-start.15) | collective-permute-done | bytes 335904 | tf_op jit(solution)/shard_map/ppermute | solution.py:34
  71.2 2.7 %collective-permute-start.16 = (bf16[144,256]{1,0:T(8,128)(2,1)S(1)}, bf16[144,256]{1,0:T(8,128)(2,1)S(1)}, u32[]{:S(2)}, u32[]{:S(2)}) collective-permute-start(bf16[144,256]{1,0:T(8,128)(2,1)S(1)} %get-tuple-element.34), channel_id=1, source_target_pairs={{0,28},{1,5},{4,0},{5,9},{8,4},{9,13},{12,8},{13,17},{16,12},{17,2... | collective-permute-start | bytes 221192 | tf_op jit(solution)/shard_map/ppermute | solution.py:30
  74.0 1.8 %collective-permute-start.18 = (bf16[144,256]{1,0:T(8,128)(2,1)S(1)}, bf16[144,256]{1,0:T(8,128)(2,1)S(1)}, u32[]{:S(2)}, u32[]{:S(2)}) collective-permute-start(bf16[144,256]{1,0:T(8,128)(2,1)S(1)} %get-tuple-element.36), channel_id=1, source_target_pairs={{0,24},{1,9},{4,28},{5,13},{8,0},{9,17},{12,4},{13,21},{16,8},{17,... | collective-permute-start | bytes 221192 | tf_op jit(solution)/shard_map/ppermute | solution.py:30
  77.4 3.8 %collective-permute-start.27 = (bf16[144,256]{1,0:T(8,128)(2,1)S(1)}, bf16[144,256]{1,0:T(8,128)(2,1)S(1)}, u32[]{:S(2)}, u32[]{:S(2)}) collective-permute-start(bf16[144,256]{1,0:T(8,128)(2,1)S(1)} %get-tuple-element.45), channel_id=1, source_target_pairs={{0,20},{1,13},{4,24},{5,17},{8,28},{9,21},{12,0},{13,25},{16,4},{1... | collective-permute-start | bytes 221192 | tf_op jit(solution)/shard_map/ppermute | solution.py:30
  82.8 3.7 %collective-permute-start.29 = (bf16[144,256]{1,0:T(8,128)(2,1)S(1)}, bf16[144,256]{1,0:T(8,128)(2,1)S(1)}, u32[]{:S(2)}, u32[]{:S(2)}) collective-permute-start(bf16[144,256]{1,0:T(8,128)(2,1)S(1)} %get-tuple-element.47), channel_id=1, source_target_pairs={{0,16},{1,17},{4,20},{5,21},{8,24},{9,25},{12,28},{13,29},{16,0},{... | collective-permute-start | bytes 221192 | tf_op jit(solution)/shard_map/ppermute | solution.py:30
  86.4 4.7 %collective-permute-done.28.refs_6_ = bf16[144,256]{1,0:T(8,128)(2,1)S(1)} collective-permute-done((bf16[144,256]{1,0:T(8,128)(2,1)S(1)}, bf16[144,256]{1,0:T(8,128)(2,1)S(1)}, u32[]{:S(2)}, u32[]{:S(2)}) %collective-permute-start.28) | collective-permute-done | bytes 73760 | tf_op jit(solution)/shard_map/ppermute | solution.py:30
  91.2 1.8 %shard_map.49 = (f32[128,2048]{1,0:T(8,128)}, f32[1,32]{1,0:T(1,128)}) custom-call(f32[128,256]{1,0:T(8,128)S(1)} %get-tuple-element.33.refs_0_, bf16[144,256]{1,0:T(8,128)(2,1)S(1)} %collective-permute-done.16.refs_1_, bf16[144,256]{1,0:T(8,128)(2,1)S(1)} %collective-permute-done.17.refs_2_, bf16[144,256]{1,0:T(8,128)(2,1)S(1)} %collective-permute-done.18.refs_3_, ...), custom_call_target="tpu_custom_call" | custom-call | bytes 2097152 | tf_op jit(solution)/shard_map/pallas_call | solution.py:270
  (51 shorter events, 16.4 us)
Async XLA Ops:
  0.6 17.0 %collective-permute-start = (bf16[128,2048]{1,0:T(8,128)(2,1)}, bf16[128,2048]{1,0:T(8,128)(2,1)S(1)}, u32[]{:S(2)}, u32[]{:S(2)}) collective-permute-start(bf16[128,2048]{1,0:T(8,128)(2,1)} %refs_0_.1), channel_id=1, source_target_pairs={{0,4},{1,29},{4,8},{5,1},{8,12},{9,5},{12,16},{13,9},{16,20},{17,1... | collective-permute-start | bytes 1572872 | tf_op jit(solution)/shard_map/ppermute | solution.py:30
  2.6 15.4 %collective-permute-start.1 = (bf16[128,2048]{1,0:T(8,128)(2,1)}, bf16[128,2048]{1,0:T(8,128)(2,1)S(1)}, u32[]{:S(2)}, u32[]{:S(2)}) collective-permute-start(bf16[128,2048]{1,0:T(8,128)(2,1)} %refs_0_.1), channel_id=1, source_target_pairs={{0,28},{1,5},{4,0},{5,9},{8,4},{9,13},{12,8},{13,17},{16,12},{17,2... | collective-permute-start | bytes 1572872 | tf_op jit(solution)/shard_map/ppermute | solution.py:30
  8.5 14.7 %collective-permute-start.4 = (bf16[128,2176]{1,0:T(8,128)(2,1)S(1)}, bf16[128,2176]{1,0:T(8,128)(2,1)S(1)}, u32[]{:S(2)}, u32[]{:S(2)}) collective-permute-start(bf16[128,2176]{1,0:T(8,128)(2,1)S(1)} %shard_map.41.refs_5_.refs_0_.refs_3_), channel_id=1, source_target_pairs={{0,32},{1,97},{32,64},{33,1},{64,96},{65,33},{96,0},{97,65},{2,34}... | collective-permute-start | bytes 1671176 | tf_op jit(solution)/shard_map/ppermute | solution.py:30
  10.1 15.0 %collective-permute-start.7 = (bf16[128,2176]{1,0:T(8,128)(2,1)S(1)}, bf16[128,2176]{1,0:T(8,128)(2,1)S(1)}, u32[]{:S(2)}, u32[]{:S(2)}) collective-permute-start(bf16[128,2176]{1,0:T(8,128)(2,1)S(1)} %shard_map.41.refs_5_.refs_0_.refs_3_), channel_id=1, source_target_pairs={{0,128},{128,0},{1,129},{129,1},{2,130},{130,2},{3,131},{131,3},{4... | collective-permute-start | bytes 1671176 | tf_op jit(solution)/shard_map/ppermute | solution.py:34
  11.3 15.5 %collective-permute-start.5 = (bf16[128,2176]{1,0:T(8,128)(2,1)S(1)}, bf16[128,2176]{1,0:T(8,128)(2,1)S(1)}, u32[]{:S(2)}, u32[]{:S(2)}) collective-permute-start(bf16[128,2176]{1,0:T(8,128)(2,1)S(1)} %shard_map.41.refs_5_.refs_0_.refs_3_), channel_id=1, source_target_pairs={{0,96},{1,33},{32,0},{33,65},{64,32},{65,97},{96,64},{97,1},{2,98}... | collective-permute-start | bytes 1671176 | tf_op jit(solution)/shard_map/ppermute | solution.py:30
  17.7 14.9 %collective-permute-start.2 = (bf16[128,2048]{1,0:T(8,128)(2,1)S(1)}, bf16[128,2048]{1,0:T(8,128)(2,1)S(1)}, u32[]{:S(2)}, u32[]{:S(2)}) collective-permute-start(bf16[128,2048]{1,0:T(8,128)(2,1)S(1)} %collective-permute-done.refs_1_), channel_id=1, source_target_pairs={{0,4},{1,29},{4,8},{5,1},{8,12},{9,5},{12,16},{13,9},{16,20},{17,1... | collective-permute-start | bytes 1572872 | tf_op jit(solution)/shard_map/ppermute | solution.py:30
  18.1 14.5 %collective-permute-start.3 = (bf16[128,2048]{1,0:T(8,128)(2,1)S(1)}, bf16[128,2048]{1,0:T(8,128)(2,1)S(1)}, u32[]{:S(2)}, u32[]{:S(2)}) collective-permute-start(bf16[128,2048]{1,0:T(8,128)(2,1)S(1)} %collective-permute-done.1.refs_2_), channel_id=1, source_target_pairs={{0,28},{1,5},{4,0},{5,9},{8,4},{9,13},{12,8},{13,17},{16,12},{17,2... | collective-permute-start | bytes 1572872 | tf_op jit(solution)/shard_map/ppermute | solution.py:30
  23.2 12.6 %collective-permute-start.6 = (bf16[128,2176]{1,0:T(8,128)(2,1)S(1)}, bf16[128,2176]{1,0:T(8,128)(2,1)S(1)}, u32[]{:S(2)}, u32[]{:S(2)}) collective-permute-start(bf16[128,2176]{1,0:T(8,128)(2,1)S(1)} %collective-permute-done.4.refs_6_.refs_1_.refs_4_), channel_id=1, source_target_pairs={{0,32},{1,97},{32,64},{33,1},{64,96},{65,33},{96,0},{97,65},{2,34}... | collective-permute-start | bytes 1671176 | tf_op jit(solution)/shard_map/ppermute | solution.py:30
  25.1 15.1 %collective-permute-start.8 = (bf16[128,2176]{1,0:T(8,128)(2,1)S(1)}, bf16[128,2176]{1,0:T(8,128)(2,1)S(1)}, u32[]{:S(2)}, u32[]{:S(2)}) collective-permute-start(bf16[128,2176]{1,0:T(8,128)(2,1)S(1)} %collective-permute-done.7.refs_9_.refs_4_.refs_7_), channel_id=1, source_target_pairs={{0,32},{1,97},{32,64},{33,1},{64,96},{65,33},{96,0},{97,65},{2,34}... | collective-permute-start | bytes 1671176 | tf_op jit(solution)/shard_map/ppermute | solution.py:30
  26.9 13.4 %collective-permute-start.9 = (bf16[128,2176]{1,0:T(8,128)(2,1)S(1)}, bf16[128,2176]{1,0:T(8,128)(2,1)S(1)}, u32[]{:S(2)}, u32[]{:S(2)}) collective-permute-start(bf16[128,2176]{1,0:T(8,128)(2,1)S(1)} %collective-permute-done.5.refs_7_.refs_2_.refs_5_), channel_id=1, source_target_pairs={{0,128},{128,0},{1,129},{129,1},{2,130},{130,2},{3,131},{131,3},{4... | collective-permute-start | bytes 1671176 | tf_op jit(solution)/shard_map/ppermute | solution.py:34
  32.6 15.6 %collective-permute-start.20 = (bf16[128,2048]{1,0:T(8,128)(2,1)S(1)}, bf16[128,2048]{1,0:T(8,128)(2,1)S(1)}, u32[]{:S(2)}, u32[]{:S(2)}) collective-permute-start(bf16[128,2048]{1,0:T(8,128)(2,1)S(1)} %collective-permute-done.2.refs_3_), channel_id=1, source_target_pairs={{0,4},{1,29},{4,8},{5,1},{8,12},{9,5},{12,16},{13,9},{16,20},{17,1... | collective-permute-start | bytes 1572872 | tf_op jit(solution)/shard_map/ppermute | solution.py:30
  32.6 15.6 %collective-permute-start.21 = (bf16[128,2048]{1,0:T(8,128)(2,1)S(1)}, bf16[128,2048]{1,0:T(8,128)(2,1)S(1)}, u32[]{:S(2)}, u32[]{:S(2)}) collective-permute-start(bf16[128,2048]{1,0:T(8,128)(2,1)S(1)} %collective-permute-done.3.refs_4_), channel_id=1, source_target_pairs={{0,28},{1,5},{4,0},{5,9},{8,4},{9,13},{12,8},{13,17},{16,12},{17,2... | collective-permute-start | bytes 1572872 | tf_op jit(solution)/shard_map/ppermute | solution.py:30
  40.2 10.7 %collective-permute-start.10 = (bf16[128,2176]{1,0:T(8,128)(2,1)S(1)}, bf16[128,2176]{1,0:T(8,128)(2,1)S(1)}, u32[]{:S(2)}, u32[]{:S(2)}) collective-permute-start(bf16[128,2176]{1,0:T(8,128)(2,1)S(1)} %collective-permute-done.8.refs_10_.refs_5_.refs_8_), channel_id=1, source_target_pairs={{0,32},{1,97},{32,64},{33,1},{64,96},{65,33},{96,0},{97,65},{2,34}... | collective-permute-start | bytes 1671176 | tf_op jit(solution)/shard_map/ppermute | solution.py:30
  48.1 10.4 %collective-permute-start.22 = (bf16[128,2048]{1,0:T(8,128)(2,1)S(1)}, bf16[128,2048]{1,0:T(8,128)(2,1)S(1)}, u32[]{:S(2)}, u32[]{:S(2)}) collective-permute-start(bf16[128,2048]{1,0:T(8,128)(2,1)S(1)} %collective-permute-done.20.refs_0_), channel_id=1, source_target_pairs={{0,4},{1,29},{4,8},{5,1},{8,12},{9,5},{12,16},{13,9},{16,20},{17,1... | collective-permute-start | bytes 1572872 | tf_op jit(solution)/shard_map/ppermute | solution.py:30
  55.0 2.4 %collective-permute-start.14 = (f32[160,512]{1,0:T(8,128)S(1)}, f32[160,512]{1,0:T(8,128)S(1)}, u32[]{:S(2)}, u32[]{:S(2)}) collective-permute-start(f32[160,512]{1,0:T(8,128)S(1)} %get-tuple-element.30), channel_id=1, source_target_pairs={{0,1},{1,0},{2,3},{3,2},{4,5},{5,4},{6,7},{7,6},{8,9},{9,8},{10,11... | collective-permute-start | bytes 983048 | tf_op jit(solution)/shard_map/ppermute | solution.py:34
  58.2 12.3 %collective-permute-start.15 = (bf16[656,256]{1,0:T(8,128)(2,1)S(1)}, bf16[656,256]{1,0:T(8,128)(2,1)S(1)}, u32[]{:S(2)}, u32[]{:S(2)}) collective-permute-start(bf16[656,256]{1,0:T(8,128)(2,1)S(1)} %get-tuple-element.32), channel_id=1, source_target_pairs={{0,2},{2,0},{1,3},{3,1},{4,6},{6,4},{5,7},{7,5},{8,10},{10,8},{9,1... | collective-permute-start | bytes 1007624 | tf_op jit(solution)/shard_map/ppermute | solution.py:34
  63.7 13.2 %collective-permute-start.26 = (bf16[400,256]{1,0:T(8,128)(2,1)S(1)}, bf16[400,256]{1,0:T(8,128)(2,1)S(1)}, u32[]{:S(2)}, u32[]{:S(2)}) collective-permute-start(bf16[400,256]{1,0:T(8,128)(2,1)S(1)} %get-tuple-element.44), channel_id=1, source_target_pairs={{0,2},{2,0},{1,3},{3,1},{4,6},{6,4},{5,7},{7,5},{8,10},{10,8},{9,1... | collective-permute-start | bytes 614408 | tf_op jit(solution)/shard_map/ppermute | solution.py:34
  71.2 10.0 %collective-permute-start.16 = (bf16[144,256]{1,0:T(8,128)(2,1)S(1)}, bf16[144,256]{1,0:T(8,128)(2,1)S(1)}, u32[]{:S(2)}, u32[]{:S(2)}) collective-permute-start(bf16[144,256]{1,0:T(8,128)(2,1)S(1)} %get-tuple-element.34), channel_id=1, source_target_pairs={{0,28},{1,5},{4,0},{5,9},{8,4},{9,13},{12,8},{13,17},{16,12},{17,2... | collective-permute-start | bytes 221192 | tf_op jit(solution)/shard_map/ppermute | solution.py:30
  74.0 8.8 %collective-permute-start.17 = (bf16[144,256]{1,0:T(8,128)(2,1)S(1)}, bf16[144,256]{1,0:T(8,128)(2,1)S(1)}, u32[]{:S(2)}, u32[]{:S(2)}) collective-permute-start(bf16[144,256]{1,0:T(8,128)(2,1)S(1)} %get-tuple-element.35), channel_id=1, source_target_pairs={{0,4},{1,29},{4,8},{5,1},{8,12},{9,5},{12,16},{13,9},{16,20},{17,1... | collective-permute-start | bytes 221192 | tf_op jit(solution)/shard_map/ppermute | solution.py:30
  74.0 12.5 %collective-permute-start.18 = (bf16[144,256]{1,0:T(8,128)(2,1)S(1)}, bf16[144,256]{1,0:T(8,128)(2,1)S(1)}, u32[]{:S(2)}, u32[]{:S(2)}) collective-permute-start(bf16[144,256]{1,0:T(8,128)(2,1)S(1)} %get-tuple-element.36), channel_id=1, source_target_pairs={{0,24},{1,9},{4,28},{5,13},{8,0},{9,17},{12,4},{13,21},{16,8},{17,... | collective-permute-start | bytes 221192 | tf_op jit(solution)/shard_map/ppermute | solution.py:30
  75.7 10.7 %collective-permute-start.19 = (bf16[144,256]{1,0:T(8,128)(2,1)S(1)}, bf16[144,256]{1,0:T(8,128)(2,1)S(1)}, u32[]{:S(2)}, u32[]{:S(2)}) collective-permute-start(bf16[144,256]{1,0:T(8,128)(2,1)S(1)} %get-tuple-element.37), channel_id=1, source_target_pairs={{0,8},{1,25},{4,12},{5,29},{8,16},{9,1},{12,20},{13,5},{16,24},{17... | collective-permute-start | bytes 221192 | tf_op jit(solution)/shard_map/ppermute | solution.py:30
  77.4 9.0 %collective-permute-start.27 = (bf16[144,256]{1,0:T(8,128)(2,1)S(1)}, bf16[144,256]{1,0:T(8,128)(2,1)S(1)}, u32[]{:S(2)}, u32[]{:S(2)}) collective-permute-start(bf16[144,256]{1,0:T(8,128)(2,1)S(1)} %get-tuple-element.45), channel_id=1, source_target_pairs={{0,20},{1,13},{4,24},{5,17},{8,28},{9,21},{12,0},{13,25},{16,4},{1... | collective-permute-start | bytes 221192 | tf_op jit(solution)/shard_map/ppermute | solution.py:30
  81.2 10.0 %collective-permute-start.28 = (bf16[144,256]{1,0:T(8,128)(2,1)S(1)}, bf16[144,256]{1,0:T(8,128)(2,1)S(1)}, u32[]{:S(2)}, u32[]{:S(2)}) collective-permute-start(bf16[144,256]{1,0:T(8,128)(2,1)S(1)} %get-tuple-element.46), channel_id=1, source_target_pairs={{0,12},{1,21},{4,16},{5,25},{8,20},{9,29},{12,24},{13,1},{16,28},{... | collective-permute-start | bytes 221192 | tf_op jit(solution)/shard_map/ppermute | solution.py:30
  82.8 8.4 %collective-permute-start.29 = (bf16[144,256]{1,0:T(8,128)(2,1)S(1)}, bf16[144,256]{1,0:T(8,128)(2,1)S(1)}, u32[]{:S(2)}, u32[]{:S(2)}) collective-permute-start(bf16[144,256]{1,0:T(8,128)(2,1)S(1)} %get-tuple-element.47), channel_id=1, source_target_pairs={{0,16},{1,17},{4,20},{5,21},{8,24},{9,25},{12,28},{13,29},{16,0},{... | collective-permute-start | bytes 221192 | tf_op jit(solution)/shard_map/ppermute | solution.py:30
  (9 other events, 55.5 us)

commit v5 on v4

--- a/solution.py
+++ b/solution.py
@@ -14,7 +14,8 @@
 F32 = jnp.float32
 GROUPS = ((0, 1, -1, 2, -2), (3, -3, 4))
 PARTS = ((160,) * 4, (128,) * 3)
-COSTS = ((0, 0, 10), (2.2, 0.5, 0.5))
+COSTS = ((0, 0, 10), (1.1, 0.5, 0.5))
+PLACE_COSTS = (0, 0)
 VMEM = pl.BlockSpec(memory_space=pltpu.VMEM)
 ANYWHERE = pl.BlockSpec(memory_space=pl.ANY)
 SMALL = pltpu.CompilerParams(vmem_limit_bytes=16 * 2**20)
@@ -83,13 +84,11 @@
     )(log_derivs, sample_vector[None])
 
 
-def products(scale, rows, columns, parts, cost):
-    m, n = ROWS * len(rows), len(rows)
+def products(scale, rows, columns, other, parts, cost):
+    n = len(rows)
 
     def kernel(*refs):
-        cols = refs[n : n + len(columns)]
-        keep, *sends = refs[n + len(columns) : -2]
-        held, sems = refs[-2:]
+        cols, outs, (held, sems) = refs[n : n + len(columns)], refs[n + len(columns) : -2], refs[-2:]
         copies = []
         for i, (ref, (ylo, back)) in enumerate(zip(cols, columns)):
             x = lax.rem(lax.axis_index("x") + NX - turn(back), NX)
@@ -97,34 +96,30 @@
             yhi = lax.rem(lax.axis_index("ylo") + ylo + lax.axis_index("yhi"), 2)
             to = pl.multiple_of(lax.rem(x, 2) * ROWS, ROWS)
             copy = pltpu.make_async_copy(
-                ref.at[:, pl.ds(0, PANEL)], held.at[2 * core + yhi, pl.ds(to, ROWS)], sems.at[i]
+                ref.at[:, pl.ds(0, PANEL)], held.at[yhi, pl.ds(to, ref.shape[0])], sems.at[i]
             )
-            copy.start()
-            copies.append(copy)
-        for copy in copies:
-            copy.wait()
+            copies.append((core == other, copy))
+        for mine, copy in copies:
+            pl.when(mine)(copy.start)
+        for mine, copy in copies:
+            pl.when(mine)(copy.wait)
         block = jnp.concatenate([r[...] for r in refs[:n]], axis=0)
-        for pair in (2, 3, 0, 1):
-            at = slice(256 * (pair % 2), 256 * (pair % 2) + 256)
+        for pair in range(2):
             value = scale * lax.dot_general(
                 block, held[pair], (((1,), (1,)), ((), ())), preferred_element_type=F32
             )
-            if pair < 2:
-                keep[:, at] = value
-            else:
-                first = 0
-                for send in sends:
-                    send[:, at] = value[first : first + send.shape[0]]
-                    first += send.shape[0]
-
-    out = [jax.ShapeDtypeStruct((count, 512), F32) for count in (m, *parts)]
-    return pl.pallas_call(
-        kernel,
-        out_shape=out,
+            first = 0
+            for out in outs:
+                out[:, 256 * pair : 256 * pair + 256] = value[first : first + out.shape[0]]
+                first += out.shape[0]
+
+    return pl.pallas_call(
+        kernel,
+        out_shape=[jax.ShapeDtypeStruct((count, 512), F32) for count in parts],
         in_specs=[VMEM] * n + [ANYWHERE] * len(columns),
-        out_specs=[VMEM] * len(out),
+        out_specs=[VMEM] * len(parts),
         scratch_shapes=[
-            pltpu.VMEM((4, 256, PANEL), jnp.bfloat16),
+            pltpu.VMEM((2, 256, PANEL), jnp.bfloat16),
             pltpu.SemaphoreType.DMA((len(columns),)),
         ],
         compiler_params=pltpu.CompilerParams(vmem_limit_bytes=24 * 2**20),
@@ -138,14 +133,15 @@
         out, held, vecs, sems = refs[len(columns) :]
         u = lax.axis_index("ylo") * NX + lax.axis_index("x")
         mine = pl.multiple_of(u * 256, 256)
-        copies = []
+        copies, to = [], 0
         for i, ref in enumerate(cols):
             for j, (part, target) in enumerate(((pl.ds(mine, 256), held), (pl.ds(PANEL, ROWS), vecs))):
                 copy = pltpu.make_async_copy(
-                    ref.at[:, part], target.at[pl.ds(ROWS * i, ROWS)], sems.at[2 * i + j]
+                    ref.at[:, part], target.at[pl.ds(to, ref.shape[0])], sems.at[2 * i + j]
                 )
                 copy.start()
                 copies.append(copy)
+            to += ref.shape[0]
         for copy in copies:
             copy.wait()
         parts = lax.dot_general(
@@ -247,37 +243,51 @@
     )(own, received, last_rows)
 
 
-def place(blocks, backs, last_rows):
+def place(blocks, total, gram, last, cost):
+    n, held = len(blocks), [] if gram is None else [gram]
+
     def kernel(*refs):
-        rows, out, update = refs[len(blocks) :]
-        total = rows[:1]
-        for block, back in zip(refs, backs):
+        out, result, stage, sems = refs[n + 1 + len(held) :]
+        sum_of = refs[n][:1]
+        copies = []
+        for i, (block, back) in enumerate(zip(refs, blocks)):
             z = lax.rem(lax.axis_index("z") + NZ + turn(back), NZ)
             at = pl.multiple_of(z * ROWS, ROWS)
             if back:
                 tail = block[ROWS:]
-                value = decode(block[:ROWS], tail)
-                total = total + jnp.sum(tail[1:4].astype(F32), axis=0, keepdims=True)
+                stage[i] = decode(block[:ROWS], tail)
+                sum_of = sum_of + jnp.sum(tail[1:4].astype(F32), axis=0, keepdims=True)
             else:
-                value = block[...]
-            out[:, pl.ds(at, ROWS)] = value[:, :ROWS]
-            out[:, pl.ds(at + NZ * ROWS, ROWS)] = value[:, ROWS:]
-        owned = jnp.zeros((1, 32), F32)
-        for z in range(NZ):
-            owned = jnp.where(lax.axis_index("z") == z, total[:, 32 * z : 32 * z + 32], owned)
-        update[...] = owned
+                stage[i] = block[...]
+            for odd in range(2):
+                copy = pltpu.make_async_copy(
+                    stage.at[i, :, pl.ds(odd * ROWS, ROWS)],
+                    out.at[:, pl.ds(at + odd * NZ * ROWS, ROWS)],
+                    sems.at[i, odd],
+                )
+                copy.start()
+                copies.append(copy)
+        if last:
+            turned = pltpu.roll(jnp.broadcast_to(sum_of, (8, 256)), 256 - 32 * lax.axis_index("z"), 1)
+            result[...] = turned[:1, :32]
+        else:
+            result[...] = jnp.broadcast_to(sum_of, (8, 256))
+        for copy in copies:
+            copy.wait()
 
     return pl.pallas_call(
         kernel,
         out_shape=(
             jax.ShapeDtypeStruct((ROWS, PANEL), F32),
-            jax.ShapeDtypeStruct((1, 32), F32),
+            jax.ShapeDtypeStruct((1, 32) if last else (8, 256), F32),
         ),
-        in_specs=[VMEM] * (len(blocks) + 1),
-        out_specs=(VMEM, VMEM),
-        compiler_params=SMALL,
-        cost_estimate=pl.CostEstimate(flops=0, bytes_accessed=2**21, transcendentals=0),
-    )(*blocks, last_rows)
+        in_specs=[VMEM] * (n + 1) + [ANYWHERE] * len(held),
+        out_specs=(ANYWHERE, VMEM),
+        scratch_shapes=[pltpu.VMEM((n, ROWS, 256), F32), pltpu.SemaphoreType.DMA((n, 2))],
+        input_output_aliases={n + 1: 0} if held else {},
+        compiler_params=SMALL,
+        cost_estimate=takes(cost),
+    )(*blocks.values(), total, *held)
 
 
 def body(log_derivs, sample_vector):
@@ -289,12 +299,19 @@
 
     blocks = {}
     for backs, parts, costs in zip(GROUPS, PARTS, COSTS):
-        keep, *sends = products(scale_gram, [rows[back] for back in backs], columns, parts, costs[0])
-        own, code = split_yhi(keep, [swap(send, "core") for send in sends], backs, costs[1])
+        factors = [rows[back] for back in backs]
+        sends = products(scale_gram, factors, columns, 1, parts, costs[0])
+        received = [swap(send, "core") for send in sends]
+        (keep,) = products(scale_gram, factors, columns, 0, (sum(parts),), costs[0])
+        own, code = split_yhi(keep, received, backs, costs[1])
         done = split_z(own, swap(code, "yhi"), last_rows, backs, costs[2])
         for back, block in zip(backs, done):
             blocks[back] = shift(block, "z", -back) if back else block
-    return place(blocks.values(), list(blocks), last_rows)
+
+    gram, total = None, last_rows
+    for backs, cost in zip(GROUPS, PLACE_COSTS):
+        gram, total = place({back: blocks[back] for back in backs}, total, gram, backs == GROUPS[-1], cost)
+    return gram, total
 
 
 def solution(mesh):

time: 94.7 us -> 91.1 us (0.962); the launches traced: 92.9 us -> 90.9 us
  starting transfers between devices: 42.5 us -> 39.2 us
  Pallas kernels: 10.5 us -> 11.8 us
    ppermute x11, starting transfers between devices: 7.43 us -> 5.67 us  [swap(): return lax.ppermute(value, axis, [(0, 1), (1, 0)])]
    ppermute x19, starting transfers between devices: 35 us -> 33.5 us  [shift(): return lax.ppermute(value, (axis, 'core'), pairs)]
    pallas_call x1 -> x2, Pallas kernels: 1.76 us -> 2.48 us  [place(): pl.pallas_call(kernel, out_shape=(jax.ShapeDtypeStruct((ROWS, PANEL), F32...]
    pallas_call x2 -> x4, Pallas kernels: 5.56 us -> 6.15 us  [products(): pl.pallas_call(kernel, out_shape=[jax.ShapeDtypeStruct((count, 512), F32)...]
  transfers between devices with their start and end apart: 30 -> 30, of which waited for: 18 -> 15; matrix products, arithmetic and copies ran while one was open for 0% -> 0% of each run, Pallas kernels for 9% -> 11%
where the time goes in v5:
time: 91.1 us; the launch traced here: 90.9 us
  starting transfers between devices  39.2 us (43%)
  waiting for transfers between devices  37.3 us (41%)
  Pallas kernels  11.8 us (13%)
  local copies, waits for them, and re-layouts  1.73 us (2%)
  between operations  0.98 us (1%)
    ppermute x19, starting transfers between devices, shift(): return lax.ppermute(value, (axis, 'core'), pairs)  33.5 us
    ppermute x19, waiting for transfers between devices, shift(): return lax.ppermute(value, (axis, 'core'), pairs)  30.3 us
    ppermute x11, waiting for transfers between devices, swap(): return lax.ppermute(value, axis, [(0, 1), (1, 0)])  6.97 us
    pallas_call x4, Pallas kernels, products(): pl.pallas_call(kernel, out_shape=[jax.ShapeDtypeStruct((count, 512), F32)...  6.15 us
    ppermute x11, starting transfers between devices, swap(): return lax.ppermute(value, axis, [(0, 1), (1, 0)])  5.67 us
    pallas_call x2, Pallas kernels, place(): pl.pallas_call(kernel, out_shape=(jax.ShapeDtypeStruct((ROWS, PANEL), F32...  2.48 us
  transfers between devices with their start and end apart: 30, of which 15 were waited for; matrix products, arithmetic and copies ran while one was open for 0% of the time, Pallas kernels for 11%

profile of v5, /device:TPU:16, one launch (start us, length us, event | category | flops | bytes accessed | tf_op | source)
XLA Modules:
  0.0 90.9 jit_solution(15677933437236127575)
XLA Ops:
  0.6 2.0 %collective-permute-start = (bf16[128,2048]{1,0:T(8,128)(2,1)}, bf16[128,2048]{1,0:T(8,128)(2,1)S(1)}, u32[]{:S(2)}, u32[]{:S(2)}) collective-permute-start(bf16[128,2048]{1,0:T(8,128)(2,1)} %refs_0_.3), channel_id=1, source_target_pairs={{0,4},{1,29},{4,8},{5,1},{8,12},{9,5},{12,16},{13,9},{16,20},{17,1... | collective-permute-start | bytes 1572872 | tf_op jit(solution)/shard_map/ppermute | solution.py:31
  2.6 4.0 %collective-permute-start.3 = (bf16[128,2048]{1,0:T(8,128)(2,1)}, bf16[128,2048]{1,0:T(8,128)(2,1)S(1)}, u32[]{:S(2)}, u32[]{:S(2)}) collective-permute-start(bf16[128,2048]{1,0:T(8,128)(2,1)} %refs_0_.3), channel_id=1, source_target_pairs={{0,28},{1,5},{4,0},{5,9},{8,4},{9,13},{12,8},{13,17},{16,12},{17,2... | collective-permute-start | bytes 1572872 | tf_op jit(solution)/shard_map/ppermute | solution.py:31
  8.5 1.4 %collective-permute-start.10 = (bf16[128,2176]{1,0:T(8,128)(2,1)S(1)}, bf16[128,2176]{1,0:T(8,128)(2,1)S(1)}, u32[]{:S(2)}, u32[]{:S(2)}) collective-permute-start(bf16[128,2176]{1,0:T(8,128)(2,1)S(1)} %shard_map.41.refs_3_.refs_0_.refs_5_), channel_id=1, source_target_pairs={{0,128},{128,0},{1,129},{129,1},{2,130},{130,2},{3,131},{131,3},{4... | collective-permute-start | bytes 1671176 | tf_op jit(solution)/shard_map/ppermute | solution.py:35
  9.9 2.8 %collective-permute-start.8 = (bf16[128,2176]{1,0:T(8,128)(2,1)S(1)}, bf16[128,2176]{1,0:T(8,128)(2,1)S(1)}, u32[]{:S(2)}, u32[]{:S(2)}) collective-permute-start(bf16[128,2176]{1,0:T(8,128)(2,1)S(1)} %shard_map.41.refs_3_.refs_0_.refs_5_), channel_id=1, source_target_pairs={{0,96},{1,33},{32,0},{33,65},{64,32},{65,97},{96,64},{97,1},{2,98}... | collective-permute-start | bytes 1671176 | tf_op jit(solution)/shard_map/ppermute | solution.py:31
  12.6 5.0 %collective-permute-done.refs_1_ = bf16[128,2048]{1,0:T(8,128)(2,1)S(1)} collective-permute-done((bf16[128,2048]{1,0:T(8,128)(2,1)}, bf16[128,2048]{1,0:T(8,128)(2,1)S(1)}, u32[]{:S(2)}, u32[]{:S(2)}) %collective-permute-start) | collective-permute-done | bytes 524320 | tf_op jit(solution)/shard_map/ppermute | solution.py:31
  18.1 3.6 %collective-permute-start.4 = (bf16[128,2048]{1,0:T(8,128)(2,1)S(1)}, bf16[128,2048]{1,0:T(8,128)(2,1)S(1)}, u32[]{:S(2)}, u32[]{:S(2)}) collective-permute-start(bf16[128,2048]{1,0:T(8,128)(2,1)S(1)} %collective-permute-done.3.refs_2_), channel_id=1, source_target_pairs={{0,28},{1,5},{4,0},{5,9},{8,4},{9,13},{12,8},{13,17},{16,12},{17,2... | collective-permute-start | bytes 1572872 | tf_op jit(solution)/shard_map/ppermute | solution.py:31
  22.6 1.5 %collective-permute-start.11 = (bf16[128,2176]{1,0:T(8,128)(2,1)S(1)}, bf16[128,2176]{1,0:T(8,128)(2,1)S(1)}, u32[]{:S(2)}, u32[]{:S(2)}) collective-permute-start(bf16[128,2176]{1,0:T(8,128)(2,1)S(1)} %collective-permute-done.10.refs_7_.refs_4_.refs_9_), channel_id=1, source_target_pairs={{0,32},{1,97},{32,64},{33,1},{64,96},{65,33},{96,0},{97,65},{2,34}... | collective-permute-start | bytes 1671176 | tf_op jit(solution)/shard_map/ppermute | solution.py:31
  26.0 1.5 %collective-permute-start.9 = (bf16[128,2176]{1,0:T(8,128)(2,1)S(1)}, bf16[128,2176]{1,0:T(8,128)(2,1)S(1)}, u32[]{:S(2)}, u32[]{:S(2)}) collective-permute-start(bf16[128,2176]{1,0:T(8,128)(2,1)S(1)} %collective-permute-done.7.refs_4_.refs_1_.refs_6_), channel_id=1, source_target_pairs={{0,32},{1,97},{32,64},{33,1},{64,96},{65,33},{96,0},{97,65},{2,34}... | collective-permute-start | bytes 1671176 | tf_op jit(solution)/shard_map/ppermute | solution.py:31
  27.5 5.0 %collective-permute-done.1.refs_3_ = bf16[128,2048]{1,0:T(8,128)(2,1)S(1)} collective-permute-done((bf16[128,2048]{1,0:T(8,128)(2,1)S(1)}, bf16[128,2048]{1,0:T(8,128)(2,1)S(1)}, u32[]{:S(2)}, u32[]{:S(2)}) %collective-permute-start.1) | collective-permute-done | bytes 524320 | tf_op jit(solution)/shard_map/ppermute | solution.py:31
  32.6 3.2 %collective-permute-start.5 = (bf16[128,2048]{1,0:T(8,128)(2,1)S(1)}, bf16[128,2048]{1,0:T(8,128)(2,1)S(1)}, u32[]{:S(2)}, u32[]{:S(2)}) collective-permute-start(bf16[128,2048]{1,0:T(8,128)(2,1)S(1)} %collective-permute-done.4.refs_4_), channel_id=1, source_target_pairs={{0,28},{1,5},{4,0},{5,9},{8,4},{9,13},{12,8},{13,17},{16,12},{17,2... | collective-permute-start | bytes 1572872 | tf_op jit(solution)/shard_map/ppermute | solution.py:31
  35.8 2.4 %collective-permute-done.12.refs_9_.refs_6_.refs_11_ = bf16[128,2176]{1,0:T(8,128)(2,1)S(1)} collective-permute-done((bf16[128,2176]{1,0:T(8,128)(2,1)S(1)}, bf16[128,2176]{1,0:T(8,128)(2,1)S(1)}, u32[]{:S(2)}, u32[]{:S(2)}) %collective-permute-start.12) | collective-permute-done | bytes 557088 | tf_op jit(solution)/shard_map/ppermute | solution.py:35
  39.6 8.5 %collective-permute-done.2.refs_0_ = bf16[128,2048]{1,0:T(8,128)(2,1)S(1)} collective-permute-done((bf16[128,2048]{1,0:T(8,128)(2,1)S(1)}, bf16[128,2048]{1,0:T(8,128)(2,1)S(1)}, u32[]{:S(2)}, u32[]{:S(2)}) %collective-permute-start.2) | collective-permute-done | bytes 524320 | tf_op jit(solution)/shard_map/ppermute | solution.py:31
  48.1 1.9 %collective-permute-done.13.refs_10_.refs_7_.refs_12_ = bf16[128,2176]{1,0:T(8,128)(2,1)S(1)} collective-permute-done((bf16[128,2176]{1,0:T(8,128)(2,1)S(1)}, bf16[128,2176]{1,0:T(8,128)(2,1)S(1)}, u32[]{:S(2)}, u32[]{:S(2)}) %collective-permute-start.13) | collective-permute-done | bytes 557088 | tf_op jit(solution)/shard_map/ppermute | solution.py:31
  50.1 1.8 %shard_map.48 = (f32[160,512]{1,0:T(8,128)S(1)}, f32[160,512]{1,0:T(8,128)S(1)}, f32[160,512]{1,0:T(8,128)S(1)}, f32[160,512]{1,0:T(8,128)S(1)}) custom-call(bf16[128,2048]{1,0:T(8,128)(2,1)S(1)} %copy-done.1, bf16[128,2048]{1,0:T(8,128)(2,1)S(1)} %collective-permute-done.refs_1_, bf16[128,2048]{1,0:T(8,128)(2,1)S(1)} %collective-permute-done.3.refs_2_, ...), custom_call_target="tpu_custom_call" | custom-call | tf_op jit(solution)/shard_map/pallas_call | solution.py:116
  53.2 1.8 %shard_map.47.a = f32[640,512]{1,0:T(8,128)S(1)} custom-call(bf16[128,2048]{1,0:T(8,128)(2,1)S(1)} %copy-done.1, bf16[128,2048]{1,0:T(8,128)(2,1)S(1)} %collective-permute-done.refs_1_, bf16[128,2048]{1,0:T(8,128)(2,1)S(1)} %collective-permute-done.3.refs_2_, bf16[128,2048]{1,0:T(8,128)(2,1)S(1)} %collective-permute-done.1.refs_3_, ...), custom_call_target="tpu_custom_call" | custom-call | tf_op jit(solution)/shard_map/pallas_call | solution.py:116
  56.4 2.1 %collective-permute-done.6.refs_2_ = bf16[128,2048]{1,0:T(8,128)(2,1)S(1)} collective-permute-done((bf16[128,2048]{1,0:T(8,128)(2,1)S(1)}, bf16[128,2048]{1,0:T(8,128)(2,1)S(1)}, u32[]{:S(2)}, u32[]{:S(2)}) %collective-permute-start.6) | collective-permute-done | bytes 524320 | tf_op jit(solution)/shard_map/ppermute | solution.py:31
  64.1 3.4 %collective-permute-done.25.code = bf16[656,256]{1,0:T(8,128)(2,1)S(1)} collective-permute-done((bf16[656,256]{1,0:T(8,128)(2,1)S(1)}, bf16[656,256]{1,0:T(8,128)(2,1)S(1)}, u32[]{:S(2)}, u32[]{:S(2)}) %collective-permute-start.25) | collective-permute-done | bytes 335904 | tf_op jit(solution)/shard_map/ppermute | solution.py:35
  68.2 3.8 %collective-permute-start.26 = (bf16[144,256]{1,0:T(8,128)(2,1)S(1)}, bf16[144,256]{1,0:T(8,128)(2,1)S(1)}, u32[]{:S(2)}, u32[]{:S(2)}) collective-permute-start(bf16[144,256]{1,0:T(8,128)(2,1)S(1)} %get-tuple-element.42), channel_id=1, source_target_pairs={{0,28},{1,5},{4,0},{5,9},{8,4},{9,13},{12,8},{13,17},{16,12},{17,2... | collective-permute-start | bytes 221192 | tf_op jit(solution)/shard_map/ppermute | solution.py:31
  72.0 1.6 %collective-permute-start.28 = (bf16[144,256]{1,0:T(8,128)(2,1)S(1)}, bf16[144,256]{1,0:T(8,128)(2,1)S(1)}, u32[]{:S(2)}, u32[]{:S(2)}) collective-permute-start(bf16[144,256]{1,0:T(8,128)(2,1)S(1)} %get-tuple-element.44), channel_id=1, source_target_pairs={{0,24},{1,9},{4,28},{5,13},{8,0},{9,17},{12,4},{13,21},{16,8},{17,... | collective-permute-start | bytes 221192 | tf_op jit(solution)/shard_map/ppermute | solution.py:31
  73.5 1.4 %collective-permute-start.29 = (bf16[144,256]{1,0:T(8,128)(2,1)S(1)}, bf16[144,256]{1,0:T(8,128)(2,1)S(1)}, u32[]{:S(2)}, u32[]{:S(2)}) collective-permute-start(bf16[144,256]{1,0:T(8,128)(2,1)S(1)} %get-tuple-element.45), channel_id=1, source_target_pairs={{0,8},{1,25},{4,12},{5,29},{8,16},{9,1},{12,20},{13,5},{16,24},{17... | collective-permute-start | bytes 221192 | tf_op jit(solution)/shard_map/ppermute | solution.py:31
  75.4 2.8 %collective-permute-start.18 = (bf16[144,256]{1,0:T(8,128)(2,1)S(1)}, bf16[144,256]{1,0:T(8,128)(2,1)S(1)}, u32[]{:S(2)}, u32[]{:S(2)}) collective-permute-start(bf16[144,256]{1,0:T(8,128)(2,1)S(1)} %get-tuple-element.32), channel_id=1, source_target_pairs={{0,20},{1,13},{4,24},{5,17},{8,28},{9,21},{12,0},{13,25},{16,4},{1... | collective-permute-start | bytes 221192 | tf_op jit(solution)/shard_map/ppermute | solution.py:31
  79.3 4.0 %collective-permute-start.20 = (bf16[144,256]{1,0:T(8,128)(2,1)S(1)}, bf16[144,256]{1,0:T(8,128)(2,1)S(1)}, u32[]{:S(2)}, u32[]{:S(2)}) collective-permute-start(bf16[144,256]{1,0:T(8,128)(2,1)S(1)} %get-tuple-element.34), channel_id=1, source_target_pairs={{0,16},{1,17},{4,20},{5,21},{8,24},{9,25},{12,28},{13,29},{16,0},{... | collective-permute-start | bytes 221192 | tf_op jit(solution)/shard_map/ppermute | solution.py:31
  85.2 3.5 %collective-permute-done.19.refs_1_ = bf16[144,256]{1,0:T(8,128)(2,1)S(1)} collective-permute-done((bf16[144,256]{1,0:T(8,128)(2,1)S(1)}, bf16[144,256]{1,0:T(8,128)(2,1)S(1)}, u32[]{:S(2)}, u32[]{:S(2)}) %collective-permute-start.19) | collective-permute-done | bytes 73760 | tf_op jit(solution)/shard_map/ppermute | solution.py:31
  89.3 1.5 %shard_map.52 = (f32[128,2048]{1,0:T(8,128)}, f32[1,32]{1,0:T(1,128)}) custom-call(bf16[144,256]{1,0:T(8,128)(2,1)S(1)} %collective-permute-done.18.refs_0_, bf16[144,256]{1,0:T(8,128)(2,1)S(1)} %collective-permute-done.19.refs_1_, bf16[144,256]{1,0:T(8,128)(2,1)S(1)} %collective-permute-done.20.refs_2_, ...), custom_call_target="tpu_custom_call", output_to_operand_aliasing={{0}: (4, {})} | custom-call | tf_op jit(solution)/shard_map/pallas_call | solution.py:278
  (54 shorter events, 19.6 us)
Async XLA Ops:
  0.6 17.0 %collective-permute-start = (bf16[128,2048]{1,0:T(8,128)(2,1)}, bf16[128,2048]{1,0:T(8,128)(2,1)S(1)}, u32[]{:S(2)}, u32[]{:S(2)}) collective-permute-start(bf16[128,2048]{1,0:T(8,128)(2,1)} %refs_0_.3), channel_id=1, source_target_pairs={{0,4},{1,29},{4,8},{5,1},{8,12},{9,5},{12,16},{13,9},{16,20},{17,1... | collective-permute-start | bytes 1572872 | tf_op jit(solution)/shard_map/ppermute | solution.py:31
  2.6 15.4 %collective-permute-start.3 = (bf16[128,2048]{1,0:T(8,128)(2,1)}, bf16[128,2048]{1,0:T(8,128)(2,1)S(1)}, u32[]{:S(2)}, u32[]{:S(2)}) collective-permute-start(bf16[128,2048]{1,0:T(8,128)(2,1)} %refs_0_.3), channel_id=1, source_target_pairs={{0,28},{1,5},{4,0},{5,9},{8,4},{9,13},{12,8},{13,17},{16,12},{17,2... | collective-permute-start | bytes 1572872 | tf_op jit(solution)/shard_map/ppermute | solution.py:31
  8.5 14.1 %collective-permute-start.10 = (bf16[128,2176]{1,0:T(8,128)(2,1)S(1)}, bf16[128,2176]{1,0:T(8,128)(2,1)S(1)}, u32[]{:S(2)}, u32[]{:S(2)}) collective-permute-start(bf16[128,2176]{1,0:T(8,128)(2,1)S(1)} %shard_map.41.refs_3_.refs_0_.refs_5_), channel_id=1, source_target_pairs={{0,128},{128,0},{1,129},{129,1},{2,130},{130,2},{3,131},{131,3},{4... | collective-permute-start | bytes 1671176 | tf_op jit(solution)/shard_map/ppermute | solution.py:35
  9.9 15.4 %collective-permute-start.8 = (bf16[128,2176]{1,0:T(8,128)(2,1)S(1)}, bf16[128,2176]{1,0:T(8,128)(2,1)S(1)}, u32[]{:S(2)}, u32[]{:S(2)}) collective-permute-start(bf16[128,2176]{1,0:T(8,128)(2,1)S(1)} %shard_map.41.refs_3_.refs_0_.refs_5_), channel_id=1, source_target_pairs={{0,96},{1,33},{32,0},{33,65},{64,32},{65,97},{96,64},{97,1},{2,98}... | collective-permute-start | bytes 1671176 | tf_op jit(solution)/shard_map/ppermute | solution.py:31
  12.6 13.4 %collective-permute-start.7 = (bf16[128,2176]{1,0:T(8,128)(2,1)S(1)}, bf16[128,2176]{1,0:T(8,128)(2,1)S(1)}, u32[]{:S(2)}, u32[]{:S(2)}) collective-permute-start(bf16[128,2176]{1,0:T(8,128)(2,1)S(1)} %shard_map.41.refs_3_.refs_0_.refs_5_), channel_id=1, source_target_pairs={{0,32},{1,97},{32,64},{33,1},{64,96},{65,33},{96,0},{97,65},{2,34}... | collective-permute-start | bytes 1671176 | tf_op jit(solution)/shard_map/ppermute | solution.py:31
  17.7 14.9 %collective-permute-start.1 = (bf16[128,2048]{1,0:T(8,128)(2,1)S(1)}, bf16[128,2048]{1,0:T(8,128)(2,1)S(1)}, u32[]{:S(2)}, u32[]{:S(2)}) collective-permute-start(bf16[128,2048]{1,0:T(8,128)(2,1)S(1)} %collective-permute-done.refs_1_), channel_id=1, source_target_pairs={{0,4},{1,29},{4,8},{5,1},{8,12},{9,5},{12,16},{13,9},{16,20},{17,1... | collective-permute-start | bytes 1572872 | tf_op jit(solution)/shard_map/ppermute | solution.py:31
  18.1 14.5 %collective-permute-start.4 = (bf16[128,2048]{1,0:T(8,128)(2,1)S(1)}, bf16[128,2048]{1,0:T(8,128)(2,1)S(1)}, u32[]{:S(2)}, u32[]{:S(2)}) collective-permute-start(bf16[128,2048]{1,0:T(8,128)(2,1)S(1)} %collective-permute-done.3.refs_2_), channel_id=1, source_target_pairs={{0,28},{1,5},{4,0},{5,9},{8,4},{9,13},{12,8},{13,17},{16,12},{17,2... | collective-permute-start | bytes 1572872 | tf_op jit(solution)/shard_map/ppermute | solution.py:31
  22.6 13.2 %collective-permute-start.11 = (bf16[128,2176]{1,0:T(8,128)(2,1)S(1)}, bf16[128,2176]{1,0:T(8,128)(2,1)S(1)}, u32[]{:S(2)}, u32[]{:S(2)}) collective-permute-start(bf16[128,2176]{1,0:T(8,128)(2,1)S(1)} %collective-permute-done.10.refs_7_.refs_4_.refs_9_), channel_id=1, source_target_pairs={{0,32},{1,97},{32,64},{33,1},{64,96},{65,33},{96,0},{97,65},{2,34}... | collective-permute-start | bytes 1671176 | tf_op jit(solution)/shard_map/ppermute | solution.py:31
  25.3 12.9 %collective-permute-start.12 = (bf16[128,2176]{1,0:T(8,128)(2,1)S(1)}, bf16[128,2176]{1,0:T(8,128)(2,1)S(1)}, u32[]{:S(2)}, u32[]{:S(2)}) collective-permute-start(bf16[128,2176]{1,0:T(8,128)(2,1)S(1)} %collective-permute-done.8.refs_5_.refs_2_.refs_7_), channel_id=1, source_target_pairs={{0,128},{128,0},{1,129},{129,1},{2,130},{130,2},{3,131},{131,3},{4... | collective-permute-start | bytes 1671176 | tf_op jit(solution)/shard_map/ppermute | solution.py:35
  26.0 13.3 %collective-permute-start.9 = (bf16[128,2176]{1,0:T(8,128)(2,1)S(1)}, bf16[128,2176]{1,0:T(8,128)(2,1)S(1)}, u32[]{:S(2)}, u32[]{:S(2)}) collective-permute-start(bf16[128,2176]{1,0:T(8,128)(2,1)S(1)} %collective-permute-done.7.refs_4_.refs_1_.refs_6_), channel_id=1, source_target_pairs={{0,32},{1,97},{32,64},{33,1},{64,96},{65,33},{96,0},{97,65},{2,34}... | collective-permute-start | bytes 1671176 | tf_op jit(solution)/shard_map/ppermute | solution.py:31
  32.6 15.6 %collective-permute-start.2 = (bf16[128,2048]{1,0:T(8,128)(2,1)S(1)}, bf16[128,2048]{1,0:T(8,128)(2,1)S(1)}, u32[]{:S(2)}, u32[]{:S(2)}) collective-permute-start(bf16[128,2048]{1,0:T(8,128)(2,1)S(1)} %collective-permute-done.1.refs_3_), channel_id=1, source_target_pairs={{0,4},{1,29},{4,8},{5,1},{8,12},{9,5},{12,16},{13,9},{16,20},{17,1... | collective-permute-start | bytes 1572872 | tf_op jit(solution)/shard_map/ppermute | solution.py:31
  32.6 15.6 %collective-permute-start.5 = (bf16[128,2048]{1,0:T(8,128)(2,1)S(1)}, bf16[128,2048]{1,0:T(8,128)(2,1)S(1)}, u32[]{:S(2)}, u32[]{:S(2)}) collective-permute-start(bf16[128,2048]{1,0:T(8,128)(2,1)S(1)} %collective-permute-done.4.refs_4_), channel_id=1, source_target_pairs={{0,28},{1,5},{4,0},{5,9},{8,4},{9,13},{12,8},{13,17},{16,12},{17,2... | collective-permute-start | bytes 1572872 | tf_op jit(solution)/shard_map/ppermute | solution.py:31
  39.3 10.7 %collective-permute-start.13 = (bf16[128,2176]{1,0:T(8,128)(2,1)S(1)}, bf16[128,2176]{1,0:T(8,128)(2,1)S(1)}, u32[]{:S(2)}, u32[]{:S(2)}) collective-permute-start(bf16[128,2176]{1,0:T(8,128)(2,1)S(1)} %collective-permute-done.11.refs_8_.refs_5_.refs_10_), channel_id=1, source_target_pairs={{0,32},{1,97},{32,64},{33,1},{64,96},{65,33},{96,0},{97,65},{2,34}... | collective-permute-start | bytes 1671176 | tf_op jit(solution)/shard_map/ppermute | solution.py:31
  48.1 10.4 %collective-permute-start.6 = (bf16[128,2048]{1,0:T(8,128)(2,1)S(1)}, bf16[128,2048]{1,0:T(8,128)(2,1)S(1)}, u32[]{:S(2)}, u32[]{:S(2)}) collective-permute-start(bf16[128,2048]{1,0:T(8,128)(2,1)S(1)} %collective-permute-done.2.refs_0_), channel_id=1, source_target_pairs={{0,4},{1,29},{4,8},{5,1},{8,12},{9,5},{12,16},{13,9},{16,20},{17,1... | collective-permute-start | bytes 1572872 | tf_op jit(solution)/shard_map/ppermute | solution.py:31
  51.9 3.1 %collective-permute-start.21 = (f32[160,512]{1,0:T(8,128)S(1)}, f32[160,512]{1,0:T(8,128)S(1)}, u32[]{:S(2)}, u32[]{:S(2)}) collective-permute-start(f32[160,512]{1,0:T(8,128)S(1)} %get-tuple-element.35), channel_id=1, source_target_pairs={{0,1},{1,0},{2,3},{3,2},{4,5},{5,4},{6,7},{7,6},{8,9},{9,8},{10,11... | collective-permute-start | bytes 983048 | tf_op jit(solution)/shard_map/ppermute | solution.py:35
  56.0 11.5 %collective-permute-start.25 = (bf16[656,256]{1,0:T(8,128)(2,1)S(1)}, bf16[656,256]{1,0:T(8,128)(2,1)S(1)}, u32[]{:S(2)}, u32[]{:S(2)}) collective-permute-start(bf16[656,256]{1,0:T(8,128)(2,1)S(1)} %get-tuple-element.40), channel_id=1, source_target_pairs={{0,2},{2,0},{1,3},{3,1},{4,6},{6,4},{5,7},{7,5},{8,10},{10,8},{9,1... | collective-permute-start | bytes 1007624 | tf_op jit(solution)/shard_map/ppermute | solution.py:35
  62.9 12.0 %collective-permute-start.17 = (bf16[400,256]{1,0:T(8,128)(2,1)S(1)}, bf16[400,256]{1,0:T(8,128)(2,1)S(1)}, u32[]{:S(2)}, u32[]{:S(2)}) collective-permute-start(bf16[400,256]{1,0:T(8,128)(2,1)S(1)} %get-tuple-element.31), channel_id=1, source_target_pairs={{0,2},{2,0},{1,3},{3,1},{4,6},{6,4},{5,7},{7,5},{8,10},{10,8},{9,1... | collective-permute-start | bytes 614408 | tf_op jit(solution)/shard_map/ppermute | solution.py:35
  68.2 10.0 %collective-permute-start.26 = (bf16[144,256]{1,0:T(8,128)(2,1)S(1)}, bf16[144,256]{1,0:T(8,128)(2,1)S(1)}, u32[]{:S(2)}, u32[]{:S(2)}) collective-permute-start(bf16[144,256]{1,0:T(8,128)(2,1)S(1)} %get-tuple-element.42), channel_id=1, source_target_pairs={{0,28},{1,5},{4,0},{5,9},{8,4},{9,13},{12,8},{13,17},{16,12},{17,2... | collective-permute-start | bytes 221192 | tf_op jit(solution)/shard_map/ppermute | solution.py:31
  72.0 7.3 %collective-permute-start.27 = (bf16[144,256]{1,0:T(8,128)(2,1)S(1)}, bf16[144,256]{1,0:T(8,128)(2,1)S(1)}, u32[]{:S(2)}, u32[]{:S(2)}) collective-permute-start(bf16[144,256]{1,0:T(8,128)(2,1)S(1)} %get-tuple-element.43), channel_id=1, source_target_pairs={{0,4},{1,29},{4,8},{5,1},{8,12},{9,5},{12,16},{13,9},{16,20},{17,1... | collective-permute-start | bytes 221192 | tf_op jit(solution)/shard_map/ppermute | solution.py:31
  72.0 11.3 %collective-permute-start.28 = (bf16[144,256]{1,0:T(8,128)(2,1)S(1)}, bf16[144,256]{1,0:T(8,128)(2,1)S(1)}, u32[]{:S(2)}, u32[]{:S(2)}) collective-permute-start(bf16[144,256]{1,0:T(8,128)(2,1)S(1)} %get-tuple-element.44), channel_id=1, source_target_pairs={{0,24},{1,9},{4,28},{5,13},{8,0},{9,17},{12,4},{13,21},{16,8},{17,... | collective-permute-start | bytes 221192 | tf_op jit(solution)/shard_map/ppermute | solution.py:31
  73.5 9.8 %collective-permute-start.29 = (bf16[144,256]{1,0:T(8,128)(2,1)S(1)}, bf16[144,256]{1,0:T(8,128)(2,1)S(1)}, u32[]{:S(2)}, u32[]{:S(2)}) collective-permute-start(bf16[144,256]{1,0:T(8,128)(2,1)S(1)} %get-tuple-element.45), channel_id=1, source_target_pairs={{0,8},{1,25},{4,12},{5,29},{8,16},{9,1},{12,20},{13,5},{16,24},{17... | collective-permute-start | bytes 221192 | tf_op jit(solution)/shard_map/ppermute | solution.py:31
  75.4 9.7 %collective-permute-start.18 = (bf16[144,256]{1,0:T(8,128)(2,1)S(1)}, bf16[144,256]{1,0:T(8,128)(2,1)S(1)}, u32[]{:S(2)}, u32[]{:S(2)}) collective-permute-start(bf16[144,256]{1,0:T(8,128)(2,1)S(1)} %get-tuple-element.32), channel_id=1, source_target_pairs={{0,20},{1,13},{4,24},{5,17},{8,28},{9,21},{12,0},{13,25},{16,4},{1... | collective-permute-start | bytes 221192 | tf_op jit(solution)/shard_map/ppermute | solution.py:31
  78.2 10.5 %collective-permute-start.19 = (bf16[144,256]{1,0:T(8,128)(2,1)S(1)}, bf16[144,256]{1,0:T(8,128)(2,1)S(1)}, u32[]{:S(2)}, u32[]{:S(2)}) collective-permute-start(bf16[144,256]{1,0:T(8,128)(2,1)S(1)} %get-tuple-element.33), channel_id=1, source_target_pairs={{0,12},{1,21},{4,16},{5,25},{8,20},{9,29},{12,24},{13,1},{16,28},{... | collective-permute-start | bytes 221192 | tf_op jit(solution)/shard_map/ppermute | solution.py:31
  79.3 10.0 %collective-permute-start.20 = (bf16[144,256]{1,0:T(8,128)(2,1)S(1)}, bf16[144,256]{1,0:T(8,128)(2,1)S(1)}, u32[]{:S(2)}, u32[]{:S(2)}) collective-permute-start(bf16[144,256]{1,0:T(8,128)(2,1)S(1)} %get-tuple-element.34), channel_id=1, source_target_pairs={{0,16},{1,17},{4,20},{5,21},{8,24},{9,25},{12,28},{13,29},{16,0},{... | collective-permute-start | bytes 221192 | tf_op jit(solution)/shard_map/ppermute | solution.py:31
  (9 other events, 58.1 us)

commit v6 on v5

--- a/solution.py
+++ b/solution.py
@@ -268,7 +268,7 @@
                 copy.start()
                 copies.append(copy)
         if last:
-            turned = pltpu.roll(jnp.broadcast_to(sum_of, (8, 256)), 256 - 32 * lax.axis_index("z"), 1)
+            turned = pltpu.roll(jnp.broadcast_to(sum_of, (8, 256)), lax.rem(256 - 32 * lax.axis_index("z"), 256), 1)
             result[...] = turned[:1, :32]
         else:
             result[...] = jnp.broadcast_to(sum_of, (8, 256))

time: 91.1 us -> 91.1 us (level)
  no operation moved by 1% of the time
where the time goes in v6:
time: 91.1 us; the launch traced here: 90.9 us
  starting transfers between devices  39.2 us (43%)
  waiting for transfers between devices  37.3 us (41%)
  Pallas kernels  11.8 us (13%)
  local copies, waits for them, and re-layouts  1.73 us (2%)
  between operations  0.98 us (1%)
    ppermute x19, starting transfers between devices, shift(): return lax.ppermute(value, (axis, 'core'), pairs)  33.5 us
    ppermute x19, waiting for transfers between devices, shift(): return lax.ppermute(value, (axis, 'core'), pairs)  30.3 us
    ppermute x11, waiting for transfers between devices, swap(): return lax.ppermute(value, axis, [(0, 1), (1, 0)])  6.97 us
    pallas_call x4, Pallas kernels, products(): pl.pallas_call(kernel, out_shape=[jax.ShapeDtypeStruct((count, 512), F32)...  6.15 us
    ppermute x11, starting transfers between devices, swap(): return lax.ppermute(value, axis, [(0, 1), (1, 0)])  5.67 us
    pallas_call x2, Pallas kernels, place(): pl.pallas_call(kernel, out_shape=(jax.ShapeDtypeStruct((ROWS, PANEL), F32...  2.48 us
  transfers between devices with their start and end apart: 30, of which 15 were waited for; matrix products, arithmetic and copies ran while one was open for 0% of the time, Pallas kernels for 11%

profile of v6, /device:TPU:16, one launch (start us, length us, event | category | flops | bytes accessed | tf_op | source)
XLA Modules:
  0.0 90.9 jit_solution(4406784260764999710)
XLA Ops:
  0.6 2.0 %collective-permute-start = (bf16[128,2048]{1,0:T(8,128)(2,1)}, bf16[128,2048]{1,0:T(8,128)(2,1)S(1)}, u32[]{:S(2)}, u32[]{:S(2)}) collective-permute-start(bf16[128,2048]{1,0:T(8,128)(2,1)} %refs_0_.3), channel_id=1, source_target_pairs={{0,4},{1,29},{4,8},{5,1},{8,12},{9,5},{12,16},{13,9},{16,20},{17,1... | collective-permute-start | bytes 1572872 | tf_op jit(solution)/shard_map/ppermute | solution.py:31
  2.6 4.0 %collective-permute-start.3 = (bf16[128,2048]{1,0:T(8,128)(2,1)}, bf16[128,2048]{1,0:T(8,128)(2,1)S(1)}, u32[]{:S(2)}, u32[]{:S(2)}) collective-permute-start(bf16[128,2048]{1,0:T(8,128)(2,1)} %refs_0_.3), channel_id=1, source_target_pairs={{0,28},{1,5},{4,0},{5,9},{8,4},{9,13},{12,8},{13,17},{16,12},{17,2... | collective-permute-start | bytes 1572872 | tf_op jit(solution)/shard_map/ppermute | solution.py:31
  8.5 1.4 %collective-permute-start.10 = (bf16[128,2176]{1,0:T(8,128)(2,1)S(1)}, bf16[128,2176]{1,0:T(8,128)(2,1)S(1)}, u32[]{:S(2)}, u32[]{:S(2)}) collective-permute-start(bf16[128,2176]{1,0:T(8,128)(2,1)S(1)} %shard_map.41.refs_3_.refs_0_.refs_5_), channel_id=1, source_target_pairs={{0,128},{128,0},{1,129},{129,1},{2,130},{130,2},{3,131},{131,3},{4... | collective-permute-start | bytes 1671176 | tf_op jit(solution)/shard_map/ppermute | solution.py:35
  9.9 2.8 %collective-permute-start.8 = (bf16[128,2176]{1,0:T(8,128)(2,1)S(1)}, bf16[128,2176]{1,0:T(8,128)(2,1)S(1)}, u32[]{:S(2)}, u32[]{:S(2)}) collective-permute-start(bf16[128,2176]{1,0:T(8,128)(2,1)S(1)} %shard_map.41.refs_3_.refs_0_.refs_5_), channel_id=1, source_target_pairs={{0,96},{1,33},{32,0},{33,65},{64,32},{65,97},{96,64},{97,1},{2,98}... | collective-permute-start | bytes 1671176 | tf_op jit(solution)/shard_map/ppermute | solution.py:31
  12.6 5.0 %collective-permute-done.refs_1_ = bf16[128,2048]{1,0:T(8,128)(2,1)S(1)} collective-permute-done((bf16[128,2048]{1,0:T(8,128)(2,1)}, bf16[128,2048]{1,0:T(8,128)(2,1)S(1)}, u32[]{:S(2)}, u32[]{:S(2)}) %collective-permute-start) | collective-permute-done | bytes 524320 | tf_op jit(solution)/shard_map/ppermute | solution.py:31
  18.1 3.6 %collective-permute-start.4 = (bf16[128,2048]{1,0:T(8,128)(2,1)S(1)}, bf16[128,2048]{1,0:T(8,128)(2,1)S(1)}, u32[]{:S(2)}, u32[]{:S(2)}) collective-permute-start(bf16[128,2048]{1,0:T(8,128)(2,1)S(1)} %collective-permute-done.3.refs_2_), channel_id=1, source_target_pairs={{0,28},{1,5},{4,0},{5,9},{8,4},{9,13},{12,8},{13,17},{16,12},{17,2... | collective-permute-start | bytes 1572872 | tf_op jit(solution)/shard_map/ppermute | solution.py:31
  22.6 1.5 %collective-permute-start.11 = (bf16[128,2176]{1,0:T(8,128)(2,1)S(1)}, bf16[128,2176]{1,0:T(8,128)(2,1)S(1)}, u32[]{:S(2)}, u32[]{:S(2)}) collective-permute-start(bf16[128,2176]{1,0:T(8,128)(2,1)S(1)} %collective-permute-done.10.refs_7_.refs_4_.refs_9_), channel_id=1, source_target_pairs={{0,32},{1,97},{32,64},{33,1},{64,96},{65,33},{96,0},{97,65},{2,34}... | collective-permute-start | bytes 1671176 | tf_op jit(solution)/shard_map/ppermute | solution.py:31
  26.0 1.5 %collective-permute-start.9 = (bf16[128,2176]{1,0:T(8,128)(2,1)S(1)}, bf16[128,2176]{1,0:T(8,128)(2,1)S(1)}, u32[]{:S(2)}, u32[]{:S(2)}) collective-permute-start(bf16[128,2176]{1,0:T(8,128)(2,1)S(1)} %collective-permute-done.7.refs_4_.refs_1_.refs_6_), channel_id=1, source_target_pairs={{0,32},{1,97},{32,64},{33,1},{64,96},{65,33},{96,0},{97,65},{2,34}... | collective-permute-start | bytes 1671176 | tf_op jit(solution)/shard_map/ppermute | solution.py:31
  27.5 5.0 %collective-permute-done.1.refs_3_ = bf16[128,2048]{1,0:T(8,128)(2,1)S(1)} collective-permute-done((bf16[128,2048]{1,0:T(8,128)(2,1)S(1)}, bf16[128,2048]{1,0:T(8,128)(2,1)S(1)}, u32[]{:S(2)}, u32[]{:S(2)}) %collective-permute-start.1) | collective-permute-done | bytes 524320 | tf_op jit(solution)/shard_map/ppermute | solution.py:31
  32.6 3.2 %collective-permute-start.5 = (bf16[128,2048]{1,0:T(8,128)(2,1)S(1)}, bf16[128,2048]{1,0:T(8,128)(2,1)S(1)}, u32[]{:S(2)}, u32[]{:S(2)}) collective-permute-start(bf16[128,2048]{1,0:T(8,128)(2,1)S(1)} %collective-permute-done.4.refs_4_), channel_id=1, source_target_pairs={{0,28},{1,5},{4,0},{5,9},{8,4},{9,13},{12,8},{13,17},{16,12},{17,2... | collective-permute-start | bytes 1572872 | tf_op jit(solution)/shard_map/ppermute | solution.py:31
  35.8 2.4 %collective-permute-done.12.refs_9_.refs_6_.refs_11_ = bf16[128,2176]{1,0:T(8,128)(2,1)S(1)} collective-permute-done((bf16[128,2176]{1,0:T(8,128)(2,1)S(1)}, bf16[128,2176]{1,0:T(8,128)(2,1)S(1)}, u32[]{:S(2)}, u32[]{:S(2)}) %collective-permute-start.12) | collective-permute-done | bytes 557088 | tf_op jit(solution)/shard_map/ppermute | solution.py:35
  39.6 8.5 %collective-permute-done.2.refs_0_ = bf16[128,2048]{1,0:T(8,128)(2,1)S(1)} collective-permute-done((bf16[128,2048]{1,0:T(8,128)(2,1)S(1)}, bf16[128,2048]{1,0:T(8,128)(2,1)S(1)}, u32[]{:S(2)}, u32[]{:S(2)}) %collective-permute-start.2) | collective-permute-done | bytes 524320 | tf_op jit(solution)/shard_map/ppermute | solution.py:31
  48.1 1.9 %collective-permute-done.13.refs_10_.refs_7_.refs_12_ = bf16[128,2176]{1,0:T(8,128)(2,1)S(1)} collective-permute-done((bf16[128,2176]{1,0:T(8,128)(2,1)S(1)}, bf16[128,2176]{1,0:T(8,128)(2,1)S(1)}, u32[]{:S(2)}, u32[]{:S(2)}) %collective-permute-start.13) | collective-permute-done | bytes 557088 | tf_op jit(solution)/shard_map/ppermute | solution.py:31
  50.1 1.8 %shard_map.48 = (f32[160,512]{1,0:T(8,128)S(1)}, f32[160,512]{1,0:T(8,128)S(1)}, f32[160,512]{1,0:T(8,128)S(1)}, f32[160,512]{1,0:T(8,128)S(1)}) custom-call(bf16[128,2048]{1,0:T(8,128)(2,1)S(1)} %copy-done.1, bf16[128,2048]{1,0:T(8,128)(2,1)S(1)} %collective-permute-done.refs_1_, bf16[128,2048]{1,0:T(8,128)(2,1)S(1)} %collective-permute-done.3.refs_2_, ...), custom_call_target="tpu_custom_call" | custom-call | tf_op jit(solution)/shard_map/pallas_call | solution.py:116
  53.2 1.8 %shard_map.47.a = f32[640,512]{1,0:T(8,128)S(1)} custom-call(bf16[128,2048]{1,0:T(8,128)(2,1)S(1)} %copy-done.1, bf16[128,2048]{1,0:T(8,128)(2,1)S(1)} %collective-permute-done.refs_1_, bf16[128,2048]{1,0:T(8,128)(2,1)S(1)} %collective-permute-done.3.refs_2_, bf16[128,2048]{1,0:T(8,128)(2,1)S(1)} %collective-permute-done.1.refs_3_, ...), custom_call_target="tpu_custom_call" | custom-call | tf_op jit(solution)/shard_map/pallas_call | solution.py:116
  56.4 2.1 %collective-permute-done.6.refs_2_ = bf16[128,2048]{1,0:T(8,128)(2,1)S(1)} collective-permute-done((bf16[128,2048]{1,0:T(8,128)(2,1)S(1)}, bf16[128,2048]{1,0:T(8,128)(2,1)S(1)}, u32[]{:S(2)}, u32[]{:S(2)}) %collective-permute-start.6) | collective-permute-done | bytes 524320 | tf_op jit(solution)/shard_map/ppermute | solution.py:31
  64.1 3.4 %collective-permute-done.25.code = bf16[656,256]{1,0:T(8,128)(2,1)S(1)} collective-permute-done((bf16[656,256]{1,0:T(8,128)(2,1)S(1)}, bf16[656,256]{1,0:T(8,128)(2,1)S(1)}, u32[]{:S(2)}, u32[]{:S(2)}) %collective-permute-start.25) | collective-permute-done | bytes 335904 | tf_op jit(solution)/shard_map/ppermute | solution.py:35
  68.2 3.8 %collective-permute-start.26 = (bf16[144,256]{1,0:T(8,128)(2,1)S(1)}, bf16[144,256]{1,0:T(8,128)(2,1)S(1)}, u32[]{:S(2)}, u32[]{:S(2)}) collective-permute-start(bf16[144,256]{1,0:T(8,128)(2,1)S(1)} %get-tuple-element.42), channel_id=1, source_target_pairs={{0,28},{1,5},{4,0},{5,9},{8,4},{9,13},{12,8},{13,17},{16,12},{17,2... | collective-permute-start | bytes 221192 | tf_op jit(solution)/shard_map/ppermute | solution.py:31
  72.0 1.6 %collective-permute-start.28 = (bf16[144,256]{1,0:T(8,128)(2,1)S(1)}, bf16[144,256]{1,0:T(8,128)(2,1)S(1)}, u32[]{:S(2)}, u32[]{:S(2)}) collective-permute-start(bf16[144,256]{1,0:T(8,128)(2,1)S(1)} %get-tuple-element.44), channel_id=1, source_target_pairs={{0,24},{1,9},{4,28},{5,13},{8,0},{9,17},{12,4},{13,21},{16,8},{17,... | collective-permute-start | bytes 221192 | tf_op jit(solution)/shard_map/ppermute | solution.py:31
  73.5 1.4 %collective-permute-start.29 = (bf16[144,256]{1,0:T(8,128)(2,1)S(1)}, bf16[144,256]{1,0:T(8,128)(2,1)S(1)}, u32[]{:S(2)}, u32[]{:S(2)}) collective-permute-start(bf16[144,256]{1,0:T(8,128)(2,1)S(1)} %get-tuple-element.45), channel_id=1, source_target_pairs={{0,8},{1,25},{4,12},{5,29},{8,16},{9,1},{12,20},{13,5},{16,24},{17... | collective-permute-start | bytes 221192 | tf_op jit(solution)/shard_map/ppermute | solution.py:31
  75.4 2.8 %collective-permute-start.18 = (bf16[144,256]{1,0:T(8,128)(2,1)S(1)}, bf16[144,256]{1,0:T(8,128)(2,1)S(1)}, u32[]{:S(2)}, u32[]{:S(2)}) collective-permute-start(bf16[144,256]{1,0:T(8,128)(2,1)S(1)} %get-tuple-element.32), channel_id=1, source_target_pairs={{0,20},{1,13},{4,24},{5,17},{8,28},{9,21},{12,0},{13,25},{16,4},{1... | collective-permute-start | bytes 221192 | tf_op jit(solution)/shard_map/ppermute | solution.py:31
  79.3 4.0 %collective-permute-start.20 = (bf16[144,256]{1,0:T(8,128)(2,1)S(1)}, bf16[144,256]{1,0:T(8,128)(2,1)S(1)}, u32[]{:S(2)}, u32[]{:S(2)}) collective-permute-start(bf16[144,256]{1,0:T(8,128)(2,1)S(1)} %get-tuple-element.34), channel_id=1, source_target_pairs={{0,16},{1,17},{4,20},{5,21},{8,24},{9,25},{12,28},{13,29},{16,0},{... | collective-permute-start | bytes 221192 | tf_op jit(solution)/shard_map/ppermute | solution.py:31
  85.2 3.5 %collective-permute-done.19.refs_1_ = bf16[144,256]{1,0:T(8,128)(2,1)S(1)} collective-permute-done((bf16[144,256]{1,0:T(8,128)(2,1)S(1)}, bf16[144,256]{1,0:T(8,128)(2,1)S(1)}, u32[]{:S(2)}, u32[]{:S(2)}) %collective-permute-start.19) | collective-permute-done | bytes 73760 | tf_op jit(solution)/shard_map/ppermute | solution.py:31
  89.3 1.4 %shard_map.52 = (f32[128,2048]{1,0:T(8,128)}, f32[1,32]{1,0:T(1,128)}) custom-call(bf16[144,256]{1,0:T(8,128)(2,1)S(1)} %collective-permute-done.18.refs_0_, bf16[144,256]{1,0:T(8,128)(2,1)S(1)} %collective-permute-done.19.refs_1_, bf16[144,256]{1,0:T(8,128)(2,1)S(1)} %collective-permute-done.20.refs_2_, ...), custom_call_target="tpu_custom_call", output_to_operand_aliasing={{0}: (4, {})} | custom-call | tf_op jit(solution)/shard_map/pallas_call | solution.py:278
  (54 shorter events, 19.6 us)
Async XLA Ops:
  0.6 17.0 %collective-permute-start = (bf16[128,2048]{1,0:T(8,128)(2,1)}, bf16[128,2048]{1,0:T(8,128)(2,1)S(1)}, u32[]{:S(2)}, u32[]{:S(2)}) collective-permute-start(bf16[128,2048]{1,0:T(8,128)(2,1)} %refs_0_.3), channel_id=1, source_target_pairs={{0,4},{1,29},{4,8},{5,1},{8,12},{9,5},{12,16},{13,9},{16,20},{17,1... | collective-permute-start | bytes 1572872 | tf_op jit(solution)/shard_map/ppermute | solution.py:31
  2.6 15.4 %collective-permute-start.3 = (bf16[128,2048]{1,0:T(8,128)(2,1)}, bf16[128,2048]{1,0:T(8,128)(2,1)S(1)}, u32[]{:S(2)}, u32[]{:S(2)}) collective-permute-start(bf16[128,2048]{1,0:T(8,128)(2,1)} %refs_0_.3), channel_id=1, source_target_pairs={{0,28},{1,5},{4,0},{5,9},{8,4},{9,13},{12,8},{13,17},{16,12},{17,2... | collective-permute-start | bytes 1572872 | tf_op jit(solution)/shard_map/ppermute | solution.py:31
  8.5 14.1 %collective-permute-start.10 = (bf16[128,2176]{1,0:T(8,128)(2,1)S(1)}, bf16[128,2176]{1,0:T(8,128)(2,1)S(1)}, u32[]{:S(2)}, u32[]{:S(2)}) collective-permute-start(bf16[128,2176]{1,0:T(8,128)(2,1)S(1)} %shard_map.41.refs_3_.refs_0_.refs_5_), channel_id=1, source_target_pairs={{0,128},{128,0},{1,129},{129,1},{2,130},{130,2},{3,131},{131,3},{4... | collective-permute-start | bytes 1671176 | tf_op jit(solution)/shard_map/ppermute | solution.py:35
  9.9 15.4 %collective-permute-start.8 = (bf16[128,2176]{1,0:T(8,128)(2,1)S(1)}, bf16[128,2176]{1,0:T(8,128)(2,1)S(1)}, u32[]{:S(2)}, u32[]{:S(2)}) collective-permute-start(bf16[128,2176]{1,0:T(8,128)(2,1)S(1)} %shard_map.41.refs_3_.refs_0_.refs_5_), channel_id=1, source_target_pairs={{0,96},{1,33},{32,0},{33,65},{64,32},{65,97},{96,64},{97,1},{2,98}... | collective-permute-start | bytes 1671176 | tf_op jit(solution)/shard_map/ppermute | solution.py:31
  12.6 13.4 %collective-permute-start.7 = (bf16[128,2176]{1,0:T(8,128)(2,1)S(1)}, bf16[128,2176]{1,0:T(8,128)(2,1)S(1)}, u32[]{:S(2)}, u32[]{:S(2)}) collective-permute-start(bf16[128,2176]{1,0:T(8,128)(2,1)S(1)} %shard_map.41.refs_3_.refs_0_.refs_5_), channel_id=1, source_target_pairs={{0,32},{1,97},{32,64},{33,1},{64,96},{65,33},{96,0},{97,65},{2,34}... | collective-permute-start | bytes 1671176 | tf_op jit(solution)/shard_map/ppermute | solution.py:31
  17.7 14.9 %collective-permute-start.1 = (bf16[128,2048]{1,0:T(8,128)(2,1)S(1)}, bf16[128,2048]{1,0:T(8,128)(2,1)S(1)}, u32[]{:S(2)}, u32[]{:S(2)}) collective-permute-start(bf16[128,2048]{1,0:T(8,128)(2,1)S(1)} %collective-permute-done.refs_1_), channel_id=1, source_target_pairs={{0,4},{1,29},{4,8},{5,1},{8,12},{9,5},{12,16},{13,9},{16,20},{17,1... | collective-permute-start | bytes 1572872 | tf_op jit(solution)/shard_map/ppermute | solution.py:31
  18.1 14.5 %collective-permute-start.4 = (bf16[128,2048]{1,0:T(8,128)(2,1)S(1)}, bf16[128,2048]{1,0:T(8,128)(2,1)S(1)}, u32[]{:S(2)}, u32[]{:S(2)}) collective-permute-start(bf16[128,2048]{1,0:T(8,128)(2,1)S(1)} %collective-permute-done.3.refs_2_), channel_id=1, source_target_pairs={{0,28},{1,5},{4,0},{5,9},{8,4},{9,13},{12,8},{13,17},{16,12},{17,2... | collective-permute-start | bytes 1572872 | tf_op jit(solution)/shard_map/ppermute | solution.py:31
  22.6 13.2 %collective-permute-start.11 = (bf16[128,2176]{1,0:T(8,128)(2,1)S(1)}, bf16[128,2176]{1,0:T(8,128)(2,1)S(1)}, u32[]{:S(2)}, u32[]{:S(2)}) collective-permute-start(bf16[128,2176]{1,0:T(8,128)(2,1)S(1)} %collective-permute-done.10.refs_7_.refs_4_.refs_9_), channel_id=1, source_target_pairs={{0,32},{1,97},{32,64},{33,1},{64,96},{65,33},{96,0},{97,65},{2,34}... | collective-permute-start | bytes 1671176 | tf_op jit(solution)/shard_map/ppermute | solution.py:31
  25.3 12.9 %collective-permute-start.12 = (bf16[128,2176]{1,0:T(8,128)(2,1)S(1)}, bf16[128,2176]{1,0:T(8,128)(2,1)S(1)}, u32[]{:S(2)}, u32[]{:S(2)}) collective-permute-start(bf16[128,2176]{1,0:T(8,128)(2,1)S(1)} %collective-permute-done.8.refs_5_.refs_2_.refs_7_), channel_id=1, source_target_pairs={{0,128},{128,0},{1,129},{129,1},{2,130},{130,2},{3,131},{131,3},{4... | collective-permute-start | bytes 1671176 | tf_op jit(solution)/shard_map/ppermute | solution.py:35
  26.0 13.3 %collective-permute-start.9 = (bf16[128,2176]{1,0:T(8,128)(2,1)S(1)}, bf16[128,2176]{1,0:T(8,128)(2,1)S(1)}, u32[]{:S(2)}, u32[]{:S(2)}) collective-permute-start(bf16[128,2176]{1,0:T(8,128)(2,1)S(1)} %collective-permute-done.7.refs_4_.refs_1_.refs_6_), channel_id=1, source_target_pairs={{0,32},{1,97},{32,64},{33,1},{64,96},{65,33},{96,0},{97,65},{2,34}... | collective-permute-start | bytes 1671176 | tf_op jit(solution)/shard_map/ppermute | solution.py:31
  32.6 15.6 %collective-permute-start.2 = (bf16[128,2048]{1,0:T(8,128)(2,1)S(1)}, bf16[128,2048]{1,0:T(8,128)(2,1)S(1)}, u32[]{:S(2)}, u32[]{:S(2)}) collective-permute-start(bf16[128,2048]{1,0:T(8,128)(2,1)S(1)} %collective-permute-done.1.refs_3_), channel_id=1, source_target_pairs={{0,4},{1,29},{4,8},{5,1},{8,12},{9,5},{12,16},{13,9},{16,20},{17,1... | collective-permute-start | bytes 1572872 | tf_op jit(solution)/shard_map/ppermute | solution.py:31
  32.6 15.6 %collective-permute-start.5 = (bf16[128,2048]{1,0:T(8,128)(2,1)S(1)}, bf16[128,2048]{1,0:T(8,128)(2,1)S(1)}, u32[]{:S(2)}, u32[]{:S(2)}) collective-permute-start(bf16[128,2048]{1,0:T(8,128)(2,1)S(1)} %collective-permute-done.4.refs_4_), channel_id=1, source_target_pairs={{0,28},{1,5},{4,0},{5,9},{8,4},{9,13},{12,8},{13,17},{16,12},{17,2... | collective-permute-start | bytes 1572872 | tf_op jit(solution)/shard_map/ppermute | solution.py:31
  39.3 10.7 %collective-permute-start.13 = (bf16[128,2176]{1,0:T(8,128)(2,1)S(1)}, bf16[128,2176]{1,0:T(8,128)(2,1)S(1)}, u32[]{:S(2)}, u32[]{:S(2)}) collective-permute-start(bf16[128,2176]{1,0:T(8,128)(2,1)S(1)} %collective-permute-done.11.refs_8_.refs_5_.refs_10_), channel_id=1, source_target_pairs={{0,32},{1,97},{32,64},{33,1},{64,96},{65,33},{96,0},{97,65},{2,34}... | collective-permute-start | bytes 1671176 | tf_op jit(solution)/shard_map/ppermute | solution.py:31
  48.1 10.4 %collective-permute-start.6 = (bf16[128,2048]{1,0:T(8,128)(2,1)S(1)}, bf16[128,2048]{1,0:T(8,128)(2,1)S(1)}, u32[]{:S(2)}, u32[]{:S(2)}) collective-permute-start(bf16[128,2048]{1,0:T(8,128)(2,1)S(1)} %collective-permute-done.2.refs_0_), channel_id=1, source_target_pairs={{0,4},{1,29},{4,8},{5,1},{8,12},{9,5},{12,16},{13,9},{16,20},{17,1... | collective-permute-start | bytes 1572872 | tf_op jit(solution)/shard_map/ppermute | solution.py:31
  51.9 3.1 %collective-permute-start.21 = (f32[160,512]{1,0:T(8,128)S(1)}, f32[160,512]{1,0:T(8,128)S(1)}, u32[]{:S(2)}, u32[]{:S(2)}) collective-permute-start(f32[160,512]{1,0:T(8,128)S(1)} %get-tuple-element.35), channel_id=1, source_target_pairs={{0,1},{1,0},{2,3},{3,2},{4,5},{5,4},{6,7},{7,6},{8,9},{9,8},{10,11... | collective-permute-start | bytes 983048 | tf_op jit(solution)/shard_map/ppermute | solution.py:35
  56.0 11.5 %collective-permute-start.25 = (bf16[656,256]{1,0:T(8,128)(2,1)S(1)}, bf16[656,256]{1,0:T(8,128)(2,1)S(1)}, u32[]{:S(2)}, u32[]{:S(2)}) collective-permute-start(bf16[656,256]{1,0:T(8,128)(2,1)S(1)} %get-tuple-element.40), channel_id=1, source_target_pairs={{0,2},{2,0},{1,3},{3,1},{4,6},{6,4},{5,7},{7,5},{8,10},{10,8},{9,1... | collective-permute-start | bytes 1007624 | tf_op jit(solution)/shard_map/ppermute | solution.py:35
  62.9 12.0 %collective-permute-start.17 = (bf16[400,256]{1,0:T(8,128)(2,1)S(1)}, bf16[400,256]{1,0:T(8,128)(2,1)S(1)}, u32[]{:S(2)}, u32[]{:S(2)}) collective-permute-start(bf16[400,256]{1,0:T(8,128)(2,1)S(1)} %get-tuple-element.31), channel_id=1, source_target_pairs={{0,2},{2,0},{1,3},{3,1},{4,6},{6,4},{5,7},{7,5},{8,10},{10,8},{9,1... | collective-permute-start | bytes 614408 | tf_op jit(solution)/shard_map/ppermute | solution.py:35
  68.2 10.0 %collective-permute-start.26 = (bf16[144,256]{1,0:T(8,128)(2,1)S(1)}, bf16[144,256]{1,0:T(8,128)(2,1)S(1)}, u32[]{:S(2)}, u32[]{:S(2)}) collective-permute-start(bf16[144,256]{1,0:T(8,128)(2,1)S(1)} %get-tuple-element.42), channel_id=1, source_target_pairs={{0,28},{1,5},{4,0},{5,9},{8,4},{9,13},{12,8},{13,17},{16,12},{17,2... | collective-permute-start | bytes 221192 | tf_op jit(solution)/shard_map/ppermute | solution.py:31
  72.0 7.3 %collective-permute-start.27 = (bf16[144,256]{1,0:T(8,128)(2,1)S(1)}, bf16[144,256]{1,0:T(8,128)(2,1)S(1)}, u32[]{:S(2)}, u32[]{:S(2)}) collective-permute-start(bf16[144,256]{1,0:T(8,128)(2,1)S(1)} %get-tuple-element.43), channel_id=1, source_target_pairs={{0,4},{1,29},{4,8},{5,1},{8,12},{9,5},{12,16},{13,9},{16,20},{17,1... | collective-permute-start | bytes 221192 | tf_op jit(solution)/shard_map/ppermute | solution.py:31
  72.0 11.3 %collective-permute-start.28 = (bf16[144,256]{1,0:T(8,128)(2,1)S(1)}, bf16[144,256]{1,0:T(8,128)(2,1)S(1)}, u32[]{:S(2)}, u32[]{:S(2)}) collective-permute-start(bf16[144,256]{1,0:T(8,128)(2,1)S(1)} %get-tuple-element.44), channel_id=1, source_target_pairs={{0,24},{1,9},{4,28},{5,13},{8,0},{9,17},{12,4},{13,21},{16,8},{17,... | collective-permute-start | bytes 221192 | tf_op jit(solution)/shard_map/ppermute | solution.py:31
  73.5 9.8 %collective-permute-start.29 = (bf16[144,256]{1,0:T(8,128)(2,1)S(1)}, bf16[144,256]{1,0:T(8,128)(2,1)S(1)}, u32[]{:S(2)}, u32[]{:S(2)}) collective-permute-start(bf16[144,256]{1,0:T(8,128)(2,1)S(1)} %get-tuple-element.45), channel_id=1, source_target_pairs={{0,8},{1,25},{4,12},{5,29},{8,16},{9,1},{12,20},{13,5},{16,24},{17... | collective-permute-start | bytes 221192 | tf_op jit(solution)/shard_map/ppermute | solution.py:31
  75.4 9.7 %collective-permute-start.18 = (bf16[144,256]{1,0:T(8,128)(2,1)S(1)}, bf16[144,256]{1,0:T(8,128)(2,1)S(1)}, u32[]{:S(2)}, u32[]{:S(2)}) collective-permute-start(bf16[144,256]{1,0:T(8,128)(2,1)S(1)} %get-tuple-element.32), channel_id=1, source_target_pairs={{0,20},{1,13},{4,24},{5,17},{8,28},{9,21},{12,0},{13,25},{16,4},{1... | collective-permute-start | bytes 221192 | tf_op jit(solution)/shard_map/ppermute | solution.py:31
  78.2 10.5 %collective-permute-start.19 = (bf16[144,256]{1,0:T(8,128)(2,1)S(1)}, bf16[144,256]{1,0:T(8,128)(2,1)S(1)}, u32[]{:S(2)}, u32[]{:S(2)}) collective-permute-start(bf16[144,256]{1,0:T(8,128)(2,1)S(1)} %get-tuple-element.33), channel_id=1, source_target_pairs={{0,12},{1,21},{4,16},{5,25},{8,20},{9,29},{12,24},{13,1},{16,28},{... | collective-permute-start | bytes 221192 | tf_op jit(solution)/shard_map/ppermute | solution.py:31
  79.3 10.0 %collective-permute-start.20 = (bf16[144,256]{1,0:T(8,128)(2,1)S(1)}, bf16[144,256]{1,0:T(8,128)(2,1)S(1)}, u32[]{:S(2)}, u32[]{:S(2)}) collective-permute-start(bf16[144,256]{1,0:T(8,128)(2,1)S(1)} %get-tuple-element.34), channel_id=1, source_target_pairs={{0,16},{1,17},{4,20},{5,21},{8,24},{9,25},{12,28},{13,29},{16,0},{... | collective-permute-start | bytes 221192 | tf_op jit(solution)/shard_map/ppermute | solution.py:31
  (9 other events, 58.1 us)

commit v7 on v6

--- a/solution.py
+++ b/solution.py
@@ -63,8 +63,7 @@
 
 
 def pack(log_derivs, sample_vector):
-    def kernel(entries, vec, out):
-        out[:, :PANEL] = entries[...]
+    def kernel(vec, out):
         left = jnp.transpose(jnp.broadcast_to(vec[...], (ROWS, ROWS)))
         lane = lax.broadcasted_iota(jnp.int32, (ROWS, ROWS), 1)
         parts = jnp.zeros((ROWS, ROWS), F32)
@@ -72,16 +71,17 @@
             part = left.astype(jnp.bfloat16).astype(F32)
             left = left - part
             parts = jnp.where(lane == i, part, parts)
-        out[:, PANEL:] = parts.astype(jnp.bfloat16)
-
-    return pl.pallas_call(
-        kernel,
-        out_shape=jax.ShapeDtypeStruct((ROWS, PANEL + ROWS), jnp.bfloat16),
-        in_specs=[VMEM] * 2,
+        out[...] = parts.astype(jnp.bfloat16)
+
+    parts = pl.pallas_call(
+        kernel,
+        out_shape=jax.ShapeDtypeStruct((ROWS, ROWS), jnp.bfloat16),
+        in_specs=[VMEM],
         out_specs=VMEM,
         compiler_params=SMALL,
         cost_estimate=takes(0),
-    )(log_derivs, sample_vector[None])
+    )(sample_vector[None])
+    return jnp.concatenate([log_derivs, parts], axis=1)
 
 
 def products(scale, rows, columns, other, parts, cost):

time: 91.1 us -> 91.1 us (level)
  other arithmetic: 0 us -> 1.08 us
  local copies, waits for them, and re-layouts: 1.73 us -> 0.66 us
    concatenate x0 -> x1, other arithmetic: none -> 1.08 us  [pack(): return jnp.concatenate([log_derivs, parts], axis=1)]
    unnamed x6 -> x4, local copies, waits for them, and re-layouts: 1.73 us -> 0.66 us
  transfers between devices with their start and end apart: 30 -> 30, of which waited for: 15 -> 15; matrix products, arithmetic and copies ran while one was open for 0% -> 1% of each run, Pallas kernels for 11% -> 11%
where the time goes in v7:
time: 91.1 us; the launch traced here: 91 us
  starting transfers between devices  39.2 us (43%)
  waiting for transfers between devices  37.3 us (41%)
  Pallas kernels  11.8 us (13%)
  other arithmetic  1.08 us (1%)
  between operations  1 us (1%)
    ppermute x19, starting transfers between devices, shift(): return lax.ppermute(value, (axis, 'core'), pairs)  33.5 us
    ppermute x19, waiting for transfers between devices, shift(): return lax.ppermute(value, (axis, 'core'), pairs)  30.4 us
    ppermute x11, waiting for transfers between devices, swap(): return lax.ppermute(value, axis, [(0, 1), (1, 0)])  6.9 us
    pallas_call x4, Pallas kernels, products(): pl.pallas_call(kernel, out_shape=[jax.ShapeDtypeStruct((count, 512), F32)...  6.16 us
    ppermute x11, starting transfers between devices, swap(): return lax.ppermute(value, axis, [(0, 1), (1, 0)])  5.63 us
    pallas_call x2, Pallas kernels, place(): pl.pallas_call(kernel, out_shape=(jax.ShapeDtypeStruct((ROWS, PANEL), F32...  2.48 us
  transfers between devices with their start and end apart: 30, of which 15 were waited for; matrix products, arithmetic and copies ran while one was open for 1% of the time, Pallas kernels for 11%

profile of v7, /device:TPU:16, one launch (start us, length us, event | category | flops | bytes accessed | tf_op | source)
XLA Modules:
  0.0 91.0 jit_solution(15492210619134423346)
XLA Ops:
  0.6 2.0 %collective-permute-start = (bf16[128,2048]{1,0:T(8,128)(2,1)}, bf16[128,2048]{1,0:T(8,128)(2,1)S(1)}, u32[]{:S(2)}, u32[]{:S(2)}) collective-permute-start(bf16[128,2048]{1,0:T(8,128)(2,1)} %refs_0_.3), channel_id=1, source_target_pairs={{0,4},{1,29},{4,8},{5,1},{8,12},{9,5},{12,16},{13,9},{16,20},{17,1... | collective-permute-start | bytes 1572872 | tf_op jit(solution)/shard_map/ppermute | solution.py:31
  2.6 4.0 %collective-permute-start.3 = (bf16[128,2048]{1,0:T(8,128)(2,1)}, bf16[128,2048]{1,0:T(8,128)(2,1)S(1)}, u32[]{:S(2)}, u32[]{:S(2)}) collective-permute-start(bf16[128,2048]{1,0:T(8,128)(2,1)} %refs_0_.3), channel_id=1, source_target_pairs={{0,28},{1,5},{4,0},{5,9},{8,4},{9,13},{12,8},{13,17},{16,12},{17,2... | collective-permute-start | bytes 1572872 | tf_op jit(solution)/shard_map/ppermute | solution.py:31
  8.5 1.4 %collective-permute-start.10 = (bf16[128,2176]{1,0:T(8,128)(2,1)S(1)}, bf16[128,2176]{1,0:T(8,128)(2,1)S(1)}, u32[]{:S(2)}, u32[]{:S(2)}) collective-permute-start(bf16[128,2176]{1,0:T(8,128)(2,1)S(1)} %pad_maximum_fusion.refs_3_.refs_0_.refs_5_), channel_id=1, source_target_pairs={{0,128},{128,0},{1,129},{129,1},{2,130},{130,2},{3,131},{131,3},{4... | collective-permute-start | bytes 1671176 | tf_op jit(solution)/shard_map/ppermute | solution.py:35
  9.9 2.8 %collective-permute-start.8 = (bf16[128,2176]{1,0:T(8,128)(2,1)S(1)}, bf16[128,2176]{1,0:T(8,128)(2,1)S(1)}, u32[]{:S(2)}, u32[]{:S(2)}) collective-permute-start(bf16[128,2176]{1,0:T(8,128)(2,1)S(1)} %pad_maximum_fusion.refs_3_.refs_0_.refs_5_), channel_id=1, source_target_pairs={{0,96},{1,33},{32,0},{33,65},{64,32},{65,97},{96,64},{97,1},{2,98}... | collective-permute-start | bytes 1671176 | tf_op jit(solution)/shard_map/ppermute | solution.py:31
  12.7 5.0 %collective-permute-done.refs_1_ = bf16[128,2048]{1,0:T(8,128)(2,1)S(1)} collective-permute-done((bf16[128,2048]{1,0:T(8,128)(2,1)}, bf16[128,2048]{1,0:T(8,128)(2,1)S(1)}, u32[]{:S(2)}, u32[]{:S(2)}) %collective-permute-start) | collective-permute-done | bytes 524320 | tf_op jit(solution)/shard_map/ppermute | solution.py:31
  18.1 3.6 %collective-permute-start.4 = (bf16[128,2048]{1,0:T(8,128)(2,1)S(1)}, bf16[128,2048]{1,0:T(8,128)(2,1)S(1)}, u32[]{:S(2)}, u32[]{:S(2)}) collective-permute-start(bf16[128,2048]{1,0:T(8,128)(2,1)S(1)} %collective-permute-done.3.refs_2_), channel_id=1, source_target_pairs={{0,28},{1,5},{4,0},{5,9},{8,4},{9,13},{12,8},{13,17},{16,12},{17,2... | collective-permute-start | bytes 1572872 | tf_op jit(solution)/shard_map/ppermute | solution.py:31
  22.6 1.5 %collective-permute-start.11 = (bf16[128,2176]{1,0:T(8,128)(2,1)S(1)}, bf16[128,2176]{1,0:T(8,128)(2,1)S(1)}, u32[]{:S(2)}, u32[]{:S(2)}) collective-permute-start(bf16[128,2176]{1,0:T(8,128)(2,1)S(1)} %collective-permute-done.10.refs_7_.refs_4_.refs_9_), channel_id=1, source_target_pairs={{0,32},{1,97},{32,64},{33,1},{64,96},{65,33},{96,0},{97,65},{2,34}... | collective-permute-start | bytes 1671176 | tf_op jit(solution)/shard_map/ppermute | solution.py:31
  26.1 1.5 %collective-permute-start.9 = (bf16[128,2176]{1,0:T(8,128)(2,1)S(1)}, bf16[128,2176]{1,0:T(8,128)(2,1)S(1)}, u32[]{:S(2)}, u32[]{:S(2)}) collective-permute-start(bf16[128,2176]{1,0:T(8,128)(2,1)S(1)} %collective-permute-done.7.refs_4_.refs_1_.refs_6_), channel_id=1, source_target_pairs={{0,32},{1,97},{32,64},{33,1},{64,96},{65,33},{96,0},{97,65},{2,34}... | collective-permute-start | bytes 1671176 | tf_op jit(solution)/shard_map/ppermute | solution.py:31
  27.6 5.0 %collective-permute-done.1.refs_3_ = bf16[128,2048]{1,0:T(8,128)(2,1)S(1)} collective-permute-done((bf16[128,2048]{1,0:T(8,128)(2,1)S(1)}, bf16[128,2048]{1,0:T(8,128)(2,1)S(1)}, u32[]{:S(2)}, u32[]{:S(2)}) %collective-permute-start.1) | collective-permute-done | bytes 524320 | tf_op jit(solution)/shard_map/ppermute | solution.py:31
  32.6 3.2 %collective-permute-start.5 = (bf16[128,2048]{1,0:T(8,128)(2,1)S(1)}, bf16[128,2048]{1,0:T(8,128)(2,1)S(1)}, u32[]{:S(2)}, u32[]{:S(2)}) collective-permute-start(bf16[128,2048]{1,0:T(8,128)(2,1)S(1)} %collective-permute-done.4.refs_4_), channel_id=1, source_target_pairs={{0,28},{1,5},{4,0},{5,9},{8,4},{9,13},{12,8},{13,17},{16,12},{17,2... | collective-permute-start | bytes 1572872 | tf_op jit(solution)/shard_map/ppermute | solution.py:31
  35.8 2.3 %collective-permute-done.12.refs_9_.refs_6_.refs_11_ = bf16[128,2176]{1,0:T(8,128)(2,1)S(1)} collective-permute-done((bf16[128,2176]{1,0:T(8,128)(2,1)S(1)}, bf16[128,2176]{1,0:T(8,128)(2,1)S(1)}, u32[]{:S(2)}, u32[]{:S(2)}) %collective-permute-start.12) | collective-permute-done | bytes 557088 | tf_op jit(solution)/shard_map/ppermute | solution.py:35
  39.6 8.5 %collective-permute-done.2.refs_0_ = bf16[128,2048]{1,0:T(8,128)(2,1)S(1)} collective-permute-done((bf16[128,2048]{1,0:T(8,128)(2,1)S(1)}, bf16[128,2048]{1,0:T(8,128)(2,1)S(1)}, u32[]{:S(2)}, u32[]{:S(2)}) %collective-permute-start.2) | collective-permute-done | bytes 524320 | tf_op jit(solution)/shard_map/ppermute | solution.py:31
  48.1 1.9 %collective-permute-done.13.refs_10_.refs_7_.refs_12_ = bf16[128,2176]{1,0:T(8,128)(2,1)S(1)} collective-permute-done((bf16[128,2176]{1,0:T(8,128)(2,1)S(1)}, bf16[128,2176]{1,0:T(8,128)(2,1)S(1)}, u32[]{:S(2)}, u32[]{:S(2)}) %collective-permute-start.13) | collective-permute-done | bytes 557088 | tf_op jit(solution)/shard_map/ppermute | solution.py:31
  50.1 1.8 %shard_map.48 = (f32[160,512]{1,0:T(8,128)S(1)}, f32[160,512]{1,0:T(8,128)S(1)}, f32[160,512]{1,0:T(8,128)S(1)}, f32[160,512]{1,0:T(8,128)S(1)}) custom-call(bf16[128,2048]{1,0:T(8,128)(2,1)S(1)} %copy-done, bf16[128,2048]{1,0:T(8,128)(2,1)S(1)} %collective-permute-done.refs_1_, bf16[128,2048]{1,0:T(8,128)(2,1)S(1)} %collective-permute-done.3.refs_2_, ...), custom_call_target="tpu_custom_call" | custom-call | tf_op jit(solution)/shard_map/pallas_call | solution.py:116
  53.2 1.8 %shard_map.47.a = f32[640,512]{1,0:T(8,128)S(1)} custom-call(bf16[128,2048]{1,0:T(8,128)(2,1)S(1)} %copy-done, bf16[128,2048]{1,0:T(8,128)(2,1)S(1)} %collective-permute-done.refs_1_, bf16[128,2048]{1,0:T(8,128)(2,1)S(1)} %collective-permute-done.3.refs_2_, bf16[128,2048]{1,0:T(8,128)(2,1)S(1)} %collective-permute-done.1.refs_3_, ...), custom_call_target="tpu_custom_call" | custom-call | tf_op jit(solution)/shard_map/pallas_call | solution.py:116
  56.4 2.2 %collective-permute-done.6.refs_2_ = bf16[128,2048]{1,0:T(8,128)(2,1)S(1)} collective-permute-done((bf16[128,2048]{1,0:T(8,128)(2,1)S(1)}, bf16[128,2048]{1,0:T(8,128)(2,1)S(1)}, u32[]{:S(2)}, u32[]{:S(2)}) %collective-permute-start.6) | collective-permute-done | bytes 524320 | tf_op jit(solution)/shard_map/ppermute | solution.py:31
  64.1 3.4 %collective-permute-done.25.code = bf16[656,256]{1,0:T(8,128)(2,1)S(1)} collective-permute-done((bf16[656,256]{1,0:T(8,128)(2,1)S(1)}, bf16[656,256]{1,0:T(8,128)(2,1)S(1)}, u32[]{:S(2)}, u32[]{:S(2)}) %collective-permute-start.25) | collective-permute-done | bytes 335904 | tf_op jit(solution)/shard_map/ppermute | solution.py:35
  68.2 3.8 %collective-permute-start.26 = (bf16[144,256]{1,0:T(8,128)(2,1)S(1)}, bf16[144,256]{1,0:T(8,128)(2,1)S(1)}, u32[]{:S(2)}, u32[]{:S(2)}) collective-permute-start(bf16[144,256]{1,0:T(8,128)(2,1)S(1)} %get-tuple-element.42), channel_id=1, source_target_pairs={{0,28},{1,5},{4,0},{5,9},{8,4},{9,13},{12,8},{13,17},{16,12},{17,2... | collective-permute-start | bytes 221192 | tf_op jit(solution)/shard_map/ppermute | solution.py:31
  72.0 1.6 %collective-permute-start.28 = (bf16[144,256]{1,0:T(8,128)(2,1)S(1)}, bf16[144,256]{1,0:T(8,128)(2,1)S(1)}, u32[]{:S(2)}, u32[]{:S(2)}) collective-permute-start(bf16[144,256]{1,0:T(8,128)(2,1)S(1)} %get-tuple-element.44), channel_id=1, source_target_pairs={{0,24},{1,9},{4,28},{5,13},{8,0},{9,17},{12,4},{13,21},{16,8},{17,... | collective-permute-start | bytes 221192 | tf_op jit(solution)/shard_map/ppermute | solution.py:31
  73.6 1.4 %collective-permute-start.29 = (bf16[144,256]{1,0:T(8,128)(2,1)S(1)}, bf16[144,256]{1,0:T(8,128)(2,1)S(1)}, u32[]{:S(2)}, u32[]{:S(2)}) collective-permute-start(bf16[144,256]{1,0:T(8,128)(2,1)S(1)} %get-tuple-element.45), channel_id=1, source_target_pairs={{0,8},{1,25},{4,12},{5,29},{8,16},{9,1},{12,20},{13,5},{16,24},{17... | collective-permute-start | bytes 221192 | tf_op jit(solution)/shard_map/ppermute | solution.py:31
  75.5 2.8 %collective-permute-start.18 = (bf16[144,256]{1,0:T(8,128)(2,1)S(1)}, bf16[144,256]{1,0:T(8,128)(2,1)S(1)}, u32[]{:S(2)}, u32[]{:S(2)}) collective-permute-start(bf16[144,256]{1,0:T(8,128)(2,1)S(1)} %get-tuple-element.32), channel_id=1, source_target_pairs={{0,20},{1,13},{4,24},{5,17},{8,28},{9,21},{12,0},{13,25},{16,4},{1... | collective-permute-start | bytes 221192 | tf_op jit(solution)/shard_map/ppermute | solution.py:31
  79.4 4.0 %collective-permute-start.20 = (bf16[144,256]{1,0:T(8,128)(2,1)S(1)}, bf16[144,256]{1,0:T(8,128)(2,1)S(1)}, u32[]{:S(2)}, u32[]{:S(2)}) collective-permute-start(bf16[144,256]{1,0:T(8,128)(2,1)S(1)} %get-tuple-element.34), channel_id=1, source_target_pairs={{0,16},{1,17},{4,20},{5,21},{8,24},{9,25},{12,28},{13,29},{16,0},{... | collective-permute-start | bytes 221192 | tf_op jit(solution)/shard_map/ppermute | solution.py:31
  85.2 3.5 %collective-permute-done.19.refs_1_ = bf16[144,256]{1,0:T(8,128)(2,1)S(1)} collective-permute-done((bf16[144,256]{1,0:T(8,128)(2,1)S(1)}, bf16[144,256]{1,0:T(8,128)(2,1)S(1)}, u32[]{:S(2)}, u32[]{:S(2)}) %collective-permute-start.19) | collective-permute-done | bytes 73760 | tf_op jit(solution)/shard_map/ppermute | solution.py:31
  89.3 1.4 %shard_map.52 = (f32[128,2048]{1,0:T(8,128)}, f32[1,32]{1,0:T(1,128)}) custom-call(bf16[144,256]{1,0:T(8,128)(2,1)S(1)} %collective-permute-done.18.refs_0_, bf16[144,256]{1,0:T(8,128)(2,1)S(1)} %collective-permute-done.19.refs_1_, bf16[144,256]{1,0:T(8,128)(2,1)S(1)} %collective-permute-done.20.refs_2_, ...), custom_call_target="tpu_custom_call", output_to_operand_aliasing={{0}: (4, {})} | custom-call | tf_op jit(solution)/shard_map/pallas_call | solution.py:278
  (53 shorter events, 19.6 us)
Async XLA Ops:
  0.6 17.0 %collective-permute-start = (bf16[128,2048]{1,0:T(8,128)(2,1)}, bf16[128,2048]{1,0:T(8,128)(2,1)S(1)}, u32[]{:S(2)}, u32[]{:S(2)}) collective-permute-start(bf16[128,2048]{1,0:T(8,128)(2,1)} %refs_0_.3), channel_id=1, source_target_pairs={{0,4},{1,29},{4,8},{5,1},{8,12},{9,5},{12,16},{13,9},{16,20},{17,1... | collective-permute-start | bytes 1572872 | tf_op jit(solution)/shard_map/ppermute | solution.py:31
  2.6 15.4 %collective-permute-start.3 = (bf16[128,2048]{1,0:T(8,128)(2,1)}, bf16[128,2048]{1,0:T(8,128)(2,1)S(1)}, u32[]{:S(2)}, u32[]{:S(2)}) collective-permute-start(bf16[128,2048]{1,0:T(8,128)(2,1)} %refs_0_.3), channel_id=1, source_target_pairs={{0,28},{1,5},{4,0},{5,9},{8,4},{9,13},{12,8},{13,17},{16,12},{17,2... | collective-permute-start | bytes 1572872 | tf_op jit(solution)/shard_map/ppermute | solution.py:31
  8.5 14.1 %collective-permute-start.10 = (bf16[128,2176]{1,0:T(8,128)(2,1)S(1)}, bf16[128,2176]{1,0:T(8,128)(2,1)S(1)}, u32[]{:S(2)}, u32[]{:S(2)}) collective-permute-start(bf16[128,2176]{1,0:T(8,128)(2,1)S(1)} %pad_maximum_fusion.refs_3_.refs_0_.refs_5_), channel_id=1, source_target_pairs={{0,128},{128,0},{1,129},{129,1},{2,130},{130,2},{3,131},{131,3},{4... | collective-permute-start | bytes 1671176 | tf_op jit(solution)/shard_map/ppermute | solution.py:35
  9.9 15.4 %collective-permute-start.8 = (bf16[128,2176]{1,0:T(8,128)(2,1)S(1)}, bf16[128,2176]{1,0:T(8,128)(2,1)S(1)}, u32[]{:S(2)}, u32[]{:S(2)}) collective-permute-start(bf16[128,2176]{1,0:T(8,128)(2,1)S(1)} %pad_maximum_fusion.refs_3_.refs_0_.refs_5_), channel_id=1, source_target_pairs={{0,96},{1,33},{32,0},{33,65},{64,32},{65,97},{96,64},{97,1},{2,98}... | collective-permute-start | bytes 1671176 | tf_op jit(solution)/shard_map/ppermute | solution.py:31
  12.7 13.4 %collective-permute-start.7 = (bf16[128,2176]{1,0:T(8,128)(2,1)S(1)}, bf16[128,2176]{1,0:T(8,128)(2,1)S(1)}, u32[]{:S(2)}, u32[]{:S(2)}) collective-permute-start(bf16[128,2176]{1,0:T(8,128)(2,1)S(1)} %pad_maximum_fusion.refs_3_.refs_0_.refs_5_), channel_id=1, source_target_pairs={{0,32},{1,97},{32,64},{33,1},{64,96},{65,33},{96,0},{97,65},{2,34}... | collective-permute-start | bytes 1671176 | tf_op jit(solution)/shard_map/ppermute | solution.py:31
  17.7 14.9 %collective-permute-start.1 = (bf16[128,2048]{1,0:T(8,128)(2,1)S(1)}, bf16[128,2048]{1,0:T(8,128)(2,1)S(1)}, u32[]{:S(2)}, u32[]{:S(2)}) collective-permute-start(bf16[128,2048]{1,0:T(8,128)(2,1)S(1)} %collective-permute-done.refs_1_), channel_id=1, source_target_pairs={{0,4},{1,29},{4,8},{5,1},{8,12},{9,5},{12,16},{13,9},{16,20},{17,1... | collective-permute-start | bytes 1572872 | tf_op jit(solution)/shard_map/ppermute | solution.py:31
  18.1 14.5 %collective-permute-start.4 = (bf16[128,2048]{1,0:T(8,128)(2,1)S(1)}, bf16[128,2048]{1,0:T(8,128)(2,1)S(1)}, u32[]{:S(2)}, u32[]{:S(2)}) collective-permute-start(bf16[128,2048]{1,0:T(8,128)(2,1)S(1)} %collective-permute-done.3.refs_2_), channel_id=1, source_target_pairs={{0,28},{1,5},{4,0},{5,9},{8,4},{9,13},{12,8},{13,17},{16,12},{17,2... | collective-permute-start | bytes 1572872 | tf_op jit(solution)/shard_map/ppermute | solution.py:31
  22.6 13.2 %collective-permute-start.11 = (bf16[128,2176]{1,0:T(8,128)(2,1)S(1)}, bf16[128,2176]{1,0:T(8,128)(2,1)S(1)}, u32[]{:S(2)}, u32[]{:S(2)}) collective-permute-start(bf16[128,2176]{1,0:T(8,128)(2,1)S(1)} %collective-permute-done.10.refs_7_.refs_4_.refs_9_), channel_id=1, source_target_pairs={{0,32},{1,97},{32,64},{33,1},{64,96},{65,33},{96,0},{97,65},{2,34}... | collective-permute-start | bytes 1671176 | tf_op jit(solution)/shard_map/ppermute | solution.py:31
  25.3 12.8 %collective-permute-start.12 = (bf16[128,2176]{1,0:T(8,128)(2,1)S(1)}, bf16[128,2176]{1,0:T(8,128)(2,1)S(1)}, u32[]{:S(2)}, u32[]{:S(2)}) collective-permute-start(bf16[128,2176]{1,0:T(8,128)(2,1)S(1)} %collective-permute-done.8.refs_5_.refs_2_.refs_7_), channel_id=1, source_target_pairs={{0,128},{128,0},{1,129},{129,1},{2,130},{130,2},{3,131},{131,3},{4... | collective-permute-start | bytes 1671176 | tf_op jit(solution)/shard_map/ppermute | solution.py:35
  26.1 13.2 %collective-permute-start.9 = (bf16[128,2176]{1,0:T(8,128)(2,1)S(1)}, bf16[128,2176]{1,0:T(8,128)(2,1)S(1)}, u32[]{:S(2)}, u32[]{:S(2)}) collective-permute-start(bf16[128,2176]{1,0:T(8,128)(2,1)S(1)} %collective-permute-done.7.refs_4_.refs_1_.refs_6_), channel_id=1, source_target_pairs={{0,32},{1,97},{32,64},{33,1},{64,96},{65,33},{96,0},{97,65},{2,34}... | collective-permute-start | bytes 1671176 | tf_op jit(solution)/shard_map/ppermute | solution.py:31
  32.6 15.6 %collective-permute-start.2 = (bf16[128,2048]{1,0:T(8,128)(2,1)S(1)}, bf16[128,2048]{1,0:T(8,128)(2,1)S(1)}, u32[]{:S(2)}, u32[]{:S(2)}) collective-permute-start(bf16[128,2048]{1,0:T(8,128)(2,1)S(1)} %collective-permute-done.1.refs_3_), channel_id=1, source_target_pairs={{0,4},{1,29},{4,8},{5,1},{8,12},{9,5},{12,16},{13,9},{16,20},{17,1... | collective-permute-start | bytes 1572872 | tf_op jit(solution)/shard_map/ppermute | solution.py:31
  32.6 15.6 %collective-permute-start.5 = (bf16[128,2048]{1,0:T(8,128)(2,1)S(1)}, bf16[128,2048]{1,0:T(8,128)(2,1)S(1)}, u32[]{:S(2)}, u32[]{:S(2)}) collective-permute-start(bf16[128,2048]{1,0:T(8,128)(2,1)S(1)} %collective-permute-done.4.refs_4_), channel_id=1, source_target_pairs={{0,28},{1,5},{4,0},{5,9},{8,4},{9,13},{12,8},{13,17},{16,12},{17,2... | collective-permute-start | bytes 1572872 | tf_op jit(solution)/shard_map/ppermute | solution.py:31
  39.3 10.7 %collective-permute-start.13 = (bf16[128,2176]{1,0:T(8,128)(2,1)S(1)}, bf16[128,2176]{1,0:T(8,128)(2,1)S(1)}, u32[]{:S(2)}, u32[]{:S(2)}) collective-permute-start(bf16[128,2176]{1,0:T(8,128)(2,1)S(1)} %collective-permute-done.11.refs_8_.refs_5_.refs_10_), channel_id=1, source_target_pairs={{0,32},{1,97},{32,64},{33,1},{64,96},{65,33},{96,0},{97,65},{2,34}... | collective-permute-start | bytes 1671176 | tf_op jit(solution)/shard_map/ppermute | solution.py:31
  48.1 10.4 %collective-permute-start.6 = (bf16[128,2048]{1,0:T(8,128)(2,1)S(1)}, bf16[128,2048]{1,0:T(8,128)(2,1)S(1)}, u32[]{:S(2)}, u32[]{:S(2)}) collective-permute-start(bf16[128,2048]{1,0:T(8,128)(2,1)S(1)} %collective-permute-done.2.refs_0_), channel_id=1, source_target_pairs={{0,4},{1,29},{4,8},{5,1},{8,12},{9,5},{12,16},{13,9},{16,20},{17,1... | collective-permute-start | bytes 1572872 | tf_op jit(solution)/shard_map/ppermute | solution.py:31
  51.9 3.1 %collective-permute-start.21 = (f32[160,512]{1,0:T(8,128)S(1)}, f32[160,512]{1,0:T(8,128)S(1)}, u32[]{:S(2)}, u32[]{:S(2)}) collective-permute-start(f32[160,512]{1,0:T(8,128)S(1)} %get-tuple-element.35), channel_id=1, source_target_pairs={{0,1},{1,0},{2,3},{3,2},{4,5},{5,4},{6,7},{7,6},{8,9},{9,8},{10,11... | collective-permute-start | bytes 983048 | tf_op jit(solution)/shard_map/ppermute | solution.py:35
  56.0 11.5 %collective-permute-start.25 = (bf16[656,256]{1,0:T(8,128)(2,1)S(1)}, bf16[656,256]{1,0:T(8,128)(2,1)S(1)}, u32[]{:S(2)}, u32[]{:S(2)}) collective-permute-start(bf16[656,256]{1,0:T(8,128)(2,1)S(1)} %get-tuple-element.40), channel_id=1, source_target_pairs={{0,2},{2,0},{1,3},{3,1},{4,6},{6,4},{5,7},{7,5},{8,10},{10,8},{9,1... | collective-permute-start | bytes 1007624 | tf_op jit(solution)/shard_map/ppermute | solution.py:35
  62.9 12.0 %collective-permute-start.17 = (bf16[400,256]{1,0:T(8,128)(2,1)S(1)}, bf16[400,256]{1,0:T(8,128)(2,1)S(1)}, u32[]{:S(2)}, u32[]{:S(2)}) collective-permute-start(bf16[400,256]{1,0:T(8,128)(2,1)S(1)} %get-tuple-element.31), channel_id=1, source_target_pairs={{0,2},{2,0},{1,3},{3,1},{4,6},{6,4},{5,7},{7,5},{8,10},{10,8},{9,1... | collective-permute-start | bytes 614408 | tf_op jit(solution)/shard_map/ppermute | solution.py:35
  68.2 10.0 %collective-permute-start.26 = (bf16[144,256]{1,0:T(8,128)(2,1)S(1)}, bf16[144,256]{1,0:T(8,128)(2,1)S(1)}, u32[]{:S(2)}, u32[]{:S(2)}) collective-permute-start(bf16[144,256]{1,0:T(8,128)(2,1)S(1)} %get-tuple-element.42), channel_id=1, source_target_pairs={{0,28},{1,5},{4,0},{5,9},{8,4},{9,13},{12,8},{13,17},{16,12},{17,2... | collective-permute-start | bytes 221192 | tf_op jit(solution)/shard_map/ppermute | solution.py:31
  72.0 7.3 %collective-permute-start.27 = (bf16[144,256]{1,0:T(8,128)(2,1)S(1)}, bf16[144,256]{1,0:T(8,128)(2,1)S(1)}, u32[]{:S(2)}, u32[]{:S(2)}) collective-permute-start(bf16[144,256]{1,0:T(8,128)(2,1)S(1)} %get-tuple-element.43), channel_id=1, source_target_pairs={{0,4},{1,29},{4,8},{5,1},{8,12},{9,5},{12,16},{13,9},{16,20},{17,1... | collective-permute-start | bytes 221192 | tf_op jit(solution)/shard_map/ppermute | solution.py:31
  72.0 11.3 %collective-permute-start.28 = (bf16[144,256]{1,0:T(8,128)(2,1)S(1)}, bf16[144,256]{1,0:T(8,128)(2,1)S(1)}, u32[]{:S(2)}, u32[]{:S(2)}) collective-permute-start(bf16[144,256]{1,0:T(8,128)(2,1)S(1)} %get-tuple-element.44), channel_id=1, source_target_pairs={{0,24},{1,9},{4,28},{5,13},{8,0},{9,17},{12,4},{13,21},{16,8},{17,... | collective-permute-start | bytes 221192 | tf_op jit(solution)/shard_map/ppermute | solution.py:31
  73.6 9.8 %collective-permute-start.29 = (bf16[144,256]{1,0:T(8,128)(2,1)S(1)}, bf16[144,256]{1,0:T(8,128)(2,1)S(1)}, u32[]{:S(2)}, u32[]{:S(2)}) collective-permute-start(bf16[144,256]{1,0:T(8,128)(2,1)S(1)} %get-tuple-element.45), channel_id=1, source_target_pairs={{0,8},{1,25},{4,12},{5,29},{8,16},{9,1},{12,20},{13,5},{16,24},{17... | collective-permute-start | bytes 221192 | tf_op jit(solution)/shard_map/ppermute | solution.py:31
  75.5 9.7 %collective-permute-start.18 = (bf16[144,256]{1,0:T(8,128)(2,1)S(1)}, bf16[144,256]{1,0:T(8,128)(2,1)S(1)}, u32[]{:S(2)}, u32[]{:S(2)}) collective-permute-start(bf16[144,256]{1,0:T(8,128)(2,1)S(1)} %get-tuple-element.32), channel_id=1, source_target_pairs={{0,20},{1,13},{4,24},{5,17},{8,28},{9,21},{12,0},{13,25},{16,4},{1... | collective-permute-start | bytes 221192 | tf_op jit(solution)/shard_map/ppermute | solution.py:31
  78.2 10.5 %collective-permute-start.19 = (bf16[144,256]{1,0:T(8,128)(2,1)S(1)}, bf16[144,256]{1,0:T(8,128)(2,1)S(1)}, u32[]{:S(2)}, u32[]{:S(2)}) collective-permute-start(bf16[144,256]{1,0:T(8,128)(2,1)S(1)} %get-tuple-element.33), channel_id=1, source_target_pairs={{0,12},{1,21},{4,16},{5,25},{8,20},{9,29},{12,24},{13,1},{16,28},{... | collective-permute-start | bytes 221192 | tf_op jit(solution)/shard_map/ppermute | solution.py:31
  79.4 10.0 %collective-permute-start.20 = (bf16[144,256]{1,0:T(8,128)(2,1)S(1)}, bf16[144,256]{1,0:T(8,128)(2,1)S(1)}, u32[]{:S(2)}, u32[]{:S(2)}) collective-permute-start(bf16[144,256]{1,0:T(8,128)(2,1)S(1)} %get-tuple-element.34), channel_id=1, source_target_pairs={{0,16},{1,17},{4,20},{5,21},{8,24},{9,25},{12,28},{13,29},{16,0},{... | collective-permute-start | bytes 221192 | tf_op jit(solution)/shard_map/ppermute | solution.py:31
  (8 other events, 64.8 us)

commit v8 on v7

--- a/solution.py
+++ b/solution.py
@@ -12,7 +12,7 @@
 ROWS, PANEL = 128, 2048
 NX, NZ = 4, 8
 F32 = jnp.float32
-GROUPS = ((0, 1, -1, 2, -2), (3, -3, 4))
+GROUPS = ((0, 2, -2, 1, -1), (3, -3, 4))
 PARTS = ((160,) * 4, (128,) * 3)
 COSTS = ((0, 0, 10), (1.1, 0.5, 0.5))
 PLACE_COSTS = (0, 0)

time: 91.1 us -> 91.5 us (level)
  transfers between devices with their start and end apart: 30 -> 30, of which waited for: 15 -> 14; matrix products, arithmetic and copies ran while one was open for 1% -> 1% of each run, Pallas kernels for 11% -> 11%
where the time goes in v8:
time: 91.5 us; the launch traced here: 91.4 us
  starting transfers between devices  39.2 us (43%)
  waiting for transfers between devices  37.7 us (41%)
  Pallas kernels  11.8 us (13%)
  other arithmetic  1.08 us (1%)
  between operations  1 us (1%)
    ppermute x19, starting transfers between devices, shift(): return lax.ppermute(value, (axis, 'core'), pairs)  33.5 us
    ppermute x19, waiting for transfers between devices, shift(): return lax.ppermute(value, (axis, 'core'), pairs)  30.8 us
    ppermute x11, waiting for transfers between devices, swap(): return lax.ppermute(value, axis, [(0, 1), (1, 0)])  6.9 us
    pallas_call x4, Pallas kernels, products(): pl.pallas_call(kernel, out_shape=[jax.ShapeDtypeStruct((count, 512), F32)...  6.16 us
    ppermute x11, starting transfers between devices, swap(): return lax.ppermute(value, axis, [(0, 1), (1, 0)])  5.63 us
    pallas_call x2, Pallas kernels, place(): pl.pallas_call(kernel, out_shape=(jax.ShapeDtypeStruct((ROWS, PANEL), F32...  2.48 us
  transfers between devices with their start and end apart: 30, of which 14 were waited for; matrix products, arithmetic and copies ran while one was open for 1% of the time, Pallas kernels for 11%

profile of v8, /device:TPU:16, one launch (start us, length us, event | category | flops | bytes accessed | tf_op | source)
XLA Modules:
  0.0 91.4 jit_solution(12803410431760554735)
XLA Ops:
  0.6 2.0 %collective-permute-start = (bf16[128,2048]{1,0:T(8,128)(2,1)}, bf16[128,2048]{1,0:T(8,128)(2,1)S(1)}, u32[]{:S(2)}, u32[]{:S(2)}) collective-permute-start(bf16[128,2048]{1,0:T(8,128)(2,1)} %refs_0_.3), channel_id=1, source_target_pairs={{0,4},{1,29},{4,8},{5,1},{8,12},{9,5},{12,16},{13,9},{16,20},{17,1... | collective-permute-start | bytes 1572872 | tf_op jit(solution)/shard_map/ppermute | solution.py:31
  2.6 4.0 %collective-permute-start.3 = (bf16[128,2048]{1,0:T(8,128)(2,1)}, bf16[128,2048]{1,0:T(8,128)(2,1)S(1)}, u32[]{:S(2)}, u32[]{:S(2)}) collective-permute-start(bf16[128,2048]{1,0:T(8,128)(2,1)} %refs_0_.3), channel_id=1, source_target_pairs={{0,28},{1,5},{4,0},{5,9},{8,4},{9,13},{12,8},{13,17},{16,12},{17,2... | collective-permute-start | bytes 1572872 | tf_op jit(solution)/shard_map/ppermute | solution.py:31
  8.5 1.4 %collective-permute-start.10 = (bf16[128,2176]{1,0:T(8,128)(2,1)S(1)}, bf16[128,2176]{1,0:T(8,128)(2,1)S(1)}, u32[]{:S(2)}, u32[]{:S(2)}) collective-permute-start(bf16[128,2176]{1,0:T(8,128)(2,1)S(1)} %pad_maximum_fusion.refs_3_.refs_0_.refs_5_), channel_id=1, source_target_pairs={{0,128},{128,0},{1,129},{129,1},{2,130},{130,2},{3,131},{131,3},{4... | collective-permute-start | bytes 1671176 | tf_op jit(solution)/shard_map/ppermute | solution.py:35
  9.9 2.8 %collective-permute-start.8 = (bf16[128,2176]{1,0:T(8,128)(2,1)S(1)}, bf16[128,2176]{1,0:T(8,128)(2,1)S(1)}, u32[]{:S(2)}, u32[]{:S(2)}) collective-permute-start(bf16[128,2176]{1,0:T(8,128)(2,1)S(1)} %pad_maximum_fusion.refs_3_.refs_0_.refs_5_), channel_id=1, source_target_pairs={{0,96},{1,33},{32,0},{33,65},{64,32},{65,97},{96,64},{97,1},{2,98}... | collective-permute-start | bytes 1671176 | tf_op jit(solution)/shard_map/ppermute | solution.py:31
  12.7 5.0 %collective-permute-done.refs_3_ = bf16[128,2048]{1,0:T(8,128)(2,1)S(1)} collective-permute-done((bf16[128,2048]{1,0:T(8,128)(2,1)}, bf16[128,2048]{1,0:T(8,128)(2,1)S(1)}, u32[]{:S(2)}, u32[]{:S(2)}) %collective-permute-start) | collective-permute-done | bytes 524320 | tf_op jit(solution)/shard_map/ppermute | solution.py:31
  18.1 3.6 %collective-permute-start.4 = (bf16[128,2048]{1,0:T(8,128)(2,1)S(1)}, bf16[128,2048]{1,0:T(8,128)(2,1)S(1)}, u32[]{:S(2)}, u32[]{:S(2)}) collective-permute-start(bf16[128,2048]{1,0:T(8,128)(2,1)S(1)} %collective-permute-done.3.refs_4_), channel_id=1, source_target_pairs={{0,28},{1,5},{4,0},{5,9},{8,4},{9,13},{12,8},{13,17},{16,12},{17,2... | collective-permute-start | bytes 1572872 | tf_op jit(solution)/shard_map/ppermute | solution.py:31
  22.6 1.5 %collective-permute-start.11 = (bf16[128,2176]{1,0:T(8,128)(2,1)S(1)}, bf16[128,2176]{1,0:T(8,128)(2,1)S(1)}, u32[]{:S(2)}, u32[]{:S(2)}) collective-permute-start(bf16[128,2176]{1,0:T(8,128)(2,1)S(1)} %collective-permute-done.10.refs_7_.refs_4_.refs_9_), channel_id=1, source_target_pairs={{0,32},{1,97},{32,64},{33,1},{64,96},{65,33},{96,0},{97,65},{2,34}... | collective-permute-start | bytes 1671176 | tf_op jit(solution)/shard_map/ppermute | solution.py:31
  26.1 1.5 %collective-permute-start.9 = (bf16[128,2176]{1,0:T(8,128)(2,1)S(1)}, bf16[128,2176]{1,0:T(8,128)(2,1)S(1)}, u32[]{:S(2)}, u32[]{:S(2)}) collective-permute-start(bf16[128,2176]{1,0:T(8,128)(2,1)S(1)} %collective-permute-done.7.refs_4_.refs_1_.refs_6_), channel_id=1, source_target_pairs={{0,32},{1,97},{32,64},{33,1},{64,96},{65,33},{96,0},{97,65},{2,34}... | collective-permute-start | bytes 1671176 | tf_op jit(solution)/shard_map/ppermute | solution.py:31
  27.6 5.0 %collective-permute-done.1.refs_1_ = bf16[128,2048]{1,0:T(8,128)(2,1)S(1)} collective-permute-done((bf16[128,2048]{1,0:T(8,128)(2,1)S(1)}, bf16[128,2048]{1,0:T(8,128)(2,1)S(1)}, u32[]{:S(2)}, u32[]{:S(2)}) %collective-permute-start.1) | collective-permute-done | bytes 524320 | tf_op jit(solution)/shard_map/ppermute | solution.py:31
  32.6 3.2 %collective-permute-start.5 = (bf16[128,2048]{1,0:T(8,128)(2,1)S(1)}, bf16[128,2048]{1,0:T(8,128)(2,1)S(1)}, u32[]{:S(2)}, u32[]{:S(2)}) collective-permute-start(bf16[128,2048]{1,0:T(8,128)(2,1)S(1)} %collective-permute-done.4.refs_2_), channel_id=1, source_target_pairs={{0,28},{1,5},{4,0},{5,9},{8,4},{9,13},{12,8},{13,17},{16,12},{17,2... | collective-permute-start | bytes 1572872 | tf_op jit(solution)/shard_map/ppermute | solution.py:31
  35.8 2.3 %collective-permute-done.12.refs_9_.refs_6_.refs_11_ = bf16[128,2176]{1,0:T(8,128)(2,1)S(1)} collective-permute-done((bf16[128,2176]{1,0:T(8,128)(2,1)S(1)}, bf16[128,2176]{1,0:T(8,128)(2,1)S(1)}, u32[]{:S(2)}, u32[]{:S(2)}) %collective-permute-start.12) | collective-permute-done | bytes 557088 | tf_op jit(solution)/shard_map/ppermute | solution.py:35
  39.6 8.5 %collective-permute-done.2.refs_0_ = bf16[128,2048]{1,0:T(8,128)(2,1)S(1)} collective-permute-done((bf16[128,2048]{1,0:T(8,128)(2,1)S(1)}, bf16[128,2048]{1,0:T(8,128)(2,1)S(1)}, u32[]{:S(2)}, u32[]{:S(2)}) %collective-permute-start.2) | collective-permute-done | bytes 524320 | tf_op jit(solution)/shard_map/ppermute | solution.py:31
  48.1 1.9 %collective-permute-done.13.refs_10_.refs_7_.refs_12_ = bf16[128,2176]{1,0:T(8,128)(2,1)S(1)} collective-permute-done((bf16[128,2176]{1,0:T(8,128)(2,1)S(1)}, bf16[128,2176]{1,0:T(8,128)(2,1)S(1)}, u32[]{:S(2)}, u32[]{:S(2)}) %collective-permute-start.13) | collective-permute-done | bytes 557088 | tf_op jit(solution)/shard_map/ppermute | solution.py:31
  50.1 1.8 %shard_map.48 = (f32[160,512]{1,0:T(8,128)S(1)}, f32[160,512]{1,0:T(8,128)S(1)}, f32[160,512]{1,0:T(8,128)S(1)}, f32[160,512]{1,0:T(8,128)S(1)}) custom-call(bf16[128,2048]{1,0:T(8,128)(2,1)S(1)} %copy-done, bf16[128,2048]{1,0:T(8,128)(2,1)S(1)} %collective-permute-done.1.refs_1_, bf16[128,2048]{1,0:T(8,128)(2,1)S(1)} %collective-permute-done.4.refs_2_, ...), custom_call_target="tpu_custom_call" | custom-call | tf_op jit(solution)/shard_map/pallas_call | solution.py:116
  53.2 1.8 %shard_map.47.a = f32[640,512]{1,0:T(8,128)S(1)} custom-call(bf16[128,2048]{1,0:T(8,128)(2,1)S(1)} %copy-done, bf16[128,2048]{1,0:T(8,128)(2,1)S(1)} %collective-permute-done.1.refs_1_, bf16[128,2048]{1,0:T(8,128)(2,1)S(1)} %collective-permute-done.4.refs_2_, bf16[128,2048]{1,0:T(8,128)(2,1)S(1)} %collective-permute-done.refs_3_, ...), custom_call_target="tpu_custom_call" | custom-call | tf_op jit(solution)/shard_map/pallas_call | solution.py:116
  56.4 2.2 %collective-permute-done.6.refs_2_ = bf16[128,2048]{1,0:T(8,128)(2,1)S(1)} collective-permute-done((bf16[128,2048]{1,0:T(8,128)(2,1)S(1)}, bf16[128,2048]{1,0:T(8,128)(2,1)S(1)}, u32[]{:S(2)}, u32[]{:S(2)}) %collective-permute-start.6) | collective-permute-done | bytes 524320 | tf_op jit(solution)/shard_map/ppermute | solution.py:31
  64.1 3.4 %collective-permute-done.25.code = bf16[656,256]{1,0:T(8,128)(2,1)S(1)} collective-permute-done((bf16[656,256]{1,0:T(8,128)(2,1)S(1)}, bf16[656,256]{1,0:T(8,128)(2,1)S(1)}, u32[]{:S(2)}, u32[]{:S(2)}) %collective-permute-start.25) | collective-permute-done | bytes 335904 | tf_op jit(solution)/shard_map/ppermute | solution.py:35
  68.2 3.1 %collective-permute-start.26 = (bf16[144,256]{1,0:T(8,128)(2,1)S(1)}, bf16[144,256]{1,0:T(8,128)(2,1)S(1)}, u32[]{:S(2)}, u32[]{:S(2)}) collective-permute-start(bf16[144,256]{1,0:T(8,128)(2,1)S(1)} %get-tuple-element.42), channel_id=1, source_target_pairs={{0,24},{1,9},{4,28},{5,13},{8,0},{9,17},{12,4},{13,21},{16,8},{17,... | collective-permute-start | bytes 221192 | tf_op jit(solution)/shard_map/ppermute | solution.py:31
  71.2 4.9 %collective-permute-start.28 = (bf16[144,256]{1,0:T(8,128)(2,1)S(1)}, bf16[144,256]{1,0:T(8,128)(2,1)S(1)}, u32[]{:S(2)}, u32[]{:S(2)}) collective-permute-start(bf16[144,256]{1,0:T(8,128)(2,1)S(1)} %get-tuple-element.44), channel_id=1, source_target_pairs={{0,28},{1,5},{4,0},{5,9},{8,4},{9,13},{12,8},{13,17},{16,12},{17,2... | collective-permute-start | bytes 221192 | tf_op jit(solution)/shard_map/ppermute | solution.py:31
  77.4 3.1 %collective-permute-start.19 = (bf16[144,256]{1,0:T(8,128)(2,1)S(1)}, bf16[144,256]{1,0:T(8,128)(2,1)S(1)}, u32[]{:S(2)}, u32[]{:S(2)}) collective-permute-start(bf16[144,256]{1,0:T(8,128)(2,1)S(1)} %get-tuple-element.33), channel_id=1, source_target_pairs={{0,12},{1,21},{4,16},{5,25},{8,20},{9,29},{12,24},{13,1},{16,28},{... | collective-permute-start | bytes 221192 | tf_op jit(solution)/shard_map/ppermute | solution.py:31
  80.6 2.8 %collective-permute-start.20 = (bf16[144,256]{1,0:T(8,128)(2,1)S(1)}, bf16[144,256]{1,0:T(8,128)(2,1)S(1)}, u32[]{:S(2)}, u32[]{:S(2)}) collective-permute-start(bf16[144,256]{1,0:T(8,128)(2,1)S(1)} %get-tuple-element.34), channel_id=1, source_target_pairs={{0,16},{1,17},{4,20},{5,21},{8,24},{9,25},{12,28},{13,29},{16,0},{... | collective-permute-start | bytes 221192 | tf_op jit(solution)/shard_map/ppermute | solution.py:31
  84.4 3.1 %collective-permute-done.18.refs_0_ = bf16[144,256]{1,0:T(8,128)(2,1)S(1)} collective-permute-done((bf16[144,256]{1,0:T(8,128)(2,1)S(1)}, bf16[144,256]{1,0:T(8,128)(2,1)S(1)}, u32[]{:S(2)}, u32[]{:S(2)}) %collective-permute-start.18) | collective-permute-done | bytes 73760 | tf_op jit(solution)/shard_map/ppermute | solution.py:31
  87.5 2.3 %collective-permute-done.20.refs_2_ = bf16[144,256]{1,0:T(8,128)(2,1)S(1)} collective-permute-done((bf16[144,256]{1,0:T(8,128)(2,1)S(1)}, bf16[144,256]{1,0:T(8,128)(2,1)S(1)}, u32[]{:S(2)}, u32[]{:S(2)}) %collective-permute-start.20) | collective-permute-done | bytes 73760 | tf_op jit(solution)/shard_map/ppermute | solution.py:31
  89.8 1.4 %shard_map.52 = (f32[128,2048]{1,0:T(8,128)}, f32[1,32]{1,0:T(1,128)}) custom-call(bf16[144,256]{1,0:T(8,128)(2,1)S(1)} %collective-permute-done.18.refs_0_, bf16[144,256]{1,0:T(8,128)(2,1)S(1)} %collective-permute-done.19.refs_1_, bf16[144,256]{1,0:T(8,128)(2,1)S(1)} %collective-permute-done.20.refs_2_, ...), custom_call_target="tpu_custom_call", output_to_operand_aliasing={{0}: (4, {})} | custom-call | tf_op jit(solution)/shard_map/pallas_call | solution.py:278
  (53 shorter events, 17.7 us)
Async XLA Ops:
  0.6 17.0 %collective-permute-start = (bf16[128,2048]{1,0:T(8,128)(2,1)}, bf16[128,2048]{1,0:T(8,128)(2,1)S(1)}, u32[]{:S(2)}, u32[]{:S(2)}) collective-permute-start(bf16[128,2048]{1,0:T(8,128)(2,1)} %refs_0_.3), channel_id=1, source_target_pairs={{0,4},{1,29},{4,8},{5,1},{8,12},{9,5},{12,16},{13,9},{16,20},{17,1... | collective-permute-start | bytes 1572872 | tf_op jit(solution)/shard_map/ppermute | solution.py:31
  2.6 15.4 %collective-permute-start.3 = (bf16[128,2048]{1,0:T(8,128)(2,1)}, bf16[128,2048]{1,0:T(8,128)(2,1)S(1)}, u32[]{:S(2)}, u32[]{:S(2)}) collective-permute-start(bf16[128,2048]{1,0:T(8,128)(2,1)} %refs_0_.3), channel_id=1, source_target_pairs={{0,28},{1,5},{4,0},{5,9},{8,4},{9,13},{12,8},{13,17},{16,12},{17,2... | collective-permute-start | bytes 1572872 | tf_op jit(solution)/shard_map/ppermute | solution.py:31
  8.5 14.1 %collective-permute-start.10 = (bf16[128,2176]{1,0:T(8,128)(2,1)S(1)}, bf16[128,2176]{1,0:T(8,128)(2,1)S(1)}, u32[]{:S(2)}, u32[]{:S(2)}) collective-permute-start(bf16[128,2176]{1,0:T(8,128)(2,1)S(1)} %pad_maximum_fusion.refs_3_.refs_0_.refs_5_), channel_id=1, source_target_pairs={{0,128},{128,0},{1,129},{129,1},{2,130},{130,2},{3,131},{131,3},{4... | collective-permute-start | bytes 1671176 | tf_op jit(solution)/shard_map/ppermute | solution.py:35
  9.9 15.4 %collective-permute-start.8 = (bf16[128,2176]{1,0:T(8,128)(2,1)S(1)}, bf16[128,2176]{1,0:T(8,128)(2,1)S(1)}, u32[]{:S(2)}, u32[]{:S(2)}) collective-permute-start(bf16[128,2176]{1,0:T(8,128)(2,1)S(1)} %pad_maximum_fusion.refs_3_.refs_0_.refs_5_), channel_id=1, source_target_pairs={{0,96},{1,33},{32,0},{33,65},{64,32},{65,97},{96,64},{97,1},{2,98}... | collective-permute-start | bytes 1671176 | tf_op jit(solution)/shard_map/ppermute | solution.py:31
  12.7 13.4 %collective-permute-start.7 = (bf16[128,2176]{1,0:T(8,128)(2,1)S(1)}, bf16[128,2176]{1,0:T(8,128)(2,1)S(1)}, u32[]{:S(2)}, u32[]{:S(2)}) collective-permute-start(bf16[128,2176]{1,0:T(8,128)(2,1)S(1)} %pad_maximum_fusion.refs_3_.refs_0_.refs_5_), channel_id=1, source_target_pairs={{0,32},{1,97},{32,64},{33,1},{64,96},{65,33},{96,0},{97,65},{2,34}... | collective-permute-start | bytes 1671176 | tf_op jit(solution)/shard_map/ppermute | solution.py:31
  17.7 14.9 %collective-permute-start.1 = (bf16[128,2048]{1,0:T(8,128)(2,1)S(1)}, bf16[128,2048]{1,0:T(8,128)(2,1)S(1)}, u32[]{:S(2)}, u32[]{:S(2)}) collective-permute-start(bf16[128,2048]{1,0:T(8,128)(2,1)S(1)} %collective-permute-done.refs_3_), channel_id=1, source_target_pairs={{0,4},{1,29},{4,8},{5,1},{8,12},{9,5},{12,16},{13,9},{16,20},{17,1... | collective-permute-start | bytes 1572872 | tf_op jit(solution)/shard_map/ppermute | solution.py:31
  18.1 14.5 %collective-permute-start.4 = (bf16[128,2048]{1,0:T(8,128)(2,1)S(1)}, bf16[128,2048]{1,0:T(8,128)(2,1)S(1)}, u32[]{:S(2)}, u32[]{:S(2)}) collective-permute-start(bf16[128,2048]{1,0:T(8,128)(2,1)S(1)} %collective-permute-done.3.refs_4_), channel_id=1, source_target_pairs={{0,28},{1,5},{4,0},{5,9},{8,4},{9,13},{12,8},{13,17},{16,12},{17,2... | collective-permute-start | bytes 1572872 | tf_op jit(solution)/shard_map/ppermute | solution.py:31
  22.6 13.2 %collective-permute-start.11 = (bf16[128,2176]{1,0:T(8,128)(2,1)S(1)}, bf16[128,2176]{1,0:T(8,128)(2,1)S(1)}, u32[]{:S(2)}, u32[]{:S(2)}) collective-permute-start(bf16[128,2176]{1,0:T(8,128)(2,1)S(1)} %collective-permute-done.10.refs_7_.refs_4_.refs_9_), channel_id=1, source_target_pairs={{0,32},{1,97},{32,64},{33,1},{64,96},{65,33},{96,0},{97,65},{2,34}... | collective-permute-start | bytes 1671176 | tf_op jit(solution)/shard_map/ppermute | solution.py:31
  25.3 12.8 %collective-permute-start.12 = (bf16[128,2176]{1,0:T(8,128)(2,1)S(1)}, bf16[128,2176]{1,0:T(8,128)(2,1)S(1)}, u32[]{:S(2)}, u32[]{:S(2)}) collective-permute-start(bf16[128,2176]{1,0:T(8,128)(2,1)S(1)} %collective-permute-done.8.refs_5_.refs_2_.refs_7_), channel_id=1, source_target_pairs={{0,128},{128,0},{1,129},{129,1},{2,130},{130,2},{3,131},{131,3},{4... | collective-permute-start | bytes 1671176 | tf_op jit(solution)/shard_map/ppermute | solution.py:35
  26.1 13.2 %collective-permute-start.9 = (bf16[128,2176]{1,0:T(8,128)(2,1)S(1)}, bf16[128,2176]{1,0:T(8,128)(2,1)S(1)}, u32[]{:S(2)}, u32[]{:S(2)}) collective-permute-start(bf16[128,2176]{1,0:T(8,128)(2,1)S(1)} %collective-permute-done.7.refs_4_.refs_1_.refs_6_), channel_id=1, source_target_pairs={{0,32},{1,97},{32,64},{33,1},{64,96},{65,33},{96,0},{97,65},{2,34}... | collective-permute-start | bytes 1671176 | tf_op jit(solution)/shard_map/ppermute | solution.py:31
  32.6 15.6 %collective-permute-start.2 = (bf16[128,2048]{1,0:T(8,128)(2,1)S(1)}, bf16[128,2048]{1,0:T(8,128)(2,1)S(1)}, u32[]{:S(2)}, u32[]{:S(2)}) collective-permute-start(bf16[128,2048]{1,0:T(8,128)(2,1)S(1)} %collective-permute-done.1.refs_1_), channel_id=1, source_target_pairs={{0,4},{1,29},{4,8},{5,1},{8,12},{9,5},{12,16},{13,9},{16,20},{17,1... | collective-permute-start | bytes 1572872 | tf_op jit(solution)/shard_map/ppermute | solution.py:31
  32.6 15.6 %collective-permute-start.5 = (bf16[128,2048]{1,0:T(8,128)(2,1)S(1)}, bf16[128,2048]{1,0:T(8,128)(2,1)S(1)}, u32[]{:S(2)}, u32[]{:S(2)}) collective-permute-start(bf16[128,2048]{1,0:T(8,128)(2,1)S(1)} %collective-permute-done.4.refs_2_), channel_id=1, source_target_pairs={{0,28},{1,5},{4,0},{5,9},{8,4},{9,13},{12,8},{13,17},{16,12},{17,2... | collective-permute-start | bytes 1572872 | tf_op jit(solution)/shard_map/ppermute | solution.py:31
  39.3 10.7 %collective-permute-start.13 = (bf16[128,2176]{1,0:T(8,128)(2,1)S(1)}, bf16[128,2176]{1,0:T(8,128)(2,1)S(1)}, u32[]{:S(2)}, u32[]{:S(2)}) collective-permute-start(bf16[128,2176]{1,0:T(8,128)(2,1)S(1)} %collective-permute-done.11.refs_8_.refs_5_.refs_10_), channel_id=1, source_target_pairs={{0,32},{1,97},{32,64},{33,1},{64,96},{65,33},{96,0},{97,65},{2,34}... | collective-permute-start | bytes 1671176 | tf_op jit(solution)/shard_map/ppermute | solution.py:31
  48.1 10.4 %collective-permute-start.6 = (bf16[128,2048]{1,0:T(8,128)(2,1)S(1)}, bf16[128,2048]{1,0:T(8,128)(2,1)S(1)}, u32[]{:S(2)}, u32[]{:S(2)}) collective-permute-start(bf16[128,2048]{1,0:T(8,128)(2,1)S(1)} %collective-permute-done.2.refs_0_), channel_id=1, source_target_pairs={{0,4},{1,29},{4,8},{5,1},{8,12},{9,5},{12,16},{13,9},{16,20},{17,1... | collective-permute-start | bytes 1572872 | tf_op jit(solution)/shard_map/ppermute | solution.py:31
  51.9 3.1 %collective-permute-start.21 = (f32[160,512]{1,0:T(8,128)S(1)}, f32[160,512]{1,0:T(8,128)S(1)}, u32[]{:S(2)}, u32[]{:S(2)}) collective-permute-start(f32[160,512]{1,0:T(8,128)S(1)} %get-tuple-element.35), channel_id=1, source_target_pairs={{0,1},{1,0},{2,3},{3,2},{4,5},{5,4},{6,7},{7,6},{8,9},{9,8},{10,11... | collective-permute-start | bytes 983048 | tf_op jit(solution)/shard_map/ppermute | solution.py:35
  56.0 11.5 %collective-permute-start.25 = (bf16[656,256]{1,0:T(8,128)(2,1)S(1)}, bf16[656,256]{1,0:T(8,128)(2,1)S(1)}, u32[]{:S(2)}, u32[]{:S(2)}) collective-permute-start(bf16[656,256]{1,0:T(8,128)(2,1)S(1)} %get-tuple-element.40), channel_id=1, source_target_pairs={{0,2},{2,0},{1,3},{3,1},{4,6},{6,4},{5,7},{7,5},{8,10},{10,8},{9,1... | collective-permute-start | bytes 1007624 | tf_op jit(solution)/shard_map/ppermute | solution.py:35
  62.9 13.2 %collective-permute-start.17 = (bf16[400,256]{1,0:T(8,128)(2,1)S(1)}, bf16[400,256]{1,0:T(8,128)(2,1)S(1)}, u32[]{:S(2)}, u32[]{:S(2)}) collective-permute-start(bf16[400,256]{1,0:T(8,128)(2,1)S(1)} %get-tuple-element.31), channel_id=1, source_target_pairs={{0,2},{2,0},{1,3},{3,1},{4,6},{6,4},{5,7},{7,5},{8,10},{10,8},{9,1... | collective-permute-start | bytes 614408 | tf_op jit(solution)/shard_map/ppermute | solution.py:35
  68.2 9.3 %collective-permute-start.26 = (bf16[144,256]{1,0:T(8,128)(2,1)S(1)}, bf16[144,256]{1,0:T(8,128)(2,1)S(1)}, u32[]{:S(2)}, u32[]{:S(2)}) collective-permute-start(bf16[144,256]{1,0:T(8,128)(2,1)S(1)} %get-tuple-element.42), channel_id=1, source_target_pairs={{0,24},{1,9},{4,28},{5,13},{8,0},{9,17},{12,4},{13,21},{16,8},{17,... | collective-permute-start | bytes 221192 | tf_op jit(solution)/shard_map/ppermute | solution.py:31
  71.2 9.3 %collective-permute-start.27 = (bf16[144,256]{1,0:T(8,128)(2,1)S(1)}, bf16[144,256]{1,0:T(8,128)(2,1)S(1)}, u32[]{:S(2)}, u32[]{:S(2)}) collective-permute-start(bf16[144,256]{1,0:T(8,128)(2,1)S(1)} %get-tuple-element.43), channel_id=1, source_target_pairs={{0,8},{1,25},{4,12},{5,29},{8,16},{9,1},{12,20},{13,5},{16,24},{17... | collective-permute-start | bytes 221192 | tf_op jit(solution)/shard_map/ppermute | solution.py:31
  71.2 12.1 %collective-permute-start.28 = (bf16[144,256]{1,0:T(8,128)(2,1)S(1)}, bf16[144,256]{1,0:T(8,128)(2,1)S(1)}, u32[]{:S(2)}, u32[]{:S(2)}) collective-permute-start(bf16[144,256]{1,0:T(8,128)(2,1)S(1)} %get-tuple-element.44), channel_id=1, source_target_pairs={{0,28},{1,5},{4,0},{5,9},{8,4},{9,13},{12,8},{13,17},{16,12},{17,2... | collective-permute-start | bytes 221192 | tf_op jit(solution)/shard_map/ppermute | solution.py:31
  76.1 7.2 %collective-permute-start.29 = (bf16[144,256]{1,0:T(8,128)(2,1)S(1)}, bf16[144,256]{1,0:T(8,128)(2,1)S(1)}, u32[]{:S(2)}, u32[]{:S(2)}) collective-permute-start(bf16[144,256]{1,0:T(8,128)(2,1)S(1)} %get-tuple-element.45), channel_id=1, source_target_pairs={{0,4},{1,29},{4,8},{5,1},{8,12},{9,5},{12,16},{13,9},{16,20},{17,1... | collective-permute-start | bytes 221192 | tf_op jit(solution)/shard_map/ppermute | solution.py:31
  76.7 10.8 %collective-permute-start.18 = (bf16[144,256]{1,0:T(8,128)(2,1)S(1)}, bf16[144,256]{1,0:T(8,128)(2,1)S(1)}, u32[]{:S(2)}, u32[]{:S(2)}) collective-permute-start(bf16[144,256]{1,0:T(8,128)(2,1)S(1)} %get-tuple-element.32), channel_id=1, source_target_pairs={{0,20},{1,13},{4,24},{5,17},{8,28},{9,21},{12,0},{13,25},{16,4},{1... | collective-permute-start | bytes 221192 | tf_op jit(solution)/shard_map/ppermute | solution.py:31
  77.4 10.1 %collective-permute-start.19 = (bf16[144,256]{1,0:T(8,128)(2,1)S(1)}, bf16[144,256]{1,0:T(8,128)(2,1)S(1)}, u32[]{:S(2)}, u32[]{:S(2)}) collective-permute-start(bf16[144,256]{1,0:T(8,128)(2,1)S(1)} %get-tuple-element.33), channel_id=1, source_target_pairs={{0,12},{1,21},{4,16},{5,25},{8,20},{9,29},{12,24},{13,1},{16,28},{... | collective-permute-start | bytes 221192 | tf_op jit(solution)/shard_map/ppermute | solution.py:31
  80.6 9.2 %collective-permute-start.20 = (bf16[144,256]{1,0:T(8,128)(2,1)S(1)}, bf16[144,256]{1,0:T(8,128)(2,1)S(1)}, u32[]{:S(2)}, u32[]{:S(2)}) collective-permute-start(bf16[144,256]{1,0:T(8,128)(2,1)S(1)} %get-tuple-element.34), channel_id=1, source_target_pairs={{0,16},{1,17},{4,20},{5,21},{8,24},{9,25},{12,28},{13,29},{16,0},{... | collective-permute-start | bytes 221192 | tf_op jit(solution)/shard_map/ppermute | solution.py:31
  (8 other events, 64.8 us)
